TPU v7x, 32 devices: a whole 2x2x4 slice. The times are simulated.
32 devices in a mesh: dp: 8 (over y, x, core), ctx: 4 (over z).
Axes of the slice: x: 2, y: 2, z: 4, core: 2. Of those that a mesh axis runs over, the one named last changes fastest.
Arguments:
- tokens: bfloat16 [8192, 1536], P(('dp', 'ctx')), may hold values from -6 to 6
- norm_attn: bfloat16 [1536], P(('dp', 'ctx')), may hold values from 0.5 to 1.5
- w_query: bfloat16 [1536, 1536], P(('dp', 'ctx')), may hold values from -0.15625 to 0.15625
- w_key: bfloat16 [1536, 256], P(('dp', 'ctx')), may hold values from -0.15625 to 0.15625
- w_value: bfloat16 [1536, 256], P(('dp', 'ctx')), may hold values from -0.15625 to 0.15625
- w_out: bfloat16 [1536, 1536], P(('dp', 'ctx')), may hold values from -0.625 to 0.625
- norm_moe: bfloat16 [1536], P(('dp', 'ctx')), may hold values from 0.5 to 1.5
- w_gate: bfloat16 [8, 1536, 768], P('dp'), may hold values from -0.15625 to 0.15625
- w_up: bfloat16 [8, 1536, 768], P('dp'), may hold values from -0.15625 to 0.15625
- w_down: bfloat16 [8, 768, 1536], P('dp'), may hold values from -0.21875 to 0.21875
- routes: int32 [8192, 4], P(('dp', 'ctx')), may hold values from 0 to 7, all different within a row; in each aligned block of 256 rows (0 to 255, 256 to 511, ...) at most 192 rows name the same one
- gate_values: float32 [8192, 4], P(('dp', 'ctx')), may hold values from 0.25 to 1
- lengths: int32 [8, 3], P('dp'), may hold values from 1 to 896, 1024 in all within a row
- cotangent: bfloat16 [8192, 1536], P(('dp', 'ctx')), may hold values from -6 to 6
Outputs:
- layer_out: bfloat16 [8192, 1536], P(('dp', 'ctx'))
- d_tokens: float32 [8192, 1536], P(('dp', 'ctx'))
- d_norm_attn: float32 [1536], P(('dp', 'ctx'))
- d_w_query: float32 [1536, 1536], P(('dp', 'ctx'))
- d_w_key: float32 [1536, 256], P(('dp', 'ctx'))
- d_w_value: float32 [1536, 256], P(('dp', 'ctx'))
- d_w_out: float32 [1536, 1536], P(('dp', 'ctx'))
- d_norm_moe: float32 [1536], P(('dp', 'ctx'))
- d_w_gate: float32 [8, 1536, 768], P('dp')
- d_w_up: float32 [8, 1536, 768], P('dp')
- d_w_down: float32 [8, 768, 1536], P('dp')
Inputs may be any that keep to these rules, and one draw needn't show every extreme that they name: `routes`: each row names 4 different experts; among the rows of one device no expert is named by more than 192 rows, a bound that some block reaches. `lengths`: each row sums to 1024; its largest entry is exactly 896.
All inputs are finite; a program needn't handle non-finite values.
Results may differ from a plain program's by a relative error of at most 0.015.
Values may be sent and summed in bfloat16 or wider, within the bound.
A program may use at most 192 MiB of HBM per device.

v0:
```python
import jax
import jax.numpy as jnp
from jax import lax
from jax.sharding import PartitionSpec as P

D = 1536
HEADS = 12
KVH = 2
HD = 128
TOP = 4
EXP_DEV = 1


epsilon = 1e-06
rope_base = 1000000.0
masked_score = -1e30


def rms_norm(values, gain):
    return values * lax.rsqrt(jnp.mean(values * values, axis=-1, keepdims=True) + epsilon) * gain


def rotate(values, within, direction):
    half_size = values.shape[-1] // 2
    frequency = rope_base ** (-jnp.arange(half_size, dtype=jnp.float32) / half_size)
    angles = direction * within.astype(jnp.float32)[:, None] * frequency[None, :]
    cosine = jnp.cos(angles)[:, None, :]
    sine = jnp.sin(angles)[:, None, :]
    first_half = values[..., :half_size]
    second = values[..., half_size:]
    return jnp.concatenate(
        [first_half * cosine - second * sine, second * cosine + first_half * sine], axis=-1
    )


def seq_tables(length_row, places):
    seq_ends = jnp.cumsum(length_row)
    passed = places[:, None] >= seq_ends[None, :]
    segment = jnp.sum(passed.astype(jnp.int32), axis=1)
    within = places - jnp.sum(jnp.where(passed, length_row[None, :], 0), axis=1)
    return (segment, within)


def collect_weights(gain_attn, w_query, w_key, w_value, w_out, gain_moe):
    return (
        lax.all_gather(gain_attn, ("dp", "ctx"), axis=0, tiled=True),
        lax.all_gather(w_query, ("dp", "ctx"), axis=0, tiled=True),
        lax.all_gather(w_key, ("dp", "ctx"), axis=0, tiled=True),
        lax.all_gather(w_value, ("dp", "ctx"), axis=0, tiled=True),
        lax.all_gather(w_out, ("dp", "ctx"), axis=0, tiled=True),
        lax.all_gather(gain_moe, ("dp", "ctx"), axis=0, tiled=True),
    )


def spread_grads(grad_gain_attn, grad_query, grad_key, grad_value, grad_outp, grad_gain_moe):
    return (
        lax.psum_scatter(grad_gain_attn, ("dp", "ctx"), scatter_dimension=0, tiled=True),
        lax.psum_scatter(grad_query, ("dp", "ctx"), scatter_dimension=0, tiled=True),
        lax.psum_scatter(grad_key, ("dp", "ctx"), scatter_dimension=0, tiled=True),
        lax.psum_scatter(grad_value, ("dp", "ctx"), scatter_dimension=0, tiled=True),
        lax.psum_scatter(grad_outp, ("dp", "ctx"), scatter_dimension=0, tiled=True),
        lax.psum_scatter(grad_gain_moe, ("dp", "ctx"), scatter_dimension=0, tiled=True),
    )


def on_device(
    tokens,
    norm_attn,
    w_query,
    w_key,
    w_value,
    w_out,
    norm_moe,
    w_gate,
    w_up,
    w_down,
    routes,
    gate_values,
    lengths,
    cotangent,
):
    tok_rows = tokens.shape[0]
    ctx_size = lax.axis_size("ctx")
    dp_size = lax.axis_size("dp")
    ctx_place = lax.axis_index("ctx")
    group_rows = tok_rows * ctx_size
    group_places = jnp.arange(group_rows, dtype=jnp.int32)
    seg_all, within_all = seq_tables(lengths[0], group_places)
    offset = ctx_place * tok_rows
    own_places = offset + jnp.arange(tok_rows, dtype=jnp.int32)
    seg_own = lax.dynamic_slice_in_dim(seg_all, offset, tok_rows)
    within_own = lax.dynamic_slice_in_dim(within_all, offset, tok_rows)
    allowed = (seg_own[:, None] == seg_all[None, :]) & (
        group_places[None, :] <= own_places[:, None]
    )
    gain_attn, full_q, full_k, full_v, full_o, gain_moe = collect_weights(
        norm_attn, w_query, w_key, w_value, w_out, norm_moe
    )
    gain_attn_f = gain_attn.astype(jnp.float32)
    gain_moe_f = gain_moe.astype(jnp.float32)
    inputs = tokens.astype(jnp.float32)
    normed_low = rms_norm(inputs, gain_attn_f).astype(jnp.bfloat16)
    query_pre = jnp.dot(normed_low, full_q, preferred_element_type=jnp.float32)
    key_pre = jnp.dot(normed_low, full_k, preferred_element_type=jnp.float32)
    value_pre = jnp.dot(normed_low, full_v, preferred_element_type=jnp.float32)
    query = rotate(query_pre.reshape(tok_rows, HEADS, HD), within_own, 1.0).astype(jnp.bfloat16)
    key_low = rotate(key_pre.reshape(tok_rows, KVH, HD), within_own, 1.0).astype(jnp.bfloat16)
    key_low = key_low.reshape(tok_rows, KVH * HD)
    value_low = value_pre.astype(jnp.bfloat16)
    all_keys, all_values = (
        lax.all_gather(key_low, "ctx", axis=0, tiled=True),
        lax.all_gather(value_low, "ctx", axis=0, tiled=True),
    )
    per_group = HEADS // KVH
    score_scale = HD ** (-0.5)
    query_groups = query.reshape(tok_rows, KVH, per_group, HD)

    def softmax_weights(group_number):
        keys_part = all_keys[:, group_number * HD : (group_number + 1) * HD]
        raw = jnp.einsum(
            "qjd,kd->jqk",
            query_groups[:, group_number],
            keys_part,
            preferred_element_type=jnp.float32,
        )
        scores = jnp.where(allowed[None], raw * score_scale, masked_score)
        row_top = jnp.max(scores, axis=-1, keepdims=True)
        expo = jnp.exp(scores - row_top)
        return expo / jnp.sum(expo, axis=-1, keepdims=True)

    mixed_parts = []
    for group_number in range(KVH):
        probs = softmax_weights(group_number)
        values_part = all_values[:, group_number * HD : (group_number + 1) * HD]
        mixed_group = jnp.einsum(
            "jqk,kd->qjd",
            probs.astype(jnp.bfloat16),
            values_part,
            preferred_element_type=jnp.float32,
        )
        mixed_parts.append(mixed_group.reshape(tok_rows, per_group * HD))
    mixed_low = jnp.concatenate(mixed_parts, axis=1).astype(jnp.bfloat16)
    middle = inputs + jnp.dot(mixed_low, full_o, preferred_element_type=jnp.float32)
    routed_low = rms_norm(middle, gain_moe_f).astype(jnp.bfloat16)
    experts_total = EXP_DEV * dp_size
    capacity = 3 * TOP * tok_rows // (2 * experts_total)
    assign_count = tok_rows * TOP
    flat_ids = routes.reshape(assign_count)
    onehot = (flat_ids[:, None] == jnp.arange(experts_total, dtype=jnp.int32)[None, :]).astype(
        jnp.int32
    )
    earlier = jnp.sum((jnp.cumsum(onehot, axis=0) - onehot) * onehot, axis=1)
    slot_index = flat_ids * capacity + earlier
    owner = (
        jnp.full((experts_total * capacity,), assign_count, jnp.int32)
        .at[slot_index]
        .set(jnp.arange(assign_count, dtype=jnp.int32))
    )
    padded = jnp.concatenate([routed_low, jnp.zeros((1, D), jnp.bfloat16)], axis=0)
    outgoing = padded[owner // TOP].reshape(experts_total, capacity, D)
    arrived = lax.all_to_all(outgoing, "dp", split_axis=0, concat_axis=0, tiled=True)
    arrived_sets = arrived.reshape(dp_size, EXP_DEV, capacity, D)
    gate_act = jnp.einsum(
        "secd,edf->secf", arrived_sets, w_gate, preferred_element_type=jnp.float32
    )
    up_act = jnp.einsum("secd,edf->secf", arrived_sets, w_up, preferred_element_type=jnp.float32)
    hidden_low = (jax.nn.silu(gate_act) * up_act).astype(jnp.bfloat16)
    produced = jnp.einsum("secf,efd->secd", hidden_low, w_down, preferred_element_type=jnp.float32)
    produced = produced.astype(jnp.bfloat16).reshape(experts_total, capacity, D)
    returned = lax.all_to_all(produced, "dp", split_axis=0, concat_axis=0, tiled=True)
    picked = returned.reshape(experts_total * capacity, D)[slot_index].reshape(tok_rows, TOP, D)
    moe_out = jnp.sum(picked.astype(jnp.float32) * gate_values[:, :, None], axis=1)
    layer_out = (middle + moe_out).astype(jnp.bfloat16)
    grad_out = cotangent.astype(jnp.float32)
    grad_assign = (grad_out[:, None, :] * gate_values[:, :, None]).astype(jnp.bfloat16)
    grad_padded = jnp.concatenate(
        [grad_assign.reshape(assign_count, D), jnp.zeros((1, D), jnp.bfloat16)], axis=0
    )
    grad_slots = grad_padded[owner].reshape(experts_total, capacity, D)
    grad_arrived = lax.all_to_all(grad_slots, "dp", split_axis=0, concat_axis=0, tiled=True)
    grad_arrived = grad_arrived.reshape(dp_size, EXP_DEV, capacity, D)
    grad_hidden = jnp.einsum(
        "secd,efd->secf", grad_arrived, w_down, preferred_element_type=jnp.float32
    )
    grad_w_down = jnp.einsum(
        "secf,secd->efd", hidden_low, grad_arrived, preferred_element_type=jnp.float32
    )
    glu_value, glu_pull = jax.vjp(
        lambda gate_in, up_in: jax.nn.silu(gate_in) * up_in, gate_act, up_act
    )
    grad_gate, grad_up = glu_pull(grad_hidden)
    grad_gate_low = grad_gate.astype(jnp.bfloat16)
    grad_up_low = grad_up.astype(jnp.bfloat16)
    grad_w_gate = jnp.einsum(
        "secd,secf->edf", arrived_sets, grad_gate_low, preferred_element_type=jnp.float32
    )
    grad_w_up = jnp.einsum(
        "secd,secf->edf", arrived_sets, grad_up_low, preferred_element_type=jnp.float32
    )
    grad_sent = jnp.einsum(
        "secf,edf->secd", grad_gate_low, w_gate, preferred_element_type=jnp.float32
    ) + jnp.einsum("secf,edf->secd", grad_up_low, w_up, preferred_element_type=jnp.float32)
    grad_sent = grad_sent.astype(jnp.bfloat16).reshape(experts_total, capacity, D)
    grad_back = lax.all_to_all(grad_sent, "dp", split_axis=0, concat_axis=0, tiled=True)
    grad_picked = grad_back.reshape(experts_total * capacity, D)[slot_index].reshape(
        tok_rows, TOP, D
    )
    grad_routed = jnp.sum(grad_picked.astype(jnp.float32), axis=1)
    expert_sums = (
        lax.psum(grad_w_gate.astype(jnp.bfloat16), "ctx").astype(jnp.float32),
        lax.psum(grad_w_up.astype(jnp.bfloat16), "ctx").astype(jnp.float32),
        lax.psum(grad_w_down.astype(jnp.bfloat16), "ctx").astype(jnp.float32),
    )
    norm_value, moe_pull = jax.vjp(rms_norm, middle, gain_moe_f)
    grad_mid_norm, grad_gain_moe = moe_pull(grad_routed)
    grad_middle = grad_out + grad_mid_norm
    grad_attn_low = grad_middle.astype(jnp.bfloat16)
    grad_w_out = jnp.einsum(
        "th,td->hd", mixed_low, grad_attn_low, preferred_element_type=jnp.float32
    )
    grad_mixed_low = jnp.einsum(
        "td,hd->th", grad_attn_low, full_o, preferred_element_type=jnp.float32
    ).astype(jnp.bfloat16)
    grad_mixed_groups = grad_mixed_low.reshape(tok_rows, KVH, per_group, HD)
    grad_query_parts = []
    prob_parts = []
    score_parts = []
    for group_number in range(KVH):
        probs = softmax_weights(group_number)
        keys_part = all_keys[:, group_number * HD : (group_number + 1) * HD]
        values_part = all_values[:, group_number * HD : (group_number + 1) * HD]
        grad_probs = jnp.einsum(
            "qjd,kd->jqk",
            grad_mixed_groups[:, group_number],
            values_part,
            preferred_element_type=jnp.float32,
        )
        grad_scores = probs * (grad_probs - jnp.sum(probs * grad_probs, axis=-1, keepdims=True))
        grad_raw_low = (grad_scores * score_scale).astype(jnp.bfloat16)
        grad_query_parts.append(
            jnp.einsum("jqk,kd->qjd", grad_raw_low, keys_part, preferred_element_type=jnp.float32)
        )
        prob_parts.append(probs.astype(jnp.bfloat16))
        score_parts.append(grad_raw_low)
    grad_query_rot = jnp.stack(grad_query_parts, axis=1).reshape(tok_rows, HEADS, HD)
    key_pieces = []
    value_pieces = []
    for group_number in range(KVH):
        score_piece = score_parts[group_number]
        prob_piece = prob_parts[group_number]
        key_pieces.append(
            jnp.einsum(
                "jqk,qjd->kd",
                score_piece,
                query_groups[:, group_number],
                preferred_element_type=jnp.float32,
            )
        )
        value_pieces.append(
            jnp.einsum(
                "jqk,qjd->kd",
                prob_piece,
                grad_mixed_groups[:, group_number],
                preferred_element_type=jnp.float32,
            )
        )
    key_value_grads = lax.psum_scatter(
        jnp.concatenate(key_pieces + value_pieces, axis=1).astype(jnp.bfloat16),
        "ctx",
        scatter_dimension=0,
        tiled=True,
    ).astype(jnp.float32)
    grad_query_low = (
        rotate(grad_query_rot, within_own, -1.0).astype(jnp.bfloat16).reshape(tok_rows, HEADS * HD)
    )
    grad_key_rot = key_value_grads[:, : KVH * HD].reshape(tok_rows, KVH, HD)
    grad_key_low = (
        rotate(grad_key_rot, within_own, -1.0).astype(jnp.bfloat16).reshape(tok_rows, KVH * HD)
    )
    grad_value_low = key_value_grads[:, KVH * HD :].astype(jnp.bfloat16)
    grad_w_query = jnp.einsum(
        "td,th->dh", normed_low, grad_query_low, preferred_element_type=jnp.float32
    )
    grad_w_key = jnp.einsum(
        "td,th->dh", normed_low, grad_key_low, preferred_element_type=jnp.float32
    )
    grad_w_value = jnp.einsum(
        "td,th->dh", normed_low, grad_value_low, preferred_element_type=jnp.float32
    )
    grad_normed = (
        jnp.einsum("th,dh->td", grad_query_low, full_q, preferred_element_type=jnp.float32)
        + jnp.einsum("th,dh->td", grad_key_low, full_k, preferred_element_type=jnp.float32)
        + jnp.einsum("th,dh->td", grad_value_low, full_v, preferred_element_type=jnp.float32)
    )
    first_value, attn_pull = jax.vjp(rms_norm, inputs, gain_attn_f)
    grad_inputs, grad_gain_attn = attn_pull(grad_normed)
    grad_tokens = grad_middle + grad_inputs
    dense_sums = spread_grads(
        grad_gain_attn, grad_w_query, grad_w_key, grad_w_value, grad_w_out, grad_gain_moe
    )
    return (
        layer_out,
        grad_tokens,
        dense_sums[0],
        dense_sums[1],
        dense_sums[2],
        dense_sums[3],
        dense_sums[4],
        dense_sums[5],
        expert_sums[0],
        expert_sums[1],
        expert_sums[2],
    )


def solution(mesh):
    return jax.shard_map(
        on_device,
        mesh=mesh,
        in_specs=(
            P(("dp", "ctx"), None),
            P(("dp", "ctx")),
            P(("dp", "ctx"), None),
            P(("dp", "ctx"), None),
            P(("dp", "ctx"), None),
            P(("dp", "ctx"), None),
            P(("dp", "ctx")),
            P("dp", None, None),
            P("dp", None, None),
            P("dp", None, None),
            P(("dp", "ctx"), None),
            P(("dp", "ctx"), None),
            P("dp", None),
            P(("dp", "ctx"), None),
        ),
        out_specs=(
            P(("dp", "ctx"), None),
            P(("dp", "ctx"), None),
            P(("dp", "ctx")),
            P(("dp", "ctx"), None),
            P(("dp", "ctx"), None),
            P(("dp", "ctx"), None),
            P(("dp", "ctx"), None),
            P(("dp", "ctx")),
            P("dp", None, None),
            P("dp", None, None),
            P("dp", None, None),
        ),
        check_vma=False,
    )
```

profile of v0, /device:TPU:0, one launch (start us, length us, event | category | flops | bytes accessed | tf_op | source)
XLA Modules:
  0.0 1425.4 jit_solution(2659112820957072039)
XLA Ops:
  35.6 12.7 gather_fusion.2
  54.2 98.7 %all-reduce.7 = (bf16[1536]{0:T(1024)(128)(2,1)S(1)}, bf16[1536]{0:T(1024)(128)(2,1)S(1)}) all-reduce(bf16[1536]{0:T(1024)(128)(2,1)S(1)} %dynamic-update-slice, bf16[1536]{0:T(1024)(128)(2,1)S(1)} %dynamic-update-slice.1), channel_id=1, replica_groups=mesh['dp'=8,'ctx'=4] {'dp','ctx'}, use_global_device_ids=true, to_apply=%add.2 | all-reduce | flops 3072 | bytes 12288
  154.8 73.6 %all_gather.27 = bf16[1536,256]{1,0:T(8,128)(2,1)S(1)} all-gather(bf16[48,256]{1,0:T(8,128)(2,1)S(1)} %copy-done.39), channel_id=1, replica_groups=mesh['dp'=8,'ctx'=4] {'dp','ctx'}, dimensions={0}, use_global_device_ids=true | all-gather | bytes 811008 | tf_op jit(solution)/shard_map/all_gather | solution.py:48
  230.1 71.1 %all_gather.25 = bf16[1536,256]{1,0:T(8,128)(2,1)S(1)} all-gather(bf16[48,256]{1,0:T(8,128)(2,1)S(1)} %copy-done.40), channel_id=1, replica_groups=mesh['dp'=8,'ctx'=4] {'dp','ctx'}, dimensions={0}, use_global_device_ids=true | all-gather | bytes 811008 | tf_op jit(solution)/shard_map/all_gather | solution.py:49
  302.5 17.3 %all_gather.26 = bf16[1024,256]{1,0:T(8,128)(2,1)} all-gather(bf16[256,256]{1,0:T(8,128)(2,1)S(1)} %convolution_convert_fusion.2), channel_id=1, replica_groups=mesh['dp'=8,'ctx'=4] {'ctx'}, dimensions={0}, use_global_device_ids=true | all-gather | bytes 655360 | tf_op jit(solution)/shard_map/all_gather | solution.py:112
  319.8 15.7 %all_gather.28 = bf16[1024,256]{1,0:T(8,128)(2,1)} all-gather(bf16[256,256]{1,0:T(8,128)(2,1)S(1)} %copy.151), channel_id=1, replica_groups=mesh['dp'=8,'ctx'=4] {'ctx'}, dimensions={0}, use_global_device_ids=true | all-gather | bytes 655360 | tf_op jit(solution)/shard_map/all_gather | solution.py:111
  382.8 9.2 fusion.40
  391.9 45.6 %all-to-all-done = bf16[8,192,1536]{2,1,0:T(8,128)(2,1)} async-done(((bf16[8,192,1536]{2,1,0:T(8,128)(2,1)}), bf16[8,192,1536]{2,1,0:T(8,128)(2,1)}, u32[]{:S(2)}, u32[]{:S(2)}) %all-to-all-start) | async-done | bytes 4718624 | tf_op jit(solution)/shard_map/all_to_all | solution.py:161
  444.1 9.5 fusion.36
  478.0 47.6 %all-to-all-done.3 = bf16[8,192,1536]{2,1,0:T(8,128)(2,1)} async-done(((bf16[8,192,1536]{2,1,0:T(8,128)(2,1)}), bf16[8,192,1536]{2,1,0:T(8,128)(2,1)}, u32[]{:S(2)}, u32[]{:S(2)}) %all-to-all-start.3) | async-done | bytes 4718624 | tf_op jit(solution)/shard_map/all_to_all | solution.py:204
  538.7 10.4 gather_fusion.3
  565.9 19.0 %all-to-all-done.1 = bf16[8,192,1536]{2,1,0:T(8,128)(2,1)} async-done(((bf16[8,192,1536]{2,1,0:T(8,128)(2,1)}), bf16[8,192,1536]{2,1,0:T(8,128)(2,1)}, u32[]{:S(2)}, u32[]{:S(2)}) %all-to-all-start.1) | async-done | bytes 4718624 | tf_op jit(solution)/shard_map/all_to_all | solution.py:170
  584.9 10.2 gather_fusion.1
  631.2 10.2 fusion.82
  641.4 10.8 fusion.81
  654.4 8.7 fusion.27
  682.8 11.0 fusion.65
  693.8 11.3 fusion.66
  725.2 43.8 %all-reduce.6 = (f32[1536]{0:T(1024)S(1)}, f32[1536]{0:T(1024)S(1)}) all-reduce(f32[1536]{0:T(1024)S(1)} %get-tuple-element.13, f32[1536]{0:T(1024)S(1)} %copy-done.38), channel_id=3, replica_groups=mesh['dp'=8,'ctx'=4] {'dp','ctx'}, use_global_device_ids=true, to_apply=%region_21.22.clone | all-reduce | flops 3072 | bytes 24576
  773.2 156.9 %all-reduce.11.cloned.1.call-done = (bf16[1,1536,768]{2,1,0:T(8,128)(2,1)}, bf16[1,1536,768]{2,1,0:T(8,128)(2,1)}, bf16[1,768,1536]{2,1,0:T(8,128)(2,1)}) async-done(((bf16[1,1536,768]{2,1,0:T(8,128)(2,1)}, bf16[1,1536,768]{2,1,0:T(8,128)(2,1)}, bf16[1,768,1536]{2,1,0:T(8,128)(2,1)}), (bf16[1,1536,768]{2,1,0:T(8,128)(2,1)}, bf16[1,1536,768]{2,1,0:T(8,128)(2,1)}, ...) | async-done | bytes 7077904 | tf_op jit(solution)/shard_map/psum | solution.py:210
  939.8 92.7 %reduce-scatter.10.cloned.1.call-done = f32[48,256]{1,0:T(8,128)} async-done(((f32[1536,256]{1,0:T(8,128)}), f32[48,256]{1,0:T(8,128)}) %reduce-scatter.10.cloned.1.call-update) | async-done | bytes 49168 | tf_op jit(solution)/shard_map/reduce_scatter | solution.py:59
  1032.5 102.6 %reduce-scatter.12.cloned.1.call-done = f32[48,256]{1,0:T(8,128)} async-done(((f32[1536,256]{1,0:T(8,128)}), f32[48,256]{1,0:T(8,128)}) %reduce-scatter.12.cloned.1.call-update) | async-done | bytes 49168 | tf_op jit(solution)/shard_map/reduce_scatter | solution.py:60
  1135.1 142.0 %reduce-scatter.8.cloned.1.call-done = f32[48,1536]{1,0:T(8,128)} async-done(((f32[1536,1536]{1,0:T(8,128)}), f32[48,1536]{1,0:T(8,128)}) %reduce-scatter.8.cloned.1.call-update) | async-done | bytes 294928 | tf_op jit(solution)/shard_map/reduce_scatter | solution.py:58
  1277.1 141.2 %reduce-scatter.14.cloned.1.call-done = f32[48,1536]{1,0:T(8,128)} async-done(((f32[1536,1536]{1,0:T(8,128)}), f32[48,1536]{1,0:T(8,128)}) %reduce-scatter.14.cloned.1.call-update) | async-done | bytes 294928 | tf_op jit(solution)/shard_map/reduce_scatter | solution.py:61
  (252 shorter events, 238.4 us)
Async XLA Ops:
  7.2 436.9 %copy-start = (bf16[1,1536,768]{2,1,0:T(8,128)(2,1)S(1)}, bf16[1,1536,768]{2,1,0:T(8,128)(2,1)}, u32[]{:S(2)}) copy-start(bf16[1,1536,768]{2,1,0:T(8,128)(2,1)} %param.21) | copy-start | bytes 7077892
  7.2 329.2 %all-gather.3.cloned.1.call-start = ((), (), s32[]{:S(2)}) async-start(), calls=%async_computation.9 | async-start | bytes 4866048 | tf_op jit(solution)/shard_map/all_gather | solution.py:47
  7.9 358.2 %all-gather.5.cloned.1.call-start = ((), (), s32[]{:S(2)}) async-start(), calls=%async_computation.10 | async-start | bytes 4866048 | tf_op jit(solution)/shard_map/all_gather | solution.py:50
  48.3 104.6 %copy-start.49 = (s32[1,3]{1,0:T(1,128)S(1)}, s32[1,3]{1,0:T(1,128)}, u32[]{:S(2)}) copy-start(s32[1,3]{1,0:T(1,128)} %param.26) | copy-start | bytes 40
  48.3 105.0 %copy-start.2 = (bf16[256,1536]{1,0:T(8,128)(2,1)S(1)}, bf16[256,1536]{1,0:T(8,128)(2,1)}, u32[]{:S(2)}) copy-start(bf16[256,1536]{1,0:T(8,128)(2,1)} %param.14) | copy-start | bytes 2359300
  48.3 106.5 %copy-start.39 = (bf16[48,256]{1,0:T(8,128)(2,1)S(1)}, bf16[48,256]{1,0:T(8,128)(2,1)}, u32[]{:S(2)}) copy-start(bf16[48,256]{1,0:T(8,128)(2,1)} %param.17) | copy-start | bytes 73732
  48.3 329.4 %all-to-all-start.2 = ((bf16[8,192,1536]{2,1,0:T(8,128)(2,1)}), bf16[8,192,1536]{2,1,0:T(8,128)(2,1)}, u32[]{:S(2)}, u32[]{:S(2)}) async-start(bf16[8,192,1536]{2,1,0:T(8,128)(2,1)} %bitcast.344), calls=%async_computation.2 | async-start | bytes 9437184 | tf_op jit(solution)/shard_map/all_to_all | solution.py:180
  53.6 176.4 %copy-start.40 = (bf16[48,256]{1,0:T(8,128)(2,1)S(1)}, bf16[48,256]{1,0:T(8,128)(2,1)}, u32[]{:S(2)}) copy-start(bf16[48,256]{1,0:T(8,128)(2,1)} %param.18) | copy-start | bytes 73732
  152.9 183.6 %copy-start.33 = (f32[1536]{0:T(1024)}, f32[1536]{0:T(1024)S(1)}, u32[]{:S(2)}) copy-start(f32[1536]{0:T(1024)S(1)} %convert_element_type.146) | copy-start | bytes 18436
  153.6 148.9 %copy-start.44 = (f32[256]{0:T(256)}, f32[256]{0:T(256)S(1)}, u32[]{:S(2)}) copy-start(f32[256]{0:T(256)S(1)} %fusion.55) | copy-start | bytes 3076
  153.6 182.8 %copy-start.36 = (f32[256]{0:T(256)}, f32[256]{0:T(256)S(1)}, u32[]{:S(2)}) copy-start(f32[256]{0:T(256)S(1)} %fusion.115) | copy-start | bytes 3076
  154.8 75.1 %copy-start.26 = (f32[256,64]{0,1:T(8,128)}, f32[256,64]{0,1:T(8,128)S(1)}, u32[]{:S(2)}) copy-start(f32[256,64]{0,1:T(8,128)S(1)} %get-tuple-element.45) | copy-start | bytes 196612
  154.8 75.1 %copy-start.28 = (f32[256,64]{0,1:T(8,128)}, f32[256,64]{0,1:T(8,128)S(1)}, u32[]{:S(2)}) copy-start(f32[256,64]{0,1:T(8,128)S(1)} %get-tuple-element.46) | copy-start | bytes 196612
  377.7 59.8 %all-to-all-start = ((bf16[8,192,1536]{2,1,0:T(8,128)(2,1)}), bf16[8,192,1536]{2,1,0:T(8,128)(2,1)}, u32[]{:S(2)}, u32[]{:S(2)}) async-start(bf16[8,192,1536]{2,1,0:T(8,128)(2,1)} %bitcast.345), calls=%async_computation | async-start | bytes 9437184 | tf_op jit(solution)/shard_map/all_to_all | solution.py:161
  465.9 59.7 %all-to-all-start.3 = ((bf16[8,192,1536]{2,1,0:T(8,128)(2,1)}), bf16[8,192,1536]{2,1,0:T(8,128)(2,1)}, u32[]{:S(2)}, u32[]{:S(2)}) async-start(bf16[8,192,1536]{2,1,0:T(8,128)(2,1)} %add_convert_fusion), calls=%async_computation.3 | async-start | bytes 9437184 | tf_op jit(solution)/shard_map/all_to_all | solution.py:204
  478.0 52.3 %copy-start.43 = (s32[1024,1]{0,1:T(1,128)S(1)}, s32[1024,1]{0,1:T(1,128)}, u32[]{:S(2)}) copy-start(s32[1024,1]{0,1:T(1,128)} %copy-done.42) | copy-start | bytes 12292
  525.6 59.4 %all-to-all-start.1 = ((bf16[8,192,1536]{2,1,0:T(8,128)(2,1)}), bf16[8,192,1536]{2,1,0:T(8,128)(2,1)}, u32[]{:S(2)}, u32[]{:S(2)}) async-start(bf16[8,192,1536]{2,1,0:T(8,128)(2,1)} %convolution_convert_fusion), calls=%async_computation.1 | async-start | bytes 9437184 | tf_op jit(solution)/shard_map/all_to_all | solution.py:170
  530.2 148.0 %reduce-scatter.6.cloned.1.call-start = ((), (), s32[]{:S(2)}) async-start(), calls=%async_computation.11 | async-start | bytes 1310720 | tf_op jit(solution)/shard_map/reduce_scatter | solution.py:267
  654.4 275.7 %all-reduce.11.cloned.1.call-start = ((), (), s32[]{:S(2)}) async-start(), calls=%async_computation.16 | async-start | bytes 14155776 | tf_op jit(solution)/shard_map/psum | solution.py:210
  670.7 361.9 %reduce-scatter.10.cloned.1.call-start = ((), (), s32[]{:S(2)}) async-start(), calls=%async_computation.13 | async-start | bytes 1622016 | tf_op jit(solution)/shard_map/reduce_scatter | solution.py:59
  681.0 454.1 %reduce-scatter.12.cloned.1.call-start = ((), (), s32[]{:S(2)}) async-start(), calls=%async_computation.14 | async-start | bytes 1622016 | tf_op jit(solution)/shard_map/reduce_scatter | solution.py:60
  682.8 594.4 %reduce-scatter.8.cloned.1.call-start = ((), (), s32[]{:S(2)}) async-start(), calls=%async_computation.12 | async-start | bytes 9732096 | tf_op jit(solution)/shard_map/reduce_scatter | solution.py:58
  712.0 706.3 %reduce-scatter.14.cloned.1.call-start = ((), (), s32[]{:S(2)}) async-start(), calls=%async_computation.15 | async-start | bytes 9732096 | tf_op jit(solution)/shard_map/reduce_scatter | solution.py:61
  937.0 481.3 %copy-start.1 = (bf16[1,1536,768]{2,1,0:T(8,128)(2,1)S(1)}, bf16[1,1536,768]{2,1,0:T(8,128)(2,1)}, u32[]{:S(2)}) copy-start(bf16[1,1536,768]{2,1,0:T(8,128)(2,1)} %param.21) | copy-start | bytes 7077892
  (51 other events, 313.8 us)
Sparse Core Ops, SparseCore 0:
  10.8 74.9 all-gather.2
  88.6 75.9 all-gather.4
  654.5 23.6 reduce-scatter.5
  681.4 248.6 all-reduce.10
  936.6 95.9 reduce-scatter.9
  1039.1 95.9 reduce-scatter.11
  1142.6 134.4 reduce-scatter.7
  1283.6 134.6 reduce-scatter.13
where the time goes:
time: 1430 us
  waiting for transfers between devices  757 us (53%)
  blocking collectives  320 us (22%)
  matrix products  179 us (13%)
  local copies, waits for them, and re-layouts  87.1 us (6%)
  other arithmetic  46.7 us (3%)
  starting transfers between devices  20.2 us (1%)
  between operations  15.2 us (1%)
    psum x1, waiting for transfers between devices, on_device(): lax.psum(grad_w_gate.astype(jnp.bfloat16), 'ctx').astype(jnp.float32)  157 us
    unnamed x2, blocking collectives  142 us
    reduce_scatter x1, waiting for transfers between devices, spread_grads(): lax.psum_scatter(grad_query, ('dp', 'ctx'), scatter_dimension=0, tiled=True)  142 us
    reduce_scatter x1, waiting for transfers between devices, spread_grads(): lax.psum_scatter(grad_outp, ('dp', 'ctx'), scatter_dimension=0, tiled=True)  141 us
    reduce_scatter x1, waiting for transfers between devices, spread_grads(): lax.psum_scatter(grad_value, ('dp', 'ctx'), scatter_dimension=0, tiled=True)  103 us
    reduce_scatter x1, waiting for transfers between devices, spread_grads(): lax.psum_scatter(grad_key, ('dp', 'ctx'), scatter_dimension=0, tiled=True)  92.7 us
    all_gather x1, blocking collectives, collect_weights(): lax.all_gather(w_key, ('dp', 'ctx'), axis=0, tiled=True)  73.6 us
    all_gather x1, blocking collectives, collect_weights(): lax.all_gather(w_value, ('dp', 'ctx'), axis=0, tiled=True)  71.1 us
  transfers between devices with their start and end apart: 12, of which 9 were waited for; matrix products, arithmetic and copies ran while one was open for 15% of the time, Pallas kernels for 0%

commit v1 on v0

--- a/solution.py
+++ b/solution.py
@@ -1,6 +1,10 @@
+import functools
+
 import jax
 import jax.numpy as jnp
 from jax import lax
+from jax.experimental import pallas as pl
+from jax.experimental.pallas import tpu as pltpu
 from jax.sharding import PartitionSpec as P
 
 D = 1536
@@ -313,9 +317,760 @@
     )
 
 
+MESH = pl.DeviceIdType.MESH
+LANES = 128
+MIB = 2**20
+ANY = pl.BlockSpec(memory_space=pl.ANY)
+VMEM = pl.BlockSpec(memory_space=pltpu.VMEM)
+
+
+def flip(index, bit):
+    return index + bit - 2 * bit * ((index // bit) % 2)
+
+
+def masked(index, mask):
+    for bit in (1, 2, 4):
+        if mask & bit:
+            index = flip(index, bit)
+    return index
+
+
+class Wires:
+    def __init__(self, send, recv):
+        self.send, self.recv, self.used = send, recv, 0
+        self.dp, self.z = lax.axis_index("dp"), lax.axis_index("ctx")
+
+    def take(self, count):
+        first = self.used
+        self.used += count
+        return first
+
+    def copy(self, src, dst, number, dp=None, z=None):
+        return pltpu.make_async_remote_copy(
+            src_ref=src,
+            dst_ref=dst,
+            send_sem=self.send.at[number],
+            recv_sem=self.recv.at[number],
+            device_id=(self.dp if dp is None else dp, self.z if z is None else z),
+            device_id_type=MESH,
+        )
+
+
+def greet(wires, masks, line):
+    barrier = pltpu.get_barrier_semaphore()
+    dp, z = wires.dp, wires.z
+    for mask in masks:
+        pl.semaphore_signal(barrier, inc=1, device_id=(masked(dp, mask), z), device_id_type=MESH)
+    for step in range(1, LINE) if line else ():
+        pl.semaphore_signal(
+            barrier, inc=1, device_id=(dp, lax.rem(z + step, LINE)), device_id_type=MESH
+        )
+    pl.semaphore_wait(barrier, len(masks) + (LINE - 1 if line else 0))
+
+
+LINE = 4
+
+
+class LineGather:
+    COPIES = 2 * (LINE - 1)
+
+    def __init__(self, wires, ref, rows_of):
+        self.wires, self.ref, self.rows_of = wires, ref, rows_of
+        self.first = wires.take(self.COPIES)
+
+    def _copy(self, block, number, z):
+        part = self.ref.at[self.rows_of(block)]
+        return self.wires.copy(part, part, self.first + number, z=z)
+
+    def start(self, step):
+        z = self.wires.z
+
+        @pl.when((z >= step) & (z < LINE - 1))
+        def _():
+            self._copy(z - step, step, z + 1).start()
+
+        @pl.when((z + step < LINE) & (z > 0))
+        def _():
+            self._copy(z + step, LINE - 1 + step, z - 1).start()
+
+    def wait(self, step):
+        z = self.wires.z
+
+        @pl.when(z - 1 - step >= 0)
+        def _():
+            self._copy(z - 1 - step, step, z).wait_recv()
+
+        @pl.when(z + 1 + step < LINE)
+        def _():
+            self._copy(z + 1 + step, LINE - 1 + step, z).wait_recv()
+
+    def finish(self):
+        z = self.wires.z
+        for step in range(LINE - 1):
+
+            @pl.when((z >= step) & (z < LINE - 1))
+            def _():
+                self._copy(z - step, step, z + 1).wait_send()
+
+            @pl.when((z + step < LINE) & (z > 0))
+            def _():
+                self._copy(z + step, LINE - 1 + step, z - 1).wait_send()
+
+
+class PlaneGather:
+    CHIP = (
+        ((2, 0, 0), (4, 0, 1)),
+        ((4, 0, 0), (4, 2, 0), (2, 0, 1), (2, 4, 1)),
+    )
+    CORE = (
+        ((1, 0, 2),),
+        ((1, 2, 0), (1, 4, 1)),
+        ((1, 4, 0), (1, 6, 0), (1, 2, 1), (1, 6, 1)),
+    )
+    COPIES = 13
+
+    def __init__(self, wires, ref, group):
+        self.wires, self.ref, self.group = wires, ref, group
+        first = wires.take(self.COPIES)
+        self.number = {}
+        for stage in self.CHIP + self.CORE:
+            for one in stage:
+                self.number[one] = first + len(self.number)
+
+    def _copy(self, one, from_me):
+        to, whose, half = one
+        dp = self.wires.dp
+        sender = dp if from_me else masked(dp, to)
+        owner = masked(sender, whose)
+        size = self.group if half == 2 else self.group // 2
+        begin = owner * self.group + (self.group // 2 if half == 1 else 0)
+        part = self.ref.at[pl.ds(pl.multiple_of(begin, 16), size)]
+        return self.wires.copy(part, part, self.number[one], dp=masked(dp, to))
+
+    def start(self, stage):
+        for one in (self.CHIP[stage] if stage < 2 else ()) + self.CORE[stage]:
+            self._copy(one, True).start()
+
+    def wait(self, stage):
+        for one in self.CHIP[stage]:
+            self._copy(one, False).wait_recv()
+
+    def finish(self):
+        for stage in self.CORE:
+            for one in stage:
+                self._copy(one, False).wait_recv()
+        for one in self.number:
+            self._copy(one, True).wait_send()
+
+
+def add_rows(out, out_row, left, left_row, right, right_row, rows):
+    @pl.loop(0, rows // 16)
+    def _(step):
+        def cut(row):
+            return pl.ds(pl.multiple_of(row + step * 16, 16), 16)
+
+        out[cut(out_row), :] = (
+            left[cut(left_row), :].astype(jnp.float32) + right[cut(right_row), :].astype(jnp.float32)
+        ).astype(out.dtype)
+
+
+class PlaneReduce:
+    COPIES = 10
+
+    def __init__(self, wires, part, group, core_in, first_in, second_in):
+        self.wires, self.part, self.group, self.half = wires, part, group, group // 2
+        self.core_in, self.first_in, self.second_in = core_in, first_in, second_in
+        self.first = wires.take(self.COPIES)
+        self.begun = []
+
+    def _send(self, src, src_row, dst, dst_row, rows, number, to):
+        return self.wires.copy(
+            src.at[pl.ds(src_row, rows)],
+            dst.at[pl.ds(dst_row, rows)],
+            self.first + number,
+            dp=masked(self.wires.dp, to),
+        )
+
+    def _core(self, slot):
+        row = pl.multiple_of(masked(self.wires.dp, 1 + 2 * slot) * self.group, 16)
+        return self._send(self.part, row, self.core_in, slot * self.group, self.group, slot, 1)
+
+    def _far(self, number):
+        g, h = self.group, self.half
+        src_row, dst, dst_row, to = (
+            (3 * g, self.first_in, h, 4),
+            (3 * g + h, self.first_in, 3 * h, 2),
+            (2 * g, self.first_in, 0, 4),
+            (1 * g + h, self.first_in, 2 * h, 2),
+            (1 * g, self.second_in, 0, 2),
+            (2 * g + h, self.second_in, h, 4),
+        )[number]
+        return self._send(self.core_in, src_row, dst, dst_row, h, 4 + number, to)
+
+    def start(self):
+        for slot in (3, 2, 1, 0):
+            self._core(slot).start()
+
+    def _sum_core(self, slot):
+        self._core(slot).wait()
+        row = pl.multiple_of(masked(self.wires.dp, 2 * slot) * self.group, 16)
+        add_rows(
+            self.core_in, slot * self.group, self.part, row, self.core_in, slot * self.group, self.group
+        )
+
+    def middle(self):
+        g, h = self.group, self.half
+        self._sum_core(3)
+        self._far(0).start()
+        self._far(1).start()
+        self._sum_core(2)
+        self._far(2).start()
+        self._sum_core(1)
+        self._far(3).start()
+        self._sum_core(0)
+        self._far(0).wait()
+        add_rows(self.core_in, 1 * g, self.core_in, 1 * g, self.first_in, h, h)
+        self._far(4).start()
+        self._far(1).wait()
+        add_rows(self.core_in, 2 * g + h, self.core_in, 2 * g + h, self.first_in, 3 * h, h)
+        self._far(5).start()
+        self._far(2).wait()
+        add_rows(self.core_in, 0, self.core_in, 0, self.first_in, 0, h)
+        self._far(3).wait()
+        add_rows(self.core_in, h, self.core_in, h, self.first_in, 2 * h, h)
+
+    def finish(self, out):
+        h = self.half
+        self._far(4).wait()
+        add_rows(out, 0, self.core_in, 0, self.second_in, 0, h)
+        self._far(5).wait()
+        add_rows(out, h, self.core_in, h, self.second_in, h, h)
+
+    @staticmethod
+    def scratch(group, columns):
+        return [
+            pltpu.VMEM((4 * group, columns), jnp.bfloat16),
+            pltpu.VMEM((2 * group, columns), jnp.bfloat16),
+            pltpu.VMEM((group, columns), jnp.bfloat16),
+        ]
+
+
+class LineReduce:
+    COPIES = 2 * (LINE - 1) * LINE
+
+    def __init__(self, wires, part, rows, landing):
+        self.wires, self.part, self.rows, self.landing = wires, part, rows, landing
+        self.first = wires.take(self.COPIES)
+
+    def _copy(self, way, hop, block, z):
+        number = ((0 if way == 1 else 1) * (LINE - 1) + hop) * LINE + block
+        return self.wires.copy(
+            self.part.at[pl.ds(block * self.rows, self.rows)],
+            self.landing.at[pl.ds(((0 if way == 1 else 1) * LINE + block) * self.rows, self.rows)],
+            self.first + number,
+            z=z,
+        )
+
+    def run(self, out):
+        z, rows = self.wires.z, self.rows
+        sends = []
+        for hop in range(LINE - 1):
+            for way in (1, -1):
+                source = hop if way == 1 else LINE - 1 - hop
+                blocks = range(LINE - 1, hop, -1) if way == 1 else range(0, LINE - 1 - hop)
+                for block in blocks:
+
+                    @pl.when(z == source)
+                    def _():
+                        self._copy(way, hop, block, z + way).start()
+
+                    sends.append((way, hop, block, source))
+            for way in (1, -1):
+                source = hop if way == 1 else LINE - 1 - hop
+                blocks = range(LINE - 1, hop, -1) if way == 1 else range(0, LINE - 1 - hop)
+                for block in blocks:
+
+                    @pl.when(z == source + way)
+                    def _():
+                        self._copy(way, hop, block, z).wait_recv()
+                        add_rows(
+                            self.part,
+                            block * rows,
+                            self.part,
+                            block * rows,
+                            self.landing,
+                            ((0 if way == 1 else 1) * LINE + block) * rows,
+                            rows,
+                        )
+
+        @pl.loop(0, rows // 16)
+        def _(step):
+            row = pl.multiple_of(z * rows + step * 16, 16)
+            out[pl.ds(pl.multiple_of(step * 16, 16), 16), :] = self.part[pl.ds(row, 16), :].astype(out.dtype)
+
+        for way, hop, block, source in sends:
+
+            @pl.when(z == source)
+            def _():
+                self._copy(way, hop, block, z + way).wait_send()
+
+    @staticmethod
+    def scratch(rows, columns):
+        return pltpu.VMEM((2 * LINE * rows, columns), jnp.bfloat16)
+
+
+def sems(count):
+    return [pltpu.SemaphoreType.DMA((count,)), pltpu.SemaphoreType.DMA((count,))]
+
+
+def kernel_params(collective_id, mib):
+    return pltpu.CompilerParams(
+        collective_id=collective_id, has_side_effects=True, vmem_limit_bytes=mib * MIB
+    )
+
+
+def gather_inputs(w_in, w_out, cotangent, gates):
+    rows, tokens = w_in.shape[0], cotangent.shape[0]
+    planes = 8
+    group = LINE * rows
+
+    def kernel(in_ref, out_ref, cot_ref, gate_ref, all_in, all_out, all_cot, all_gate, here, send, recv):
+        wires = Wires(send, recv)
+        dp, z = wires.dp, wires.z
+        own = pl.ds(pl.multiple_of((dp * LINE + z) * rows, 16), rows)
+        locals_ = [
+            pltpu.make_async_copy(in_ref, all_in.at[own], here.at[0]),
+            pltpu.make_async_copy(out_ref, all_out.at[own], here.at[1]),
+            pltpu.make_async_copy(
+                cot_ref, all_cot.at[pl.ds(pl.multiple_of(dp * tokens, 16), tokens)], here.at[2]
+            ),
+            pltpu.make_async_copy(gate_ref, all_gate.at[pl.ds(pl.multiple_of(dp * 8, 8), 8)], here.at[3]),
+        ]
+        for one in locals_:
+            one.start()
+        greet(wires, range(1, planes), True)
+        for one in locals_:
+            one.wait()
+
+        def block_rows(block):
+            return pl.ds(pl.multiple_of((dp * LINE + block) * rows, 16), rows)
+
+        lines = [LineGather(wires, all_in, block_rows), LineGather(wires, all_out, block_rows)]
+        spreads = [
+            PlaneGather(wires, all_in, group),
+            PlaneGather(wires, all_out, group),
+            PlaneGather(wires, all_cot, tokens),
+        ]
+        first = wires.take(planes - 1)
+
+        def gate_copy(mask, owner):
+            part = all_gate.at[pl.ds(pl.multiple_of(owner * 8, 8), 8)]
+            return wires.copy(part, part, first + mask - 1, dp=masked(dp, mask))
+
+        for mask in range(1, planes):
+            gate_copy(mask, dp).start()
+        for step in range(LINE - 1):
+            lines[0].start(step)
+            lines[0].wait(step)
+        spreads[0].start(0)
+        for step in range(LINE - 1):
+            lines[1].start(step)
+            lines[1].wait(step)
+        spreads[0].wait(0)
+        spreads[0].start(1)
+        spreads[1].start(0)
+        spreads[2].start(0)
+        spreads[0].wait(1)
+        spreads[0].start(2)
+        spreads[1].wait(0)
+        spreads[1].start(1)
+        spreads[2].wait(0)
+        spreads[2].start(1)
+        spreads[1].wait(1)
+        spreads[1].start(2)
+        spreads[2].wait(1)
+        spreads[2].start(2)
+        for one in lines + spreads:
+            one.finish()
+        for mask in range(1, planes):
+            gate_copy(mask, masked(dp, mask)).wait_recv()
+        for mask in range(1, planes):
+            gate_copy(mask, dp).wait_send()
+
+    copies = 2 * LineGather.COPIES + 3 * PlaneGather.COPIES + planes - 1
+    return pl.pallas_call(
+        kernel,
+        out_shape=(
+            jax.ShapeDtypeStruct((planes * group, w_in.shape[1]), jnp.bfloat16),
+            jax.ShapeDtypeStruct((planes * group, w_out.shape[1]), jnp.bfloat16),
+            jax.ShapeDtypeStruct((planes * tokens, cotangent.shape[1]), jnp.bfloat16),
+            jax.ShapeDtypeStruct((planes * 8, tokens), jnp.float32),
+        ),
+        in_specs=[ANY] * 4,
+        out_specs=(ANY,) * 4,
+        scratch_shapes=[pltpu.SemaphoreType.DMA((4,))] + sems(copies),
+        compiler_params=kernel_params(0, 60),
+        name="gather_inputs",
+    )(w_in, w_out, cotangent, gates)
+
+
+def gather_line(block):
+    rows, columns = block.shape
+
+    def kernel(block_ref, all_ref, here, send, recv):
+        wires = Wires(send, recv)
+        own = pltpu.make_async_copy(
+            block_ref, all_ref.at[pl.ds(pl.multiple_of(wires.z * rows, 16), rows)], here.at[0]
+        )
+        own.start()
+        greet(wires, (), True)
+        own.wait()
+        line = LineGather(wires, all_ref, lambda b: pl.ds(pl.multiple_of(b * rows, 16), rows))
+        for step in range(LINE - 1):
+            line.start(step)
+            line.wait(step)
+        line.finish()
+
+    return pl.pallas_call(
+        kernel,
+        out_shape=jax.ShapeDtypeStruct((LINE * rows, columns), block.dtype),
+        in_specs=[VMEM],
+        out_specs=VMEM,
+        scratch_shapes=[pltpu.SemaphoreType.DMA((1,))] + sems(LineGather.COPIES),
+        compiler_params=kernel_params(1, 60),
+        name="gather_line",
+    )(block)
+
+
+def gather_plane(block):
+    rows, columns = block.shape
+
+    def kernel(block_ref, all_ref, here, send, recv):
+        wires = Wires(send, recv)
+        own = pltpu.make_async_copy(
+            block_ref, all_ref.at[pl.ds(pl.multiple_of(wires.dp * rows, 16), rows)], here.at[0]
+        )
+        own.start()
+        greet(wires, (1, 2, 4), False)
+        own.wait()
+        spread = PlaneGather(wires, all_ref, rows)
+        spread.start(0)
+        spread.wait(0)
+        spread.start(1)
+        spread.wait(1)
+        spread.start(2)
+        spread.finish()
+
+    return pl.pallas_call(
+        kernel,
+        out_shape=jax.ShapeDtypeStruct((8 * rows, columns), block.dtype),
+        in_specs=[VMEM],
+        out_specs=VMEM,
+        scratch_shapes=[pltpu.SemaphoreType.DMA((1,))] + sems(PlaneGather.COPIES),
+        compiler_params=kernel_params(2, 60),
+        name="gather_plane",
+    )(block)
+
+
+def reduce_plane(part, collective_id):
+    rows, columns = part.shape[0] // 8, part.shape[1]
+
+    def kernel(part_ref, out_ref, core_in, first_in, second_in, send, recv):
+        wires = Wires(send, recv)
+        greet(wires, (1, 2, 4), False)
+        total = PlaneReduce(wires, part_ref, rows, core_in, first_in, second_in)
+        total.start()
+        total.middle()
+        total.finish(out_ref)
+
+    return pl.pallas_call(
+        kernel,
+        out_shape=jax.ShapeDtypeStruct((rows, columns), jnp.float32),
+        in_specs=[VMEM],
+        out_specs=VMEM,
+        scratch_shapes=PlaneReduce.scratch(rows, columns) + sems(PlaneReduce.COPIES),
+        compiler_params=kernel_params(collective_id, 60),
+        name=f"reduce_plane_{collective_id}",
+    )(part)
+
+
+def reduce_line(part):
+    rows, columns = part.shape[0] // LINE, part.shape[1]
+
+    def kernel(part_ref, out_ref, sums, landing, here, send, recv):
+        wires = Wires(send, recv)
+        own = pltpu.make_async_copy(part_ref, sums, here.at[0])
+        own.start()
+        greet(wires, (), True)
+        own.wait()
+        LineReduce(wires, sums, rows, landing).run(out_ref)
+
+    return pl.pallas_call(
+        kernel,
+        out_shape=jax.ShapeDtypeStruct((rows, columns), jnp.float32),
+        in_specs=[VMEM],
+        out_specs=VMEM,
+        scratch_shapes=[
+            pltpu.VMEM(part.shape, jnp.bfloat16),
+            LineReduce.scratch(rows, columns),
+            pltpu.SemaphoreType.DMA((1,)),
+        ]
+        + sems(LineReduce.COPIES),
+        compiler_params=kernel_params(5, 60),
+        name="reduce_line",
+    )(part)
+
+
+def reduce_all(part):
+    rows, columns = part.shape[0] // (8 * LINE), part.shape[1]
+    group = LINE * rows
+
+    def kernel(part_ref, out_ref, core_in, first_in, second_in, sums, landing, send, recv):
+        wires = Wires(send, recv)
+        greet(wires, (1, 2, 4), True)
+        total = PlaneReduce(wires, part_ref, group, core_in, first_in, second_in)
+        total.start()
+        total.middle()
+        total.finish(sums)
+        LineReduce(wires, sums, rows, landing).run(out_ref)
+
+    return pl.pallas_call(
+        kernel,
+        out_shape=jax.ShapeDtypeStruct((rows, columns), jnp.float32),
+        in_specs=[VMEM],
+        out_specs=VMEM,
+        scratch_shapes=PlaneReduce.scratch(group, columns)
+        + [pltpu.VMEM((group, columns), jnp.bfloat16), LineReduce.scratch(rows, columns)]
+        + sems(PlaneReduce.COPIES + LineReduce.COPIES),
+        compiler_params=kernel_params(6, 60),
+        name="reduce_all",
+    )(part)
+
+
+def on_plane_device(
+    tokens,
+    norm_attn,
+    w_query,
+    w_key,
+    w_value,
+    w_out,
+    norm_moe,
+    w_gate,
+    w_up,
+    w_down,
+    routes,
+    gate_values,
+    lengths,
+    cotangent,
+):
+    tok_rows = tokens.shape[0]
+    ctx_size = lax.axis_size("ctx")
+    ctx_place = lax.axis_index("ctx")
+    group_rows = tok_rows * ctx_size
+    group_places = jnp.arange(group_rows, dtype=jnp.int32)
+    seg_all, within_all = seq_tables(lengths[0], group_places)
+    offset = ctx_place * tok_rows
+    own_places = offset + jnp.arange(tok_rows, dtype=jnp.int32)
+    seg_own = lax.dynamic_slice_in_dim(seg_all, offset, tok_rows)
+    within_own = lax.dynamic_slice_in_dim(within_all, offset, tok_rows)
+    allowed = (seg_own[:, None] == seg_all[None, :]) & (
+        group_places[None, :] <= own_places[:, None]
+    )
+    kv_columns = KVH * HD
+    q_columns = HEADS * HD
+    gains = jnp.pad(jnp.stack([norm_attn, norm_moe], axis=1), ((0, 0), (0, LANES - 2)))
+    w_in = jnp.concatenate([w_query, w_key, w_value, gains], axis=1)
+    experts = jnp.arange(8, dtype=jnp.int32)
+    gates = jnp.sum(
+        jnp.where(routes[None, :, :] == experts[:, None, None], gate_values[None], 0.0), axis=2
+    )
+    full_in, full_o, cot_all, gates_all = gather_inputs(w_in, w_out, cotangent, gates)
+    full_q = full_in[:, :q_columns]
+    full_k = full_in[:, q_columns : q_columns + kv_columns]
+    full_v = full_in[:, q_columns + kv_columns : q_columns + 2 * kv_columns]
+    both_gains = full_in[:, q_columns + 2 * kv_columns :][:, :2].astype(jnp.float32).T
+    gain_attn_f, gain_moe_f = both_gains[0], both_gains[1]
+    inputs = tokens.astype(jnp.float32)
+    normed_low = rms_norm(inputs, gain_attn_f).astype(jnp.bfloat16)
+    pre = jnp.dot(
+        normed_low, full_in[:, : q_columns + 2 * kv_columns], preferred_element_type=jnp.float32
+    )
+    query_pre = pre[:, :q_columns]
+    key_pre = pre[:, q_columns : q_columns + kv_columns]
+    value_pre = pre[:, q_columns + kv_columns :]
+    query = rotate(query_pre.reshape(tok_rows, HEADS, HD), within_own, 1.0).astype(jnp.bfloat16)
+    key_low = rotate(key_pre.reshape(tok_rows, KVH, HD), within_own, 1.0).astype(jnp.bfloat16)
+    key_low = key_low.reshape(tok_rows, kv_columns)
+    all_kv = gather_line(jnp.concatenate([key_low, value_pre.astype(jnp.bfloat16)], axis=1))
+    all_keys, all_values = all_kv[:, :kv_columns], all_kv[:, kv_columns:]
+    per_group = HEADS // KVH
+    score_scale = HD ** (-0.5)
+    query_groups = query.reshape(tok_rows, KVH, per_group, HD)
+
+    def softmax_weights(group_number):
+        keys_part = all_keys[:, group_number * HD : (group_number + 1) * HD]
+        raw = jnp.einsum(
+            "qjd,kd->jqk",
+            query_groups[:, group_number],
+            keys_part,
+            preferred_element_type=jnp.float32,
+        )
+        scores = jnp.where(allowed[None], raw * score_scale, masked_score)
+        row_top = jnp.max(scores, axis=-1, keepdims=True)
+        expo = jnp.exp(scores - row_top)
+        return expo / jnp.sum(expo, axis=-1, keepdims=True)
+
+    mixed_parts = []
+    for group_number in range(KVH):
+        probs = softmax_weights(group_number)
+        values_part = all_values[:, group_number * HD : (group_number + 1) * HD]
+        mixed_group = jnp.einsum(
+            "jqk,kd->qjd",
+            probs.astype(jnp.bfloat16),
+            values_part,
+            preferred_element_type=jnp.float32,
+        )
+        mixed_parts.append(mixed_group.reshape(tok_rows, per_group * HD))
+    mixed_low = jnp.concatenate(mixed_parts, axis=1).astype(jnp.bfloat16)
+    middle = inputs + jnp.dot(mixed_low, full_o, preferred_element_type=jnp.float32)
+    routed_low = rms_norm(middle, gain_moe_f).astype(jnp.bfloat16)
+
+    routed_all = gather_plane(routed_low)
+    my_expert = lax.axis_index("dp")
+    gate_mine = lax.dynamic_index_in_dim(
+        gates_all.reshape(8, 8, tok_rows), my_expert, axis=1, keepdims=False
+    ).reshape(8 * tok_rows, 1)
+    w_gate_e, w_up_e, w_down_e = w_gate[0], w_up[0], w_down[0]
+    gate_act = jnp.dot(routed_all, w_gate_e, preferred_element_type=jnp.float32)
+    up_act = jnp.dot(routed_all, w_up_e, preferred_element_type=jnp.float32)
+    hidden_low = (jax.nn.silu(gate_act) * up_act).astype(jnp.bfloat16)
+    grad_arrived = (cot_all.astype(jnp.float32) * gate_mine).astype(jnp.bfloat16)
+    grad_hidden = jnp.einsum(
+        "cd,fd->cf", grad_arrived, w_down_e, preferred_element_type=jnp.float32
+    )
+    grad_w_down = jnp.einsum(
+        "cf,cd->fd", hidden_low, grad_arrived, preferred_element_type=jnp.float32
+    )
+    glu_value, glu_pull = jax.vjp(
+        lambda gate_in, up_in: jax.nn.silu(gate_in) * up_in, gate_act, up_act
+    )
+    grad_gate, grad_up = glu_pull(grad_hidden)
+    grad_gate_low = grad_gate.astype(jnp.bfloat16)
+    grad_up_low = grad_up.astype(jnp.bfloat16)
+    grad_w_gate = jnp.einsum(
+        "cd,cf->df", routed_all, grad_gate_low, preferred_element_type=jnp.float32
+    )
+    grad_w_up = jnp.einsum(
+        "cd,cf->df", routed_all, grad_up_low, preferred_element_type=jnp.float32
+    )
+    expert_sums = (
+        lax.psum(grad_w_gate.astype(jnp.bfloat16), "ctx").astype(jnp.float32),
+        lax.psum(grad_w_up.astype(jnp.bfloat16), "ctx").astype(jnp.float32),
+        lax.psum(grad_w_down.astype(jnp.bfloat16), "ctx").astype(jnp.float32),
+    )
+    grad_sent = (
+        jnp.einsum("cf,df->cd", grad_gate_low, w_gate_e, preferred_element_type=jnp.float32)
+        + jnp.einsum("cf,df->cd", grad_up_low, w_up_e, preferred_element_type=jnp.float32)
+    ).astype(jnp.bfloat16)
+    grad_routed = reduce_plane(grad_sent, 3)
+    produced = jnp.dot(hidden_low, w_down_e, preferred_element_type=jnp.float32)
+    produced = produced.astype(jnp.bfloat16).astype(jnp.float32) * gate_mine
+    moe_out = reduce_plane(produced.astype(jnp.bfloat16), 4)
+    layer_out = (middle + moe_out).astype(jnp.bfloat16)
+
+    grad_out = cotangent.astype(jnp.float32)
+    norm_value, moe_pull = jax.vjp(rms_norm, middle, gain_moe_f)
+    grad_mid_norm, grad_gain_moe = moe_pull(grad_routed)
+    grad_middle = grad_out + grad_mid_norm
+    grad_attn_low = grad_middle.astype(jnp.bfloat16)
+    grad_w_out = jnp.einsum(
+        "th,td->hd", mixed_low, grad_attn_low, preferred_element_type=jnp.float32
+    )
+    grad_mixed_low = jnp.einsum(
+        "td,hd->th", grad_attn_low, full_o, preferred_element_type=jnp.float32
+    ).astype(jnp.bfloat16)
+    grad_mixed_groups = grad_mixed_low.reshape(tok_rows, KVH, per_group, HD)
+    grad_query_parts = []
+    key_pieces = []
+    value_pieces = []
+    for group_number in range(KVH):
+        probs = softmax_weights(group_number)
+        keys_part = all_keys[:, group_number * HD : (group_number + 1) * HD]
+        values_part = all_values[:, group_number * HD : (group_number + 1) * HD]
+        grad_probs = jnp.einsum(
+            "qjd,kd->jqk",
+            grad_mixed_groups[:, group_number],
+            values_part,
+            preferred_element_type=jnp.float32,
+        )
+        grad_scores = probs * (grad_probs - jnp.sum(probs * grad_probs, axis=-1, keepdims=True))
+        grad_raw_low = (grad_scores * score_scale).astype(jnp.bfloat16)
+        grad_query_parts.append(
+            jnp.einsum("jqk,kd->qjd", grad_raw_low, keys_part, preferred_element_type=jnp.float32)
+        )
+        key_pieces.append(
+            jnp.einsum(
+                "jqk,qjd->kd",
+                grad_raw_low,
+                query_groups[:, group_number],
+                preferred_element_type=jnp.float32,
+            )
+        )
+        value_pieces.append(
+            jnp.einsum(
+                "jqk,qjd->kd",
+                probs.astype(jnp.bfloat16),
+                grad_mixed_groups[:, group_number],
+                preferred_element_type=jnp.float32,
+            )
+        )
+    grad_query_rot = jnp.stack(grad_query_parts, axis=1).reshape(tok_rows, HEADS, HD)
+    key_value_grads = reduce_line(
+        jnp.concatenate(key_pieces + value_pieces, axis=1).astype(jnp.bfloat16)
+    )
+    grad_query_low = (
+        rotate(grad_query_rot, within_own, -1.0).astype(jnp.bfloat16).reshape(tok_rows, q_columns)
+    )
+    grad_key_rot = key_value_grads[:, :kv_columns].reshape(tok_rows, KVH, HD)
+    grad_key_low = (
+        rotate(grad_key_rot, within_own, -1.0).astype(jnp.bfloat16).reshape(tok_rows, kv_columns)
+    )
+    grad_value_low = key_value_grads[:, kv_columns:].astype(jnp.bfloat16)
+    grad_pre = jnp.concatenate([grad_query_low, grad_key_low, grad_value_low], axis=1)
+    grad_w_in = jnp.einsum("td,th->dh", normed_low, grad_pre, preferred_element_type=jnp.float32)
+    grad_normed = jnp.einsum(
+        "th,dh->td",
+        grad_pre,
+        full_in[:, : q_columns + 2 * kv_columns],
+        preferred_element_type=jnp.float32,
+    )
+    first_value, attn_pull = jax.vjp(rms_norm, inputs, gain_attn_f)
+    grad_inputs, grad_gain_attn = attn_pull(grad_normed)
+    grad_tokens = grad_middle + grad_inputs
+    grad_gains = jnp.pad(jnp.stack([grad_gain_attn, grad_gain_moe], axis=1), ((0, 0), (0, LANES - 2)))
+    dense = reduce_all(
+        jnp.concatenate([grad_w_in, grad_gains, grad_w_out], axis=1).astype(jnp.bfloat16)
+    )
+    edge = q_columns + 2 * kv_columns
+    return (
+        layer_out,
+        grad_tokens,
+        dense[:, edge],
+        dense[:, :q_columns],
+        dense[:, q_columns : q_columns + kv_columns],
+        dense[:, q_columns + kv_columns : edge],
+        dense[:, edge + LANES :],
+        dense[:, edge + 1],
+        expert_sums[0][None],
+        expert_sums[1][None],
+        expert_sums[2][None],
+    )
+
+
 def solution(mesh):
+    on_plane = mesh.shape["dp"] == 8 and mesh.shape["ctx"] == LINE
     return jax.shard_map(
-        on_device,
+        on_plane_device if on_plane else on_device,
         mesh=mesh,
         in_specs=(
             P(("dp", "ctx"), None),

time: 1430 us -> 747 us (0.52)
  waiting for transfers between devices: 757 us -> 0.02 us
  Pallas kernels: 0 us -> 482 us
  blocking collectives: 320 us -> 0 us
  local copies, waits for them, and re-layouts: 87.1 us -> 23 us
  starting transfers between devices: 20.2 us -> 0.04 us
    reduce_scatter x5 -> x0, waiting for transfers between devices: 486 us -> none  [the longest x1 142 us: spread_grads(): lax.psum_scatter(grad_query, ('dp', 'ctx'), scatter_dimension=0, tiled=True)]
    pallas_call x0 -> x7, Pallas kernels: none -> 482 us  [the longest x1 135 us: gather_inputs(): pl.pallas_call(kernel, out_shape=(jax.ShapeDtypeStruct((planes * group, w...]
    all_gather x4 -> x0, blocking collectives: 178 us -> none  [the longest x1 73.6 us: collect_weights(): lax.all_gather(w_key, ('dp', 'ctx'), axis=0, tiled=True)]
    psum x1, waiting for transfers between devices: 157 us -> 0.01 us  [on_plane_device(): lax.psum(grad_w_gate.astype(jnp.bfloat16), 'ctx').astype(jnp.float32)]
    unnamed x2 -> x0, blocking collectives: 142 us -> none
    all_to_all x4 -> x0, waiting for transfers between devices: 112 us -> none  [the longest x1 47.6 us: on_device(): lax.all_to_all(grad_sent, 'dp', split_axis=0, concat_axis=0, tiled=True)]
    gather x4 -> x0, local copies, waits for them, and re-layouts: 39.5 us -> none  [the longest x1 12.7 us: on_device(): grad_slots = grad_padded[owner].reshape(experts_total, capacity, D)]
    all_to_all x4 -> x0, starting transfers between devices: 19.9 us -> none  [the longest x1 5.32 us: on_device(): lax.all_to_all(grad_slots, 'dp', split_axis=0, concat_axis=0, tiled=True)]
  transfers between devices with their start and end apart: 12 -> 1, of which waited for: 9 -> 0; matrix products, arithmetic and copies ran while one was open for 15% -> 17% of each run, Pallas kernels for 0% -> 38%
where the time goes in v1:
time: 747 us; the launch traced here: 742 us
  Pallas kernels  482 us (65%)
  matrix products  180 us (24%)
  other arithmetic  42.4 us (6%)
  local copies, waits for them, and re-layouts  23 us (3%)
  between operations  15 us (2%)
    pallas_call x1, Pallas kernels, gather_inputs(): pl.pallas_call(kernel, out_shape=(jax.ShapeDtypeStruct((planes * group, w...  135 us
    pallas_call x1, Pallas kernels, reduce_all(): pl.pallas_call(kernel, out_shape=jax.ShapeDtypeStruct((rows, columns), jn...  109 us
    pallas_call x1, Pallas kernels, reduce_line(): pl.pallas_call(kernel, out_shape=jax.ShapeDtypeStruct((rows, columns), jn...  105 us
    pallas_call x2, Pallas kernels, reduce_plane(): pl.pallas_call(kernel, out_shape=jax.ShapeDtypeStruct((rows, columns), jn...  71.4 us
    pallas_call x1, Pallas kernels, gather_plane(): pl.pallas_call(kernel, out_shape=jax.ShapeDtypeStruct((8 * rows, columns)...  35.2 us
    pallas_call x1, Pallas kernels, gather_line(): pl.pallas_call(kernel, out_shape=jax.ShapeDtypeStruct((LINE * rows, colum...  26.2 us
    dot_general x2, matrix products, on_plane_device(): jnp.einsum('jqk,kd->qjd', grad_raw_low, keys_part, preferred_element_type...  22.7 us
    dot_general x2, matrix products, on_plane_device(): jnp.einsum('jqk,qjd->kd', grad_raw_low, query_groups[:, group_number], pr...  21.9 us
  transfers between devices with their start and end apart: 1, of which 0 were waited for; matrix products, arithmetic and copies ran while one was open for 17% of the time, Pallas kernels for 38%

profile of v1, /device:TPU:0, one launch (start us, length us, event | category | flops | bytes accessed | tf_op | source)
XLA Modules:
  0.0 742.2 jit_solution(13505931310863139843)
XLA Ops:
  11.2 135.3 %gather_inputs.1 = (bf16[1536,2176]{1,0:T(8,128)(2,1)}, bf16[1536,1536]{1,0:T(8,128)(2,1)}, bf16[2048,1536]{1,0:T(8,128)(2,1)}, f32[64,256]{1,0:T(8,128)}) custom-call(bf16[48,2176]{1,0:T(8,128)(2,1)} %fusion.128.in_ref, bf16[48,1536]{1,0:T(8,128)(2,1)} %out_ref.1, bf16[256,1536]{1,0:T(8,128)(2,1)} %cot_ref.1, f32[8,256]{1,0:T(8,128)} %select_reduce_fusion.gate_ref), custom_call_target="tpu_custom_call" | custom-call | tf_op jit(solution)/shard_map/gather_inputs/pallas_call | solution.py:701
  159.9 26.2 %gather_line.1 = bf16[1024,512]{1,0:T(8,128)(2,1)} custom-call(bf16[256,512]{1,0:T(8,128)(2,1)} %pad_maximum_fusion.10.block_ref), custom_call_target="tpu_custom_call" | custom-call | tf_op jit(solution)/shard_map/gather_line/pallas_call | solution.py:734
  196.3 6.2 fusion.169
  202.5 6.4 fusion.164
  219.7 35.2 %gather_plane.1 = bf16[2048,1536]{1,0:T(8,128)(2,1)} custom-call(bf16[256,1536]{1,0:T(8,128)(2,1)} %multiply_convert_fusion.6.block_ref), custom_call_target="tpu_custom_call" | custom-call | tf_op jit(solution)/shard_map/gather_plane/pallas_call | solution.py:764
  254.9 9.7 %fusion.43 = f32[2048,768]{1,0:T(8,128)} fusion(bf16[2048,1536]{1,0:T(8,128)(2,1)} %gather_plane.1, bf16[1,1536,768]{2,1,0:T(8,128)(2,1)} %param.22), kind=kOutput, calls=%fused_computation.76 | convolution fusion | flops 4831838208 | bytes 14942208 | tf_op jit(solution)/shard_map/dot_general | solution.py:945
  264.6 7.1 fusion.47
  272.5 11.0 %multiply_convert_fusion.2 = (bf16[2048,768]{1,0:T(8,128)(2,1)S(1)}, bf16[2048,768]{1,0:T(8,128)(2,1)S(1)}, bf16[2048,768]{1,0:T(8,128)(2,1)S(1)}) fusion(f32[2048,768]{1,0:T(8,128)} %fusion.47, f32[2048,768]{1,0:T(8,128)} %fusion.43, bf16[1,768,1536]{2,1,0:T(8,128)(2,1)S(1)} %copy-done, bf16[2048,1536]{1,0:T(8,128)(2,1)} %get-tuple-element.18, ...), kind=kOutput, calls=%fused_computation.32 | convolution fusion | flops 4866441216 | bytes 30679040 | tf_op jit(solution)/shard_map/cd,fd->cf/dot_general | solution.py:948
  283.6 12.6 %fusion.30 = bf16[1,1536,768]{2,1,0:T(8,128)(2,1)} fusion(bf16[2048,1536]{1,0:T(8,128)(2,1)} %gather_plane.1, bf16[2048,768]{1,0:T(8,128)(2,1)S(1)} %get-tuple-element.35), kind=kOutput, calls=%fused_computation.60 | convolution fusion | flops 4833017856 | bytes 11796480 | tf_op jit(solution)/shard_map/cd,cf->df/dot_general | solution.py:960
  296.2 9.5 %fusion.31 = bf16[1,1536,768]{2,1,0:T(8,128)(2,1)} fusion(bf16[2048,1536]{1,0:T(8,128)(2,1)} %gather_plane.1, bf16[2048,768]{1,0:T(8,128)(2,1)S(1)} %get-tuple-element.34), kind=kOutput, calls=%fused_computation.61 | convolution fusion | flops 4833017856 | bytes 11796480 | tf_op jit(solution)/shard_map/cd,cf->df/dot_general | solution.py:963
  305.7 6.9 fusion.32
  312.6 9.6 %multiply_convert_fusion.1.part_ref = bf16[2048,1536]{1,0:T(8,128)(2,1)} fusion(bf16[2048,768]{1,0:T(8,128)(2,1)} %copy-done.42, f32[2048]{0:T(1024)S(1)} %bitcast.271, bf16[1,768,1536]{2,1,0:T(8,128)(2,1)S(1)} %copy-done), kind=kOutput, calls=%fused_computation.10 | convolution fusion | flops 4844421120 | bytes 11804672 | tf_op jit(solution)/shard_map/dot_general | solution.py:976
  322.2 8.3 %fusion.45 = f32[2048,1536]{1,0:T(8,128)} fusion(bf16[2048,768]{1,0:T(8,128)(2,1)S(1)} %copy-done.41, bf16[1,1536,768]{2,1,0:T(8,128)(2,1)S(1)} %copy-done.36), kind=kOutput, calls=%fused_computation.78 | convolution fusion | flops 4831838208 | bytes 18087936 | tf_op jit(solution)/shard_map/cf,df->cd/dot_general | solution.py:972
  330.5 35.9 %reduce_plane_4.1 = f32[256,1536]{1,0:T(8,128)} custom-call(bf16[2048,1536]{1,0:T(8,128)(2,1)} %multiply_convert_fusion.1.part_ref), custom_call_target="tpu_custom_call" | custom-call | tf_op jit(solution)/shard_map/reduce_plane_4/pallas_call | solution.py:786
  366.5 10.9 %add_convert_fusion.part_ref = bf16[2048,1536]{1,0:T(8,128)(2,1)} fusion(f32[2048,1536]{1,0:T(8,128)} %fusion.45, bf16[2048,768]{1,0:T(8,128)(2,1)} %copy-done.39, bf16[1,1536,768]{2,1,0:T(8,128)(2,1)S(1)} %copy-done.37), kind=kOutput, calls=%fused_computation.8 | convolution fusion | flops 4838129664 | bytes 24379392 | tf_op jit(solution)/shard_map/cf,df->cd/dot_general | solution.py:973
  377.3 35.5 %reduce_plane_3.1 = f32[256,1536]{1,0:T(8,128)} custom-call(bf16[2048,1536]{1,0:T(8,128)(2,1)} %add_convert_fusion.part_ref), custom_call_target="tpu_custom_call" | custom-call | tf_op jit(solution)/shard_map/reduce_plane_3/pallas_call | solution.py:786
  433.0 10.7 %fusion.82 = bf16[1024,128]{1,0:T(8,128)(2,1)} fusion(bf16[256,6,128]{2,0,1:T(8,128)(2,1)S(1)} %copy-done.25, f32[1024,256,6]{1,0,2:T(8,128)} %fusion.101, f32[6,256,1024]{1,2,0:T(8,128)} %get-tuple-element.58, f32[6,256]{1,0:T(8,128)} %get-tuple-element.57), kind=kOutput, calls=%fused_computation.113 | convolution fusion | flops 413796864 | bytes 13244416 | tf_op jit(solution)/shard_map/jqk,qjd->kd/dot_general | solution.py:1012
  443.8 11.1 %fusion.81 = bf16[1024,128]{1,0:T(8,128)(2,1)} fusion(f32[1024,256,6]{1,0,2:T(8,128)} %fusion.100, bf16[256,2,6,64]{3,0,2,1:T(8,128)(2,1)S(1)} %bitcast.256, bf16[256,2,6,64]{3,0,2,1:T(8,128)(2,1)S(1)} %bitcast.253, f32[6,256,1024]{1,2,0:T(8,128)} %get-tuple-element.60, f32[6,256]{1,0:T(8,128)S(1)} %copy-done.44), kind=kOutput, calls=%fused_computation.112 | convolution fusion | flops 414583296 | bytes 27017216 | tf_op jit(solution)/shard_map/jqk,qjd->kd/dot_general | solution.py:1012
  457.3 104.6 %reduce_line.1 = f32[256,512]{1,0:T(8,128)} custom-call(bf16[1024,512]{1,0:T(8,128)(2,1)} %pad_maximum_fusion.1.part_ref), custom_call_target="tpu_custom_call" | custom-call | tf_op jit(solution)/shard_map/reduce_line/pallas_call | solution.py:808
  568.1 11.2 %fusion.66 = f32[256,1,6,128]{0,3,2,1:T(8,128)} fusion(f32[1024,256,6]{1,0,2:T(8,128)} %fusion.100, bf16[1024,512]{1,0:T(8,128)(2,1)S(1)} %copy-done.14, f32[6,256,1024]{1,2,0:T(8,128)} %get-tuple-element.60, f32[6,256]{1,0:T(8,128)S(1)} %copy-done.44), kind=kOutput, calls=%fused_computation.105 | convolution fusion | flops 413665792 | bytes 26230784 | tf_op jit(solution)/shard_map/jqk,kd->qjd/dot_general | solution.py:1009
  579.4 11.5 %fusion.65 = f32[256,1,6,128]{0,3,2,1:T(8,128)} fusion(f32[1024,256,6]{1,0,2:T(8,128)} %fusion.101, bf16[1024,512]{1,0:T(8,128)(2,1)S(1)} %copy-done.14, f32[6,256,1024]{1,2,0:T(8,128)} %get-tuple-element.58, f32[6,256]{1,0:T(8,128)S(1)} %copy-done.47), kind=kOutput, calls=%fused_computation.104 | convolution fusion | flops 413665792 | bytes 26230784 | tf_op jit(solution)/shard_map/jqk,kd->qjd/dot_general | solution.py:1009
  592.8 6.5 fusion.52
  604.8 5.0 fusion.7.part_ref
  609.8 109.1 %reduce_all.1 = f32[48,3712]{1,0:T(8,128)} custom-call(bf16[1536,3712]{1,0:T(8,128)(2,1)} %fusion.7.part_ref), custom_call_target="tpu_custom_call" | custom-call | tf_op jit(solution)/shard_map/reduce_all/pallas_call | solution.py:837
  (199 shorter events, 91.2 us)
Async XLA Ops:
  7.2 265.4 %copy-start = (bf16[1,768,1536]{2,1,0:T(8,128)(2,1)S(1)}, bf16[1,768,1536]{2,1,0:T(8,128)(2,1)}, u32[]{:S(2)}) copy-start(bf16[1,768,1536]{2,1,0:T(8,128)(2,1)} %param.23) | copy-start | bytes 7077892
  7.2 718.2 %all-reduce.5.cloned.1.call-start = ((), (), s32[]{:S(2)}) async-start(), calls=%async_computation | async-start | bytes 14155776 | tf_op jit(solution)/shard_map/psum | solution.py:967
  192.8 9.7 %copy-start.8 = (bf16[256,12,64]{2,0,1:T(8,128)(2,1)}, bf16[256,12,64]{2,0,1:T(8,128)(2,1)S(1)}, u32[]{:S(2)}) copy-start(bf16[256,12,64]{2,0,1:T(8,128)(2,1)S(1)} %copy.139) | copy-start | bytes 1179652
  196.3 12.7 %copy-start.24 = (bf16[256,6,128]{2,0,1:T(8,128)(2,1)}, bf16[256,6,128]{2,0,1:T(8,128)(2,1)S(1)}, u32[]{:S(2)}) copy-start(bf16[256,6,128]{2,0,1:T(8,128)(2,1)S(1)} %fusion.97) | copy-start | bytes 1179652
  202.5 10.1 %copy-start.43 = (f32[6,256]{1,0:T(8,128)}, f32[6,256]{1,0:T(8,128)S(1)}, u32[]{:S(2)}) copy-start(f32[6,256]{1,0:T(8,128)S(1)} %get-tuple-element.59) | copy-start | bytes 18436
  254.9 9.7 %copy-start.6 = (bf16[2048,1536]{1,0:T(8,128)(2,1)S(1)}, bf16[2048,1536]{1,0:T(8,128)(2,1)}, u32[]{:S(2)}) copy-start(bf16[2048,1536]{1,0:T(8,128)(2,1)} %gather_plane.1) | copy-start | bytes 18874372
  254.9 9.7 %copy-start.35 = (bf16[1,1536,768]{2,1,0:T(8,128)(2,1)S(1)}, bf16[1,1536,768]{2,1,0:T(8,128)(2,1)}, u32[]{:S(2)}) copy-start(bf16[1,1536,768]{2,1,0:T(8,128)(2,1)} %param.21) | copy-start | bytes 7077892
  283.5 12.7 %copy-start.40 = (bf16[2048,768]{1,0:T(8,128)(2,1)}, bf16[2048,768]{1,0:T(8,128)(2,1)S(1)}, u32[]{:S(2)}) copy-start(bf16[2048,768]{1,0:T(8,128)(2,1)S(1)} %get-tuple-element.35) | copy-start | bytes 9437188
  283.6 12.7 %copy-start.39 = (bf16[2048,768]{1,0:T(8,128)(2,1)}, bf16[2048,768]{1,0:T(8,128)(2,1)S(1)}, u32[]{:S(2)}) copy-start(bf16[2048,768]{1,0:T(8,128)(2,1)S(1)} %get-tuple-element.34) | copy-start | bytes 9437188
  283.6 22.1 %copy-start.42 = (bf16[2048,768]{1,0:T(8,128)(2,1)}, bf16[2048,768]{1,0:T(8,128)(2,1)S(1)}, u32[]{:S(2)}) copy-start(bf16[2048,768]{1,0:T(8,128)(2,1)S(1)} %get-tuple-element.36) | copy-start | bytes 9437188
  283.6 22.1 %slice-start = ((s8[6291456]{0:T(1024)(128)(4,1)}), s8[4194304]{0:T(1024)(128)(4,1)S(1)}, s32[]{:S(2)}) async-start(s8[6291456]{0:T(1024)(128)(4,1)} %bitcast.276), calls=%async_computation.1 | async-start | bytes 8388608
  330.5 35.9 %copy-start.37 = (bf16[1,1536,768]{2,1,0:T(8,128)(2,1)S(1)}, bf16[1,1536,768]{2,1,0:T(8,128)(2,1)}, u32[]{:S(2)}) copy-start(bf16[1,1536,768]{2,1,0:T(8,128)(2,1)} %param.22) | copy-start | bytes 7077892
  377.3 35.5 %copy-start.3 = (f32[256,1536]{1,0:T(8,128)S(1)}, f32[256,1536]{1,0:T(8,128)}, u32[]{:S(2)}) copy-start(f32[256,1536]{1,0:T(8,128)} %copy-done.2) | copy-start | bytes 4718596
  377.3 37.5 %copy-start.7 = (bf16[256,1536]{1,0:T(8,128)(2,1)S(1)}, bf16[256,1536]{1,0:T(8,128)(2,1)}, u32[]{:S(2)}) copy-start(bf16[256,1536]{1,0:T(8,128)(2,1)} %cot_ref.1) | copy-start | bytes 2359300
  433.0 10.7 %copy-start.9 = (bf16[256,12,64]{2,0,1:T(8,128)(2,1)S(1)}, bf16[256,12,64]{2,0,1:T(8,128)(2,1)}, u32[]{:S(2)}) copy-start(bf16[256,12,64]{2,0,1:T(8,128)(2,1)} %copy-done.8) | copy-start | bytes 1179652
  433.0 10.7 %copy-start.10 = (bf16[256,12,64]{2,0,1:T(8,128)(2,1)S(1)}, bf16[256,12,64]{2,0,1:T(8,128)(2,1)}, u32[]{:S(2)}) copy-start(bf16[256,12,64]{2,0,1:T(8,128)(2,1)} %copy.138) | copy-start | bytes 1179652
  443.8 120.2 %copy-start.16 = (f32[256,64]{0,1:T(8,128)S(1)}, f32[256,64]{0,1:T(8,128)}, u32[]{:S(2)}) copy-start(f32[256,64]{0,1:T(8,128)} %get-tuple-element.51) | copy-start | bytes 196612
  443.8 120.3 %copy-start.17 = (f32[256,64]{0,1:T(8,128)S(1)}, f32[256,64]{0,1:T(8,128)}, u32[]{:S(2)}) copy-start(f32[256,64]{0,1:T(8,128)} %get-tuple-element.52) | copy-start | bytes 196612
  454.9 113.2 %copy-start.14 = (bf16[1024,512]{1,0:T(8,128)(2,1)S(1)}, bf16[1024,512]{1,0:T(8,128)(2,1)}, u32[]{:S(2)}) copy-start(bf16[1024,512]{1,0:T(8,128)(2,1)} %gather_line.1) | copy-start | bytes 3145732
  568.1 11.2 %copy-start.47 = (f32[6,256]{1,0:T(8,128)S(1)}, f32[6,256]{1,0:T(8,128)}, u32[]{:S(2)}) copy-start(f32[6,256]{1,0:T(8,128)} %get-tuple-element.57) | copy-start | bytes 18436
  609.8 110.6 %copy-start.32 = (f32[256]{0:T(256)S(1)}, f32[256]{0:T(256)}, u32[]{:S(2)}) copy-start(f32[256]{0:T(256)} %copy-done.31) | copy-start | bytes 3076
  609.8 110.6 %copy-start.33 = (f32[256]{0:T(256)S(1)}, f32[256]{0:T(256)}, u32[]{:S(2)}) copy-start(f32[256]{0:T(256)} %get-tuple-element.22) | copy-start | bytes 3076
  609.8 114.0 %copy-start.15 = (f32[256,1536]{1,0:T(8,128)S(1)}, f32[256,1536]{1,0:T(8,128)}, u32[]{:S(2)}) copy-start(f32[256,1536]{1,0:T(8,128)} %get-tuple-element.63) | copy-start | bytes 4718596
  609.8 114.0 %copy-start.30 = (f32[256]{0:T(256)S(1)}, f32[256]{0:T(256)}, u32[]{:S(2)}) copy-start(f32[256]{0:T(256)} %copy-done.28) | copy-start | bytes 3076
  (35 other events, 151.7 us)
Sparse Core Ops, SparseCore 0:
  312.7 262.0 all-reduce.4

commit v2 on v1

--- a/solution.py
+++ b/solution.py
@@ -476,12 +476,13 @@
 
 class PlaneReduce:
     COPIES = 10
-
-    def __init__(self, wires, part, group, core_in, first_in, second_in):
+    STEPS = 6
+
+    def __init__(self, wires, part, group, own, own_row, core_in, first_in, second_in, out):
         self.wires, self.part, self.group, self.half = wires, part, group, group // 2
+        self.own, self.own_row, self.out = own, own_row, out
         self.core_in, self.first_in, self.second_in = core_in, first_in, second_in
         self.first = wires.take(self.COPIES)
-        self.begun = []
 
     def _send(self, src, src_row, dst, dst_row, rows, number, to):
         return self.wires.copy(
@@ -507,44 +508,43 @@
         )[number]
         return self._send(self.core_in, src_row, dst, dst_row, h, 4 + number, to)
 
-    def start(self):
-        for slot in (3, 2, 1, 0):
-            self._core(slot).start()
-
     def _sum_core(self, slot):
         self._core(slot).wait()
-        row = pl.multiple_of(masked(self.wires.dp, 2 * slot) * self.group, 16)
-        add_rows(
-            self.core_in, slot * self.group, self.part, row, self.core_in, slot * self.group, self.group
-        )
-
-    def middle(self):
+        row = slot * self.group
+        add_rows(self.core_in, row, self.own, self.own_row(slot), self.core_in, row, self.group)
+
+    def _sum_far(self, number, row, in_row):
+        self._far(number).wait()
+        add_rows(self.core_in, row, self.core_in, row, self.first_in, in_row, self.half)
+
+    def step(self, number):
         g, h = self.group, self.half
-        self._sum_core(3)
-        self._far(0).start()
-        self._far(1).start()
-        self._sum_core(2)
-        self._far(2).start()
-        self._sum_core(1)
-        self._far(3).start()
-        self._sum_core(0)
-        self._far(0).wait()
-        add_rows(self.core_in, 1 * g, self.core_in, 1 * g, self.first_in, h, h)
-        self._far(4).start()
-        self._far(1).wait()
-        add_rows(self.core_in, 2 * g + h, self.core_in, 2 * g + h, self.first_in, 3 * h, h)
-        self._far(5).start()
-        self._far(2).wait()
-        add_rows(self.core_in, 0, self.core_in, 0, self.first_in, 0, h)
-        self._far(3).wait()
-        add_rows(self.core_in, h, self.core_in, h, self.first_in, 2 * h, h)
-
-    def finish(self, out):
-        h = self.half
-        self._far(4).wait()
-        add_rows(out, 0, self.core_in, 0, self.second_in, 0, h)
-        self._far(5).wait()
-        add_rows(out, h, self.core_in, h, self.second_in, h, h)
+        if number == 0:
+            for slot in (3, 2, 1, 0):
+                self._core(slot).start()
+        elif number == 1:
+            self._sum_core(3)
+            self._far(0).start()
+            self._far(1).start()
+        elif number == 2:
+            self._sum_core(2)
+            self._far(2).start()
+            self._sum_core(1)
+            self._far(3).start()
+            self._sum_core(0)
+        elif number == 3:
+            self._sum_far(0, 1 * g, h)
+            self._far(4).start()
+            self._sum_far(1, 2 * g + h, 3 * h)
+            self._far(5).start()
+        elif number == 4:
+            self._sum_far(2, 0, 0)
+            self._sum_far(3, h, 2 * h)
+        else:
+            self._far(4).wait()
+            add_rows(self.out, 0, self.core_in, 0, self.second_in, 0, h)
+            self._far(5).wait()
+            add_rows(self.out, h, self.core_in, h, self.second_in, h, h)
 
     @staticmethod
     def scratch(group, columns):
@@ -571,48 +571,48 @@
             z=z,
         )
 
-    def run(self, out):
+    def _moves(self, hop):
+        for way in (1, -1):
+            source = hop if way == 1 else LINE - 1 - hop
+            for block in range(LINE - 1, hop, -1) if way == 1 else range(0, LINE - 1 - hop):
+                yield way, block, source
+
+    def start(self, hop):
+        z = self.wires.z
+        for way, block, source in self._moves(hop):
+
+            @pl.when(z == source)
+            def _():
+                self._copy(way, hop, block, z + way).start()
+
+    def add(self, hop):
         z, rows = self.wires.z, self.rows
-        sends = []
-        for hop in range(LINE - 1):
-            for way in (1, -1):
-                source = hop if way == 1 else LINE - 1 - hop
-                blocks = range(LINE - 1, hop, -1) if way == 1 else range(0, LINE - 1 - hop)
-                for block in blocks:
-
-                    @pl.when(z == source)
-                    def _():
-                        self._copy(way, hop, block, z + way).start()
-
-                    sends.append((way, hop, block, source))
-            for way in (1, -1):
-                source = hop if way == 1 else LINE - 1 - hop
-                blocks = range(LINE - 1, hop, -1) if way == 1 else range(0, LINE - 1 - hop)
-                for block in blocks:
-
-                    @pl.when(z == source + way)
-                    def _():
-                        self._copy(way, hop, block, z).wait_recv()
-                        add_rows(
-                            self.part,
-                            block * rows,
-                            self.part,
-                            block * rows,
-                            self.landing,
-                            ((0 if way == 1 else 1) * LINE + block) * rows,
-                            rows,
-                        )
+        for way, block, source in self._moves(hop):
+
+            @pl.when(z == source + way)
+            def _():
+                self._copy(way, hop, block, z).wait_recv()
+                place = ((0 if way == 1 else 1) * LINE + block) * rows
+                add_rows(
+                    self.part, block * rows, self.part, block * rows, self.landing, place, rows
+                )
+
+    def finish(self, out):
+        z, rows = self.wires.z, self.rows
 
         @pl.loop(0, rows // 16)
         def _(step):
             row = pl.multiple_of(z * rows + step * 16, 16)
-            out[pl.ds(pl.multiple_of(step * 16, 16), 16), :] = self.part[pl.ds(row, 16), :].astype(out.dtype)
-
-        for way, hop, block, source in sends:
-
-            @pl.when(z == source)
-            def _():
-                self._copy(way, hop, block, z + way).wait_send()
+            out[pl.ds(pl.multiple_of(step * 16, 16), 16), :] = self.part[pl.ds(row, 16), :].astype(
+                out.dtype
+            )
+
+        for hop in range(LINE - 1):
+            for way, block, source in self._moves(hop):
+
+                @pl.when(z == source)
+                def _():
+                    self._copy(way, hop, block, z + way).wait_send()
 
     @staticmethod
     def scratch(rows, columns):
@@ -772,79 +772,463 @@
     )(block)
 
 
-def reduce_plane(part, collective_id):
-    rows, columns = part.shape[0] // 8, part.shape[1]
-
-    def kernel(part_ref, out_ref, core_in, first_in, second_in, send, recv):
+class LineSum:
+    def __init__(self, wires, own, out, landing, rows, chunks):
+        self.wires, self.own, self.out, self.landing = wires, own, out, landing
+        self.rows, self.chunks, self.now = rows, chunks, 0
+        self.first = wires.take(3 * chunks)
+        z = wires.z
+        self.inner = (z == 1) | (z == 2)
+        self.outer = (z == 0) | (z == 3)
+        self.end = 3 * (z - 1)
+        self.near = 1 + z // 3
+        self.peer = 3 - z
+
+    def _cut(self, ref, chunk):
+        return ref.at[pl.ds(pl.multiple_of(chunk * self.rows, 16), self.rows)]
+
+    def _in(self, chunk):
+        return self.wires.copy(
+            self._cut(self.own, chunk), self._cut(self.out, chunk), self.first + chunk, z=self.near
+        )
+
+    def _across(self, chunk):
+        number = self.first + self.chunks + chunk
+        return self.wires.copy(
+            self._cut(self.own, chunk), self._cut(self.landing, chunk), number, z=self.peer
+        )
+
+    def _back(self, chunk):
+        number = self.first + 2 * self.chunks + chunk
+        return self.wires.copy(
+            self._cut(self.out, chunk), self._cut(self.out, chunk), number, z=self.end
+        )
+
+    def begin(self):
+        @pl.when(self.outer)
+        def _():
+            for chunk in range(min(2, self.chunks)):
+                self._in(chunk).start()
+
+    def tick(self, count=1):
+        for _ in range(count):
+            if self.now <= self.chunks:
+                self._tick(self.now)
+            self.now += 1
+
+    def _tick(self, chunk):
+        if chunk < self.chunks:
+
+            @pl.when(self.outer)
+            def _():
+                self._in(chunk).wait_send()
+                if chunk + 2 < self.chunks:
+                    self._in(chunk + 2).start()
+
+        @pl.when(self.inner)
+        def _():
+            if chunk < self.chunks:
+                row = chunk * self.rows
+                self._in(chunk).wait_recv()
+                add_rows(self.own, row, self.own, row, self.out, row, self.rows)
+                self._across(chunk).start()
+            if chunk >= 1:
+                row = (chunk - 1) * self.rows
+                self._across(chunk - 1).wait_recv()
+                add_rows(self.out, row, self.own, row, self.landing, row, self.rows)
+                self._back(chunk - 1).start()
+
+    def finish(self):
+        self.tick(max(0, self.chunks + 1 - self.now))
+
+        @pl.when(self.outer)
+        def _():
+            @pl.loop(0, self.chunks)
+            def _(chunk):
+                self._back(chunk).wait_recv()
+
+        @pl.when(self.inner)
+        def _():
+            @pl.loop(0, self.chunks)
+            def _(chunk):
+                self._across(chunk).wait_send()
+                self._back(chunk).wait_send()
+
+
+def dot(left, right, left_dim, right_dim):
+    return lax.dot_general(
+        left, right, (((left_dim,), (right_dim,)), ((), ())), preferred_element_type=jnp.float32
+    )
+
+
+def norm_back(values, gain, grad):
+    scale = lax.rsqrt(jnp.mean(values * values, axis=-1, keepdims=True) + epsilon)
+    normal = values * scale
+    inner = grad * gain
+    to_values = scale * (inner - normal * jnp.mean(inner * normal, axis=-1, keepdims=True))
+    return to_values, grad * normal
+
+
+def turned(values, cosine, sine):
+    return values * cosine + pltpu.roll(values, HD // 2, 1) * sine
+
+
+CHUNK = 192
+SPLIT = 11
+
+
+def back_attention(
+    sums_in,
+    grad_sent,
+    full_o,
+    middle,
+    cotangent,
+    gain_moe,
+    mixed,
+    query,
+    all_kv,
+    lse,
+    starts,
+    cosine,
+    sine,
+):
+    tok_rows, width = middle.shape
+    keys, kv_width = all_kv.shape
+    w_rows = width
+    group = w_rows // 8
+    chunks = SPLIT
+
+    def kernel(
+        sums_ref, sent_ref, full_o_ref, middle_ref, cot_ref, gain_ref, mixed_ref, query_ref, kv_ref, lse_ref,
+        starts_ref, cos_ref, sin_ref,
+        total_ref, grad_mid_ref, grad_pre_ref, gain_row_ref, w_out_ref,
+        sums_own, sums_land, own, core_in, first_in, second_in, routed_grad, attn_low, mixed_grad, part_o, o_core,
+        o_first, o_second, bias, key_t, kv_grad, kv_part, kv_land, kv_out, here, send, recv,
+    ):
         wires = Wires(send, recv)
-        greet(wires, (1, 2, 4), False)
-        total = PlaneReduce(wires, part_ref, rows, core_in, first_in, second_in)
-        total.start()
-        total.middle()
-        total.finish(out_ref)
-
+        dp, z = wires.dp, wires.z
+        loads = [pltpu.make_async_copy(sums_ref.at[pl.ds(0, chunks * CHUNK)], sums_own, here.at[0])]
+        for slot in range(4):
+            row = pl.multiple_of(masked(dp, 2 * slot) * tok_rows, 16)
+            loads.append(
+                pltpu.make_async_copy(
+                    sent_ref.at[pl.ds(row, tok_rows)],
+                    own.at[pl.ds(slot * tok_rows, tok_rows)],
+                    here.at[1 + slot],
+                )
+            )
+        for one in loads:
+            one.start()
+        greet(wires, (1, 2, 4), True)
+        summed = LineSum(wires, sums_own, total_ref, sums_land, CHUNK, chunks)
+        plane = PlaneReduce(
+            wires, sent_ref, tok_rows, own, lambda slot: slot * tok_rows, core_in, first_in, second_in,
+            routed_grad,
+        )
+        dense = PlaneReduce(
+            wires, part_o, group, part_o, lambda slot: pl.multiple_of(masked(dp, 2 * slot) * group, 16),
+            o_core, o_first, o_second, w_out_ref,
+        )
+        line = LineReduce(wires, kv_part, tok_rows, kv_land)
+        plane.step(0)
+        loads[0].wait()
+        summed.begin()
+        key_place = lax.broadcasted_iota(jnp.int32, (keys, tok_rows), 0)
+        query_place = lax.broadcasted_iota(jnp.int32, (keys, tok_rows), 1) + z * tok_rows
+        allowed = (key_place >= starts_ref[0:1, :]) & (key_place <= query_place)
+        bias[...] = jnp.where(allowed, 0.0, masked_score)
+        key_t[...] = kv_ref[:, : kv_width // 2].astype(jnp.float32).T.astype(jnp.bfloat16)
+        kv_grad[...] = jnp.zeros_like(kv_grad)
+        for one in loads[1:]:
+            one.wait()
+        plane.step(1)
+        plane.step(2)
+        summed.tick()
+        summed.tick()
+        plane.step(3)
+        summed.tick()
+        plane.step(4)
+        summed.tick()
+        plane.step(5)
+
+        tile = 32
+        gain_row_ref[...] = jnp.zeros_like(gain_row_ref)
+
+        @pl.loop(0, tok_rows // tile)
+        def _(step):
+            cut = pl.ds(pl.multiple_of(step * tile, tile), tile)
+            to_middle, terms = norm_back(middle_ref[cut, :], gain_ref[1:2, :], routed_grad[cut, :])
+            to_middle = cot_ref[cut, :].astype(jnp.float32) + to_middle
+            grad_mid_ref[cut, :] = to_middle
+            attn_low[cut, :] = to_middle.astype(jnp.bfloat16)
+            gain_row_ref[0:1, :] += jnp.sum(terms, axis=0, keepdims=True)
+
+        wide = 512
+
+        @pl.loop(0, width // wide)
+        def _(step):
+            cut = pl.ds(pl.multiple_of(step * wide, wide), wide)
+            mixed_grad[:, cut] = dot(attn_low[...], full_o_ref[cut, :], 1, 1).astype(jnp.bfloat16)
+
+        @pl.loop(0, width // 256)
+        def _(step):
+            cut = pl.ds(pl.multiple_of(step * 256, 256), 256)
+            part_o[cut, :] = dot(mixed_ref[:, cut], attn_low[...], 0, 0).astype(jnp.bfloat16)
+
+        dense.step(0)
+        summed.tick()
+        score_scale = HD ** (-0.5)
+        per_group = HEADS // KVH
+
+        def heads(first, last):
+            @pl.loop(first, last)
+            def _(head):
+                own_cut = pl.ds(pl.multiple_of(head * HD, HD), HD)
+                pair = head // per_group
+                key_cut = pl.ds(pl.multiple_of(pair * HD, HD), HD)
+                value_cut = pl.ds(pl.multiple_of((KVH + pair) * HD, HD), HD)
+                q, do = query_ref[:, own_cut], mixed_grad[:, own_cut]
+                k, v = kv_ref[:, key_cut], kv_ref[:, value_cut]
+                scores = dot(k, q, 1, 1) * score_scale + bias[...]
+                probs = jnp.exp(scores - lse_ref[pl.ds(head, 1), :])
+                grad_probs = dot(v, do, 1, 1)
+                inner = jnp.sum(probs * grad_probs, axis=0, keepdims=True)
+                grad_raw = (probs * (grad_probs - inner) * score_scale).astype(jnp.bfloat16)
+                kv_grad[:, value_cut] += dot(probs.astype(jnp.bfloat16), do, 1, 0)
+                kv_grad[:, key_cut] += dot(grad_raw, q, 1, 0)
+                to_query = dot(key_t[key_cut, :], grad_raw, 1, 0).T
+                grad_pre_ref[:, own_cut] = turned(to_query, cos_ref[...], -sin_ref[...]).astype(
+                    jnp.bfloat16
+                )
+
+        heads(0, 3)
+        dense.step(1)
+        dense.step(2)
+        summed.tick()
+        heads(3, 6)
+        dense.step(3)
+        summed.tick()
+        heads(6, 9)
+        dense.step(4)
+        summed.tick()
+        heads(9, 12)
+        kv_part[...] = kv_grad[...].astype(jnp.bfloat16)
+        line.start(0)
+        dense.step(5)
+        summed.tick()
+        line.add(0)
+        line.start(1)
+        summed.tick()
+        line.add(1)
+        line.start(2)
+        summed.tick()
+        line.add(2)
+        line.finish(kv_out)
+        q_width = HEADS * HD
+        for pair in range(KVH):
+            cut = slice(pair * HD, (pair + 1) * HD)
+            grad_pre_ref[:, q_width + pair * HD : q_width + (pair + 1) * HD] = turned(
+                kv_out[:, cut], cos_ref[...], -sin_ref[...]
+            ).astype(jnp.bfloat16)
+        grad_pre_ref[:, q_width + kv_width // 2 :] = kv_out[:, kv_width // 2 :].astype(jnp.bfloat16)
+        summed.finish()
+
+    f32, low = jnp.float32, jnp.bfloat16
     return pl.pallas_call(
         kernel,
-        out_shape=jax.ShapeDtypeStruct((rows, columns), jnp.float32),
-        in_specs=[VMEM],
-        out_specs=VMEM,
-        scratch_shapes=PlaneReduce.scratch(rows, columns) + sems(PlaneReduce.COPIES),
-        compiler_params=kernel_params(collective_id, 60),
-        name=f"reduce_plane_{collective_id}",
-    )(part)
-
-
-def reduce_line(part):
-    rows, columns = part.shape[0] // LINE, part.shape[1]
-
-    def kernel(part_ref, out_ref, sums, landing, here, send, recv):
+        out_shape=(
+            jax.ShapeDtypeStruct((chunks * CHUNK, sums_in.shape[1]), low),
+            jax.ShapeDtypeStruct((tok_rows, width), f32),
+            jax.ShapeDtypeStruct((tok_rows, width + kv_width), low),
+            jax.ShapeDtypeStruct((8, width), f32),
+            jax.ShapeDtypeStruct((group, width), low),
+        ),
+        in_specs=[ANY, ANY] + [VMEM] * 11,
+        out_specs=(VMEM,) * 5,
+        scratch_shapes=[
+            pltpu.VMEM((chunks * CHUNK, sums_in.shape[1]), low),
+            pltpu.VMEM((chunks * CHUNK, sums_in.shape[1]), low),
+            pltpu.VMEM((4 * tok_rows, width), low),
+        ]
+        + PlaneReduce.scratch(tok_rows, width)
+        + [
+            pltpu.VMEM((tok_rows, width), f32),
+            pltpu.VMEM((tok_rows, width), low),
+            pltpu.VMEM((tok_rows, width), low),
+            pltpu.VMEM((w_rows, width), low),
+        ]
+        + PlaneReduce.scratch(group, width)
+        + [
+            pltpu.VMEM((keys, tok_rows), f32),
+            pltpu.VMEM((kv_width // 2, keys), low),
+            pltpu.VMEM((keys, kv_width), f32),
+            pltpu.VMEM((keys, kv_width), low),
+            LineReduce.scratch(tok_rows, kv_width),
+            pltpu.VMEM((tok_rows, kv_width), f32),
+            pltpu.SemaphoreType.DMA((5,)),
+        ]
+        + sems(3 * chunks + 2 * PlaneReduce.COPIES + LineReduce.COPIES),
+        compiler_params=kernel_params(3, 63),
+        name="back_attention",
+    )(
+        sums_in, grad_sent, full_o, middle, cotangent, gain_moe, mixed, query, all_kv, lse, starts, cosine, sine
+    )
+
+
+def back_dense(sums_in, produced, full_in, normed, grad_pre, tokens, gains, grad_mid, gain_row, w_out_part, middle):
+    tok_rows, width = middle.shape
+    in_width = full_in.shape[1]
+    pre_width = in_width - LANES
+    w_rows = width
+    group, rows = w_rows // 8, w_rows // (8 * LINE)
+    chunks = sums_in.shape[0] // CHUNK - SPLIT
+
+    def kernel(
+        sums_ref, prod_ref, full_ref, normed_ref, pre_ref, tok_ref, gain_ref, mid_grad_ref, gain_row_ref, o_part_ref,
+        middle_ref,
+        total_ref, layer_ref, tok_grad_ref, in_ref, out_ref,
+        sums_own, sums_land, own, core_in, first_in, second_in, moe, part, d_core, d_first, d_second, in_sums,
+        in_land, o_sums, o_land, normed_grad, gain_rows, here, send, recv,
+    ):
         wires = Wires(send, recv)
-        own = pltpu.make_async_copy(part_ref, sums, here.at[0])
-        own.start()
-        greet(wires, (), True)
-        own.wait()
-        LineReduce(wires, sums, rows, landing).run(out_ref)
-
+        dp, z = wires.dp, wires.z
+        loads = [
+            pltpu.make_async_copy(
+                sums_ref.at[pl.ds(SPLIT * CHUNK, chunks * CHUNK)], sums_own, here.at[0]
+            )
+        ]
+        for slot in range(4):
+            row = pl.multiple_of(masked(dp, 2 * slot) * tok_rows, 16)
+            loads.append(
+                pltpu.make_async_copy(
+                    prod_ref.at[pl.ds(row, tok_rows)],
+                    own.at[pl.ds(slot * tok_rows, tok_rows)],
+                    here.at[1 + slot],
+                )
+            )
+        for one in loads:
+            one.start()
+        greet(wires, (1, 2, 4), True)
+        summed = LineSum(wires, sums_own, total_ref, sums_land, CHUNK, chunks)
+        dense = PlaneReduce(
+            wires, part, group, part, lambda slot: pl.multiple_of(masked(dp, 2 * slot) * group, 16),
+            d_core, d_first, d_second, in_sums,
+        )
+        plane = PlaneReduce(
+            wires, prod_ref, tok_rows, own, lambda slot: slot * tok_rows, core_in, first_in, second_in, moe
+        )
+        o_line = LineReduce(wires, o_sums, rows, o_land)
+        in_line = LineReduce(wires, in_sums, rows, in_land)
+        loads[0].wait()
+        summed.begin()
+        o_sums[...] = o_part_ref[...]
+        wide = 512
+
+        @pl.loop(0, width // wide)
+        def _(step):
+            cut = pl.ds(pl.multiple_of(step * wide, wide), wide)
+            normed_grad[:, cut] = dot(pre_ref[...], full_ref[cut, :pre_width], 1, 1)
+
+        gain_rows[...] = jnp.zeros_like(gain_rows)
+        gain_rows[1:2, :] = gain_row_ref[0:1, :]
+        tile = 32
+
+        @pl.loop(0, tok_rows // tile)
+        def _(step):
+            cut = pl.ds(pl.multiple_of(step * tile, tile), tile)
+            to_tokens, terms = norm_back(
+                tok_ref[cut, :].astype(jnp.float32), gain_ref[0:1, :], normed_grad[cut, :]
+            )
+            tok_grad_ref[cut, :] = mid_grad_ref[cut, :] + to_tokens
+            gain_rows[0:1, :] += jnp.sum(terms, axis=0, keepdims=True)
+
+        part[:, pre_width:] = gain_rows[...].T.astype(jnp.bfloat16)
+
+        @pl.loop(0, w_rows // 256)
+        def _(step):
+            cut = pl.ds(pl.multiple_of(step * 256, 256), 256)
+            part[cut, :pre_width] = dot(normed_ref[:, cut], pre_ref[...], 0, 0).astype(jnp.bfloat16)
+
+        dense.step(0)
+        summed.tick()
+        dense.step(1)
+        dense.step(2)
+        summed.tick()
+        for one in loads[1:]:
+            one.wait()
+        summed.tick()
+        dense.step(3)
+        plane.step(0)
+        summed.tick()
+        dense.step(4)
+        o_line.start(0)
+        summed.tick()
+        dense.step(5)
+        in_line.start(0)
+        plane.step(1)
+        plane.step(2)
+        o_line.add(0)
+        o_line.start(1)
+        summed.tick()
+        in_line.add(0)
+        in_line.start(1)
+        plane.step(3)
+        summed.tick()
+        o_line.add(1)
+        o_line.start(2)
+        summed.tick()
+        in_line.add(1)
+        in_line.start(2)
+        plane.step(4)
+        summed.tick()
+        o_line.add(2)
+        in_line.add(2)
+        plane.step(5)
+
+        @pl.loop(0, tok_rows // tile)
+        def _(step):
+            cut = pl.ds(pl.multiple_of(step * tile, tile), tile)
+            layer_ref[cut, :] = (middle_ref[cut, :] + moe[cut, :]).astype(jnp.bfloat16)
+
+        o_line.finish(out_ref)
+        in_line.finish(in_ref)
+        summed.finish()
+
+    f32, low = jnp.float32, jnp.bfloat16
     return pl.pallas_call(
         kernel,
-        out_shape=jax.ShapeDtypeStruct((rows, columns), jnp.float32),
-        in_specs=[VMEM],
-        out_specs=VMEM,
+        out_shape=(
+            jax.ShapeDtypeStruct((chunks * CHUNK, sums_in.shape[1]), low),
+            jax.ShapeDtypeStruct((tok_rows, width), low),
+            jax.ShapeDtypeStruct((tok_rows, width), f32),
+            jax.ShapeDtypeStruct((rows, in_width), f32),
+            jax.ShapeDtypeStruct((rows, width), f32),
+        ),
+        in_specs=[ANY, ANY] + [VMEM] * 9,
+        out_specs=(VMEM,) * 5,
         scratch_shapes=[
-            pltpu.VMEM(part.shape, jnp.bfloat16),
-            LineReduce.scratch(rows, columns),
-            pltpu.SemaphoreType.DMA((1,)),
+            pltpu.VMEM((chunks * CHUNK, sums_in.shape[1]), low),
+            pltpu.VMEM((chunks * CHUNK, sums_in.shape[1]), low),
+            pltpu.VMEM((4 * tok_rows, width), low),
         ]
-        + sems(LineReduce.COPIES),
-        compiler_params=kernel_params(5, 60),
-        name="reduce_line",
-    )(part)
-
-
-def reduce_all(part):
-    rows, columns = part.shape[0] // (8 * LINE), part.shape[1]
-    group = LINE * rows
-
-    def kernel(part_ref, out_ref, core_in, first_in, second_in, sums, landing, send, recv):
-        wires = Wires(send, recv)
-        greet(wires, (1, 2, 4), True)
-        total = PlaneReduce(wires, part_ref, group, core_in, first_in, second_in)
-        total.start()
-        total.middle()
-        total.finish(sums)
-        LineReduce(wires, sums, rows, landing).run(out_ref)
-
-    return pl.pallas_call(
-        kernel,
-        out_shape=jax.ShapeDtypeStruct((rows, columns), jnp.float32),
-        in_specs=[VMEM],
-        out_specs=VMEM,
-        scratch_shapes=PlaneReduce.scratch(group, columns)
-        + [pltpu.VMEM((group, columns), jnp.bfloat16), LineReduce.scratch(rows, columns)]
-        + sems(PlaneReduce.COPIES + LineReduce.COPIES),
-        compiler_params=kernel_params(6, 60),
-        name="reduce_all",
-    )(part)
+        + PlaneReduce.scratch(tok_rows, width)
+        + [pltpu.VMEM((tok_rows, width), f32), pltpu.VMEM((w_rows, in_width), low)]
+        + PlaneReduce.scratch(group, in_width)
+        + [
+            pltpu.VMEM((group, in_width), low),
+            LineReduce.scratch(rows, in_width),
+            pltpu.VMEM((group, width), low),
+            LineReduce.scratch(rows, width),
+            pltpu.VMEM((tok_rows, width), f32),
+            pltpu.VMEM((LANES, width), f32),
+            pltpu.SemaphoreType.DMA((5,)),
+        ]
+        + sems(3 * chunks + 2 * PlaneReduce.COPIES + 2 * LineReduce.COPIES),
+        compiler_params=kernel_params(4, 63),
+        name="back_dense",
+    )(
+        sums_in, produced, full_in, normed, grad_pre, tokens, gains, grad_mid, gain_row, w_out_part, middle
+    )
 
 
 def on_plane_device(
@@ -918,11 +1302,14 @@
         scores = jnp.where(allowed[None], raw * score_scale, masked_score)
         row_top = jnp.max(scores, axis=-1, keepdims=True)
         expo = jnp.exp(scores - row_top)
-        return expo / jnp.sum(expo, axis=-1, keepdims=True)
+        row_sum = jnp.sum(expo, axis=-1, keepdims=True)
+        return expo / row_sum, (row_top + jnp.log(row_sum))[:, :, 0]
 
     mixed_parts = []
+    lse_parts = []
     for group_number in range(KVH):
-        probs = softmax_weights(group_number)
+        probs, lse_part = softmax_weights(group_number)
+        lse_parts.append(lse_part)
         values_part = all_values[:, group_number * HD : (group_number + 1) * HD]
         mixed_group = jnp.einsum(
             "jqk,kd->qjd",
@@ -932,6 +1319,14 @@
         )
         mixed_parts.append(mixed_group.reshape(tok_rows, per_group * HD))
     mixed_low = jnp.concatenate(mixed_parts, axis=1).astype(jnp.bfloat16)
+    lse = jnp.pad(jnp.concatenate(lse_parts, axis=0), ((0, 16 - HEADS), (0, 0)))
+    half_size = HD // 2
+    frequency = rope_base ** (-jnp.arange(half_size, dtype=jnp.float32) / half_size)
+    angles = within_own.astype(jnp.float32)[:, None] * frequency[None, :]
+    cosine = jnp.concatenate([jnp.cos(angles), jnp.cos(angles)], axis=1)
+    sine = jnp.concatenate([-jnp.sin(angles), jnp.sin(angles)], axis=1)
+    starts = jnp.broadcast_to((own_places - within_own)[None, :], (8, tok_rows))
+    gain_rows = jnp.pad(both_gains, ((0, 6), (0, 0)))
     middle = inputs + jnp.dot(mixed_low, full_o, preferred_element_type=jnp.float32)
     routed_low = rms_norm(middle, gain_moe_f).astype(jnp.bfloat16)
 
@@ -963,107 +1358,62 @@
     grad_w_up = jnp.einsum(
         "cd,cf->df", routed_all, grad_up_low, preferred_element_type=jnp.float32
     )
-    expert_sums = (
-        lax.psum(grad_w_gate.astype(jnp.bfloat16), "ctx").astype(jnp.float32),
-        lax.psum(grad_w_up.astype(jnp.bfloat16), "ctx").astype(jnp.float32),
-        lax.psum(grad_w_down.astype(jnp.bfloat16), "ctx").astype(jnp.float32),
-    )
+    half = grad_w_down.shape[1] // 2
+    partial_sums = jnp.concatenate(
+        [grad_w_gate, grad_w_up, grad_w_down[:, :half], grad_w_down[:, half:]], axis=0
+    ).astype(jnp.bfloat16)
     grad_sent = (
         jnp.einsum("cf,df->cd", grad_gate_low, w_gate_e, preferred_element_type=jnp.float32)
         + jnp.einsum("cf,df->cd", grad_up_low, w_up_e, preferred_element_type=jnp.float32)
     ).astype(jnp.bfloat16)
-    grad_routed = reduce_plane(grad_sent, 3)
     produced = jnp.dot(hidden_low, w_down_e, preferred_element_type=jnp.float32)
     produced = produced.astype(jnp.bfloat16).astype(jnp.float32) * gate_mine
-    moe_out = reduce_plane(produced.astype(jnp.bfloat16), 4)
-    layer_out = (middle + moe_out).astype(jnp.bfloat16)
-
-    grad_out = cotangent.astype(jnp.float32)
-    norm_value, moe_pull = jax.vjp(rms_norm, middle, gain_moe_f)
-    grad_mid_norm, grad_gain_moe = moe_pull(grad_routed)
-    grad_middle = grad_out + grad_mid_norm
-    grad_attn_low = grad_middle.astype(jnp.bfloat16)
-    grad_w_out = jnp.einsum(
-        "th,td->hd", mixed_low, grad_attn_low, preferred_element_type=jnp.float32
-    )
-    grad_mixed_low = jnp.einsum(
-        "td,hd->th", grad_attn_low, full_o, preferred_element_type=jnp.float32
-    ).astype(jnp.bfloat16)
-    grad_mixed_groups = grad_mixed_low.reshape(tok_rows, KVH, per_group, HD)
-    grad_query_parts = []
-    key_pieces = []
-    value_pieces = []
-    for group_number in range(KVH):
-        probs = softmax_weights(group_number)
-        keys_part = all_keys[:, group_number * HD : (group_number + 1) * HD]
-        values_part = all_values[:, group_number * HD : (group_number + 1) * HD]
-        grad_probs = jnp.einsum(
-            "qjd,kd->jqk",
-            grad_mixed_groups[:, group_number],
-            values_part,
-            preferred_element_type=jnp.float32,
-        )
-        grad_scores = probs * (grad_probs - jnp.sum(probs * grad_probs, axis=-1, keepdims=True))
-        grad_raw_low = (grad_scores * score_scale).astype(jnp.bfloat16)
-        grad_query_parts.append(
-            jnp.einsum("jqk,kd->qjd", grad_raw_low, keys_part, preferred_element_type=jnp.float32)
-        )
-        key_pieces.append(
-            jnp.einsum(
-                "jqk,qjd->kd",
-                grad_raw_low,
-                query_groups[:, group_number],
-                preferred_element_type=jnp.float32,
-            )
-        )
-        value_pieces.append(
-            jnp.einsum(
-                "jqk,qjd->kd",
-                probs.astype(jnp.bfloat16),
-                grad_mixed_groups[:, group_number],
-                preferred_element_type=jnp.float32,
-            )
-        )
-    grad_query_rot = jnp.stack(grad_query_parts, axis=1).reshape(tok_rows, HEADS, HD)
-    key_value_grads = reduce_line(
-        jnp.concatenate(key_pieces + value_pieces, axis=1).astype(jnp.bfloat16)
-    )
-    grad_query_low = (
-        rotate(grad_query_rot, within_own, -1.0).astype(jnp.bfloat16).reshape(tok_rows, q_columns)
-    )
-    grad_key_rot = key_value_grads[:, :kv_columns].reshape(tok_rows, KVH, HD)
-    grad_key_low = (
-        rotate(grad_key_rot, within_own, -1.0).astype(jnp.bfloat16).reshape(tok_rows, kv_columns)
-    )
-    grad_value_low = key_value_grads[:, kv_columns:].astype(jnp.bfloat16)
-    grad_pre = jnp.concatenate([grad_query_low, grad_key_low, grad_value_low], axis=1)
-    grad_w_in = jnp.einsum("td,th->dh", normed_low, grad_pre, preferred_element_type=jnp.float32)
-    grad_normed = jnp.einsum(
-        "th,dh->td",
+    produced = produced.astype(jnp.bfloat16)
+    sums_head, grad_mid, grad_pre, gain_row, w_out_part = back_attention(
+        partial_sums,
+        grad_sent,
+        full_o,
+        middle,
+        cotangent,
+        gain_rows,
+        mixed_low,
+        query.reshape(tok_rows, q_columns),
+        all_kv,
+        lse,
+        starts,
+        cosine,
+        sine,
+    )
+    sums_tail, layer_out, grad_tokens, in_sums, out_sums = back_dense(
+        partial_sums,
+        produced,
+        full_in,
+        normed_low,
         grad_pre,
-        full_in[:, : q_columns + 2 * kv_columns],
-        preferred_element_type=jnp.float32,
-    )
-    first_value, attn_pull = jax.vjp(rms_norm, inputs, gain_attn_f)
-    grad_inputs, grad_gain_attn = attn_pull(grad_normed)
-    grad_tokens = grad_middle + grad_inputs
-    grad_gains = jnp.pad(jnp.stack([grad_gain_attn, grad_gain_moe], axis=1), ((0, 0), (0, LANES - 2)))
-    dense = reduce_all(
-        jnp.concatenate([grad_w_in, grad_gains, grad_w_out], axis=1).astype(jnp.bfloat16)
-    )
+        tokens,
+        gain_rows,
+        grad_mid,
+        gain_row,
+        w_out_part,
+        middle,
+    )
+    expert_sums = jnp.concatenate([sums_head, sums_tail], axis=0).astype(jnp.float32)
+    width = D
     edge = q_columns + 2 * kv_columns
     return (
         layer_out,
         grad_tokens,
-        dense[:, edge],
-        dense[:, :q_columns],
-        dense[:, q_columns : q_columns + kv_columns],
-        dense[:, q_columns + kv_columns : edge],
-        dense[:, edge + LANES :],
-        dense[:, edge + 1],
-        expert_sums[0][None],
-        expert_sums[1][None],
-        expert_sums[2][None],
+        in_sums[:, edge],
+        in_sums[:, :q_columns],
+        in_sums[:, q_columns : q_columns + kv_columns],
+        in_sums[:, q_columns + kv_columns : edge],
+        out_sums,
+        in_sums[:, edge + 1],
+        expert_sums[None, :width],
+        expert_sums[None, width : 2 * width],
+        jnp.concatenate(
+            [expert_sums[None, 2 * width : 2 * width + half], expert_sums[None, 2 * width + half :]], axis=2
+        ),
     )
 
 

time: 747 us -> 675 us (0.904)
  matrix products: 180 us -> 99.7 us
  local copies, waits for them, and re-layouts: 23 us -> 42.3 us
  Pallas kernels: 482 us -> 465 us
  other arithmetic: 42.4 us -> 58 us
  between operations: 15 us -> 1.56 us
    dot_general x12 -> x2, matrix products: 69.5 us -> 8.22 us  [softmax_weights(): jnp.einsum('qjd,kd->jqk', query_groups[:, group_number], keys_part, prefe...]
    concatenate x2 -> x6, other arithmetic: 7.33 us -> 31.8 us  [the longest x1 25.7 us: on_plane_device(): jnp.concatenate([grad_w_gate, grad_w_up, grad_w_down[:, :half], grad_w_do...]
    pallas_call x4 -> x2, Pallas kernels: 285 us -> 268 us  [the longest x1 142 us: back_dense(): pl.pallas_call(kernel, out_shape=(jax.ShapeDtypeStruct((chunks * CHUNK, s...]
    sub x2 -> x0, matrix products: 12.6 us -> none  [softmax_weights(): expo = jnp.exp(scores - row_top)]
    pallas_call x0 -> x1, local copies, waits for them, and re-layouts: none -> 9.83 us  [gather_inputs(): pl.pallas_call(kernel, out_shape=(jax.ShapeDtypeStruct((planes * group, w...]
    broadcast_in_dim x0 -> x2, local copies, waits for them, and re-layouts: none -> 8.86 us  [the longest x1 8.25 us: on_plane_device(): expert_sums[None, width:2 * width]]
    broadcast_in_dim x3 -> x1, other arithmetic: 9.73 us -> 1.99 us  [on_plane_device(): expert_sums[None, 2 * width:2 * width + half]]
  transfers between devices with their start and end apart: 1 -> 0, of which waited for: 0 -> 0; matrix products, arithmetic and copies ran while one was open for 17% -> 0% of each run, Pallas kernels for 38% -> 0%
where the time goes in v2:
time: 675 us; the launch traced here: 666 us
  Pallas kernels  465 us (69%)
  matrix products  99.7 us (15%)
  other arithmetic  58 us (9%)
  local copies, waits for them, and re-layouts  42.3 us (6%)
    pallas_call x1, Pallas kernels, back_dense(): pl.pallas_call(kernel, out_shape=(jax.ShapeDtypeStruct((chunks * CHUNK, s...  142 us
    pallas_call x1, Pallas kernels, gather_inputs(): pl.pallas_call(kernel, out_shape=(jax.ShapeDtypeStruct((planes * group, w...  135 us
    pallas_call x1, Pallas kernels, back_attention(): pl.pallas_call(kernel, out_shape=(jax.ShapeDtypeStruct((chunks * CHUNK, s...  126 us
    pallas_call x1, Pallas kernels, gather_plane(): pl.pallas_call(kernel, out_shape=jax.ShapeDtypeStruct((8 * rows, columns)...  35.3 us
    pallas_call x1, Pallas kernels, gather_line(): pl.pallas_call(kernel, out_shape=jax.ShapeDtypeStruct((LINE * rows, colum...  26.1 us
    concatenate x1, other arithmetic, on_plane_device(): jnp.concatenate([grad_w_gate, grad_w_up, grad_w_down[:, :half], grad_w_do...  25.7 us

profile of v2, /device:TPU:0, one launch (start us, length us, event | category | flops | bytes accessed | tf_op | source)
XLA Modules:
  0.0 666.0 jit_solution(339624856549612151)
XLA Ops:
  11.3 135.3 %gather_inputs.1 = (bf16[1536,2176]{1,0:T(8,128)(2,1)}, bf16[1536,1536]{1,0:T(8,128)(2,1)}, bf16[2048,1536]{1,0:T(8,128)(2,1)}, f32[64,256]{1,0:T(8,128)}) custom-call(bf16[48,2176]{1,0:T(8,128)(2,1)} %fusion.45.in_ref, bf16[48,1536]{1,0:T(8,128)(2,1)} %out_ref.1, bf16[256,1536]{1,0:T(8,128)(2,1)} %cot_ref.3, f32[8,256]{1,0:T(8,128)} %select_reduce_fusion.gate_ref), custom_call_target="tpu_custom_call" | custom-call | tf_op jit(solution)/shard_map/gather_inputs/pallas_call | solution.py:701
  147.4 9.6 %fusion.12 = f32[2048,768]{1,0:T(8,128)} fusion(bf16[2048,1536]{1,0:T(8,128)(2,1)} %get-tuple-element.27, f32[2048]{0:T(1024)S(1)} %bitcast.118, bf16[1,768,1536]{2,1,0:T(8,128)(2,1)} %param.23), kind=kOutput, calls=%fused_computation.35 | convolution fusion | flops 4841275392 | bytes 14950400 | tf_op jit(solution)/shard_map/cd,fd->cf/dot_general | solution.py:1343
  157.0 9.8 %copy.72 = bf16[1536,2176]{0,1:T(8,128)(2,1)} copy(bf16[1536,2176]{1,0:T(8,128)(2,1)} %get-tuple-element.25.full_ref) | data formatting | bytes 13369344 | tf_op jit(solution)/shard_map/gather_inputs/pallas_call | solution.py:701
  169.1 5.0 fusion.4
  182.5 26.1 %gather_line.1.kv_ref = bf16[1024,512]{1,0:T(8,128)(2,1)} custom-call(bf16[256,512]{1,0:T(8,128)(2,1)} %pad_maximum_fusion.5.block_ref), custom_call_target="tpu_custom_call" | custom-call | tf_op jit(solution)/shard_map/gather_line/pallas_call | solution.py:734
  217.0 5.5 fusion.6
  224.6 4.1 fusion.7
  228.7 4.7 fusion.25
  235.1 3.8 multiply_reduce_fusion
  241.1 35.3 %gather_plane.1 = bf16[2048,1536]{1,0:T(8,128)(2,1)} custom-call(bf16[256,1536]{1,0:T(8,128)(2,1)} %multiply_convert_fusion.6.block_ref), custom_call_target="tpu_custom_call" | custom-call | tf_op jit(solution)/shard_map/gather_plane/pallas_call | solution.py:764
  276.5 9.8 %fusion.18 = f32[2048,768]{1,0:T(8,128)} fusion(bf16[2048,1536]{1,0:T(8,128)(2,1)} %gather_plane.1, bf16[1,1536,768]{2,1,0:T(8,128)(2,1)S(1)} %copy-done.18), kind=kOutput, calls=%fused_computation.45 | convolution fusion | flops 4831838208 | bytes 14942208 | tf_op jit(solution)/shard_map/dot_general | solution.py:1340
  286.3 12.4 %fusion.2 = (bf16[2048,768]{1,0:T(8,128)(2,1)}, bf16[2048,768]{1,0:T(8,128)(2,1)}, bf16[2048,768]{1,0:T(8,128)(2,1)}) fusion(f32[2048,768]{1,0:T(8,128)} %fusion.12, f32[2048,768]{1,0:T(8,128)} %fusion.18, bf16[2048,1536]{1,0:T(8,128)(2,1)S(1)} %copy-done.4, bf16[1,1536,768]{2,1,0:T(8,128)(2,1)S(1)} %copy-done.17), kind=kOutput, calls=%fused_computation.9 | convolution fusion | flops 4857004032 | bytes 30670848 | tf_op jit(solution)/shard_map/dot_general | solution.py:1339
  298.7 8.2 %convolution_convert_fusion.1 = bf16[768,1536]{1,0:T(8,128)(2,1)S(1)} fusion(bf16[2048,768]{1,0:T(8,128)(2,1)} %get-tuple-element.50, bf16[2048,1536]{1,0:T(8,128)(2,1)S(1)} %bitcast.126, f32[2048]{0:T(1024)S(1)} %bitcast.119), kind=kOutput, calls=%fused_computation.29 | convolution fusion | flops 4842455040 | bytes 11804672 | tf_op jit(solution)/shard_map/cf,cd->fd/dot_general | solution.py:1346
  307.1 5.5 convolution_convert_fusion.3
  312.6 5.4 convolution_convert_fusion.2
  318.1 25.7 %pad_maximum_fusion.sums_ref = bf16[4608,768]{1,0:T(8,128)(2,1)} fusion(bf16[768,768]{1,0:T(8,128)(2,1)S(1)} %get-tuple-element.55, bf16[768,768]{1,0:T(8,128)(2,1)S(1)} %get-tuple-element.54, bf16[1536,768]{1,0:T(8,128)(2,1)S(1)} %convolution_convert_fusion.2, bf16[1536,768]{1,0:T(8,128)(2,1)S(1)} %convolution_convert_fusion.3), kind=kLoop, calls=%fused_computation.5 | loop fusion | flops 28311552 | bytes 14155776 | tf_op jit(solution)/shard_map/concatenate | solution.py:1362
  343.8 6.8 %multiply_convert_fusion.prod_ref = bf16[2048,1536]{1,0:T(8,128)(2,1)} fusion(bf16[2048,768]{1,0:T(8,128)(2,1)S(1)} %copy-done.21, f32[2048]{0:T(1024)S(1)} %bitcast.120, bf16[1,768,1536]{2,1,0:T(8,128)(2,1)S(1)} %copy-done.16), kind=kOutput, calls=%fused_computation.1 | convolution fusion | flops 4844421120 | bytes 11804672 | tf_op jit(solution)/shard_map/dot_general | solution.py:1369
  350.6 8.3 %fusion.13 = f32[2048,1536]{1,0:T(8,128)} fusion(bf16[2048,768]{1,0:T(8,128)(2,1)S(1)} %copy-done.20, bf16[1,1536,768]{2,1,0:T(8,128)(2,1)S(1)} %copy-done.17), kind=kOutput, calls=%fused_computation.40 | convolution fusion | flops 4831838208 | bytes 18087936 | tf_op jit(solution)/shard_map/cf,df->cd/dot_general | solution.py:1366
  358.9 10.0 %add_convert_fusion.sent_ref = bf16[2048,1536]{1,0:T(8,128)(2,1)} fusion(f32[2048,1536]{1,0:T(8,128)} %fusion.13, bf16[2048,768]{1,0:T(8,128)(2,1)S(1)} %copy-done.19, bf16[1,1536,768]{2,1,0:T(8,128)(2,1)S(1)} %copy-done.18), kind=kOutput, calls=%fused_computation | convolution fusion | flops 4838129664 | bytes 24379392 | tf_op jit(solution)/shard_map/cf,df->cd/dot_general | solution.py:1367
  369.0 125.9 %back_attention.1 = (bf16[2112,768]{1,0:T(8,128)(2,1)}, f32[256,1536]{1,0:T(8,128)}, bf16[256,2048]{1,0:T(8,128)(2,1)}, f32[8,1536]{1,0:T(8,128)}, bf16[192,1536]{1,0:T(8,128)(2,1)}) custom-call(bf16[4608,768]{1,0:T(8,128)(2,1)} %pad_maximum_fusion.sums_ref, bf16[2048,1536]{1,0:T(8,128)(2,1)} %add_convert_fusion.sent_ref, ...), custom_call_target="tpu_custom_call" | custom-call | tf_op jit(solution)/shard_map/back_attention/pallas_call | solution.py:1037
  494.9 142.1 %back_dense.1 = (bf16[2496,768]{1,0:T(8,128)(2,1)}, bf16[256,1536]{1,0:T(8,128)(2,1)}, f32[256,1536]{1,0:T(8,128)}, f32[48,2176]{1,0:T(8,128)}, f32[48,1536]{1,0:T(8,128)}) custom-call(bf16[4608,768]{1,0:T(8,128)(2,1)} %pad_maximum_fusion.sums_ref, bf16[2048,1536]{1,0:T(8,128)(2,1)} %multiply_convert_fusion.prod_ref, ...), custom_call_target="tpu_custom_call" | custom-call | tf_op jit(solution)/shard_map/back_dense/pallas_call | solution.py:1198
  643.6 3.1 pad_maximum_fusion.1
  648.4 6.2 maximum_convert_fusion
  654.6 8.3 %slice_bitcast_fusion = (f32[1,1536,768]{2,1,0:T(8,128)}, f32[1,1536,768]{2,1,0:T(8,128)}) fusion(f32[4608,768]{1,0:T(8,128)} %maximum_convert_fusion), kind=kLoop, calls=%fused_computation.26 | loop fusion | bytes 18874368 | tf_op jit(solution)/shard_map/broadcast_in_dim | solution.py:1413
  (105 shorter events, 47.7 us)
Async XLA Ops:
  147.4 9.6 %copy-start.14 = (f32[8,1,256]{2,1,0:T(1,128)}, f32[8,1,256]{2,1,0:T(1,128)S(1)}, u32[]{:S(2)}) copy-start(f32[8,1,256]{2,1,0:T(1,128)S(1)} %constant_dynamic-slice_fusion) | copy-start | bytes 24580
  157.0 11.8 %copy-start.3 = (bf16[256,1536]{1,0:T(8,128)(2,1)S(1)}, bf16[256,1536]{1,0:T(8,128)(2,1)}, u32[]{:S(2)}) copy-start(bf16[256,1536]{1,0:T(8,128)(2,1)} %tok_ref.1) | copy-start | bytes 2359300
  169.1 6.4 copy-start.6
  209.5 7.4 %copy-start.5 = (bf16[1024,512]{1,0:T(8,128)(2,1)S(1)}, bf16[1024,512]{1,0:T(8,128)(2,1)}, u32[]{:S(2)}) copy-start(bf16[1024,512]{1,0:T(8,128)(2,1)} %gather_line.1.kv_ref) | copy-start | bytes 3145732
  214.2 2.7 copy-start.7
  214.2 2.7 copy-start.8
  216.9 5.6 copy-start.9
  235.1 5.0 copy-start.13
  238.9 1.1 copy-start.1
  238.9 37.5 %copy-start.18 = (bf16[1,1536,768]{2,1,0:T(8,128)(2,1)S(1)}, bf16[1,1536,768]{2,1,0:T(8,128)(2,1)}, u32[]{:S(2)}) copy-start(bf16[1,1536,768]{2,1,0:T(8,128)(2,1)} %param.22) | copy-start | bytes 7077892
  276.4 9.8 %copy-start.4 = (bf16[2048,1536]{1,0:T(8,128)(2,1)S(1)}, bf16[2048,1536]{1,0:T(8,128)(2,1)}, u32[]{:S(2)}) copy-start(bf16[2048,1536]{1,0:T(8,128)(2,1)} %gather_plane.1) | copy-start | bytes 18874372
  276.5 9.8 %copy-start.17 = (bf16[1,1536,768]{2,1,0:T(8,128)(2,1)S(1)}, bf16[1,1536,768]{2,1,0:T(8,128)(2,1)}, u32[]{:S(2)}) copy-start(bf16[1,1536,768]{2,1,0:T(8,128)(2,1)} %param.21) | copy-start | bytes 7077892
  276.5 22.2 %slice-start = ((s8[6291456]{0:T(1024)(128)(4,1)}), s8[4194304]{0:T(1024)(128)(4,1)S(1)}, s32[]{:S(2)}) async-start(s8[6291456]{0:T(1024)(128)(4,1)} %bitcast.125), calls=%async_computation | async-start | bytes 8388608
  286.2 12.4 %copy-start.15 = (f32[8,1,256]{2,1,0:T(1,128)S(1)}, f32[8,1,256]{2,1,0:T(1,128)}, u32[]{:S(2)}) copy-start(f32[8,1,256]{2,1,0:T(1,128)} %copy-done.14) | copy-start | bytes 24580
  286.2 12.4 %slice-start.1 = ((s8[6291456]{0:T(1024)(128)(4,1)}), s8[2097152]{0:T(1024)(128)(4,1)S(1)}, s32[]{:S(2)}) async-start(s8[6291456]{0:T(1024)(128)(4,1)} %bitcast.125), calls=%async_computation.1 | async-start | bytes 4194304
  298.7 8.4 %copy-start.20 = (bf16[2048,768]{1,0:T(8,128)(2,1)S(1)}, bf16[2048,768]{1,0:T(8,128)(2,1)}, u32[]{:S(2)}) copy-start(bf16[2048,768]{1,0:T(8,128)(2,1)} %get-tuple-element.49) | copy-start | bytes 9437188
  307.1 5.6 copy-start.19
  318.1 25.7 %copy-start.16 = (bf16[1,768,1536]{2,1,0:T(8,128)(2,1)S(1)}, bf16[1,768,1536]{2,1,0:T(8,128)(2,1)}, u32[]{:S(2)}) copy-start(bf16[1,768,1536]{2,1,0:T(8,128)(2,1)} %param.23) | copy-start | bytes 7077892
  318.1 25.7 %copy-start.21 = (bf16[2048,768]{1,0:T(8,128)(2,1)S(1)}, bf16[2048,768]{1,0:T(8,128)(2,1)}, u32[]{:S(2)}) copy-start(bf16[2048,768]{1,0:T(8,128)(2,1)} %get-tuple-element.50) | copy-start | bytes 9437188
  643.6 3.1 copy-start
  643.6 4.8 copy-start.2
  654.6 8.3 %copy-start.11 = (bf16[256,1536]{1,0:T(8,128)(2,1)S(1)}, bf16[256,1536]{1,0:T(8,128)(2,1)}, u32[]{:S(2)}) copy-start(bf16[256,1536]{1,0:T(8,128)(2,1)} %get-tuple-element.84) | copy-start | bytes 2359300
  654.6 9.1 %copy-start.10 = (f32[256,1536]{1,0:T(8,128)S(1)}, f32[256,1536]{1,0:T(8,128)}, u32[]{:S(2)}) copy-start(f32[256,1536]{1,0:T(8,128)} %get-tuple-element.85) | copy-start | bytes 4718596
  654.6 10.3 %copy-start.12 = (f32[48,1536]{1,0:T(8,128)S(1)}, f32[48,1536]{1,0:T(8,128)}, u32[]{:S(2)}) copy-start(f32[48,1536]{1,0:T(8,128)} %get-tuple-element.90) | copy-start | bytes 884740

commit v3 on v2

--- a/solution.py
+++ b/solution.py
@@ -597,15 +597,18 @@
                     self.part, block * rows, self.part, block * rows, self.landing, place, rows
                 )
 
-    def finish(self, out):
+    def finish(self, outs):
         z, rows = self.wires.z, self.rows
 
         @pl.loop(0, rows // 16)
         def _(step):
             row = pl.multiple_of(z * rows + step * 16, 16)
-            out[pl.ds(pl.multiple_of(step * 16, 16), 16), :] = self.part[pl.ds(row, 16), :].astype(
-                out.dtype
-            )
+            begin = 0
+            for out in outs:
+                out[pl.ds(pl.multiple_of(step * 16, 16), 16), :] = self.part[
+                    pl.ds(row, 16), begin : begin + out.shape[1]
+                ].astype(out.dtype)
+                begin += out.shape[1]
 
         for hop in range(LINE - 1):
             for way, block, source in self._moves(hop):
@@ -629,23 +632,47 @@
     )
 
 
-def gather_inputs(w_in, w_out, cotangent, gates):
-    rows, tokens = w_in.shape[0], cotangent.shape[0]
+def dot(left, right, left_dim, right_dim):
+    return lax.dot_general(
+        left, right, (((left_dim,), (right_dim,)), ((), ())), preferred_element_type=jnp.float32
+    )
+
+
+def rows_at(begin, size):
+    return pl.ds(pl.multiple_of(begin, 16), size)
+
+
+def front(w_query, w_key, w_value, gains, w_out, cotangent, gates, tokens, starts, cosine, sine):
+    rows, width = w_query.shape
+    kv_width = w_key.shape[1] + w_value.shape[1]
+    key_width = w_key.shape[1]
+    tok_rows = tokens.shape[0]
+    keys = LINE * tok_rows
     planes = 8
     group = LINE * rows
-
-    def kernel(in_ref, out_ref, cot_ref, gate_ref, all_in, all_out, all_cot, all_gate, here, send, recv):
+    w_rows = planes * group
+    score_scale = HD ** (-0.5)
+    per_group = HEADS // KVH
+
+    def kernel(
+        wq_ref, wk_ref, wv_ref, gains_ref, wo_ref, cot_ref, gate_ref, tok_ref, starts_ref, cos_ref, sin_ref,
+        out_q, out_kv, out_o, out_cot, all_gate, query_ref, all_kv, lse_ref, mixed_ref, middle_ref, normed_ref,
+        routed_ref, gain_rows_ref,
+        full_q, full_kv, full_o, all_cot, bias, value_t, here, there, send, recv,
+    ):
         wires = Wires(send, recv)
         dp, z = wires.dp, wires.z
-        own = pl.ds(pl.multiple_of((dp * LINE + z) * rows, 16), rows)
+        own = rows_at((dp * LINE + z) * rows, rows)
         locals_ = [
-            pltpu.make_async_copy(in_ref, all_in.at[own], here.at[0]),
-            pltpu.make_async_copy(out_ref, all_out.at[own], here.at[1]),
-            pltpu.make_async_copy(
-                cot_ref, all_cot.at[pl.ds(pl.multiple_of(dp * tokens, 16), tokens)], here.at[2]
-            ),
-            pltpu.make_async_copy(gate_ref, all_gate.at[pl.ds(pl.multiple_of(dp * 8, 8), 8)], here.at[3]),
+            (wk_ref, full_kv.at[own, pl.ds(0, key_width)]),
+            (wv_ref, full_kv.at[own, pl.ds(key_width, kv_width - key_width)]),
+            (gains_ref, full_kv.at[own, pl.ds(kv_width, LANES)]),
+            (wq_ref, full_q.at[own]),
+            (wo_ref, full_o.at[own]),
+            (cot_ref, all_cot.at[rows_at(dp * tok_rows, tok_rows)]),
+            (gate_ref, all_gate.at[pl.ds(pl.multiple_of(dp * 8, 8), 8)]),
         ]
+        locals_ = [pltpu.make_async_copy(a, b, here.at[i]) for i, (a, b) in enumerate(locals_)]
         for one in locals_:
             one.start()
         greet(wires, range(1, planes), True)
@@ -653,123 +680,304 @@
             one.wait()
 
         def block_rows(block):
-            return pl.ds(pl.multiple_of((dp * LINE + block) * rows, 16), rows)
-
-        lines = [LineGather(wires, all_in, block_rows), LineGather(wires, all_out, block_rows)]
-        spreads = [
-            PlaneGather(wires, all_in, group),
-            PlaneGather(wires, all_out, group),
-            PlaneGather(wires, all_cot, tokens),
-        ]
+            return rows_at((dp * LINE + block) * rows, rows)
+
+        line_kv, line_q, line_o = [LineGather(wires, r, block_rows) for r in (full_kv, full_q, full_o)]
+        plane_kv, plane_q, plane_o = [PlaneGather(wires, r, group) for r in (full_kv, full_q, full_o)]
+        plane_cot = PlaneGather(wires, all_cot, tok_rows)
+        line_keys = LineGather(wires, all_kv, lambda block: rows_at(block * tok_rows, tok_rows))
         first = wires.take(planes - 1)
 
         def gate_copy(mask, owner):
             part = all_gate.at[pl.ds(pl.multiple_of(owner * 8, 8), 8)]
             return wires.copy(part, part, first + mask - 1, dp=masked(dp, mask))
 
-        for mask in range(1, planes):
-            gate_copy(mask, dp).start()
         for step in range(LINE - 1):
-            lines[0].start(step)
-            lines[0].wait(step)
-        spreads[0].start(0)
-        for step in range(LINE - 1):
-            lines[1].start(step)
-            lines[1].wait(step)
-        spreads[0].wait(0)
-        spreads[0].start(1)
-        spreads[1].start(0)
-        spreads[2].start(0)
-        spreads[0].wait(1)
-        spreads[0].start(2)
-        spreads[1].wait(0)
-        spreads[1].start(1)
-        spreads[2].wait(0)
-        spreads[2].start(1)
-        spreads[1].wait(1)
-        spreads[1].start(2)
-        spreads[2].wait(1)
-        spreads[2].start(2)
-        for one in lines + spreads:
-            one.finish()
+            line_kv.start(step)
+            line_q.start(step)
+            if step == 0:
+                for mask in range(1, planes):
+                    gate_copy(mask, dp).start()
+                key_place = lax.broadcasted_iota(jnp.int32, (keys, tok_rows), 0)
+                query_place = lax.broadcasted_iota(jnp.int32, (keys, tok_rows), 1) + z * tok_rows
+                allowed = (key_place >= starts_ref[0:1, :]) & (key_place <= query_place)
+                bias[...] = jnp.where(allowed, 0.0, masked_score)
+            line_kv.wait(step)
+            if step == LINE - 2:
+                plane_kv.start(0)
+            line_q.wait(step)
+        plane_q.start(0)
+        plane_kv.wait(0)
+        plane_kv.start(1)
+        line_o.start(0)
+        plane_kv.wait(1)
+        plane_kv.start(2)
+        plane_q.wait(0)
+        plane_q.start(1)
+        line_o.wait(0)
+        line_o.start(1)
+        plane_kv.finish()
+
+        gain_rows_ref[...] = full_kv[:, kv_width:].astype(jnp.float32).T[:8, :]
+        tile = 32
+
+        @pl.loop(0, tok_rows // tile)
+        def _(step):
+            cut = pl.ds(pl.multiple_of(step * tile, tile), tile)
+            normed_ref[cut, :] = rms_norm(
+                tok_ref[cut, :].astype(jnp.float32), gain_rows_ref[0:1, :]
+            ).astype(jnp.bfloat16)
+
+        own_keys = rows_at(z * tok_rows, tok_rows)
+        pre = dot(normed_ref[...], full_kv[:, :kv_width], 1, 0)
+        for pair in range(KVH):
+            cut = slice(pair * HD, (pair + 1) * HD)
+            all_kv[own_keys, cut] = turned(pre[:, cut], cos_ref[...], sin_ref[...]).astype(jnp.bfloat16)
+        all_kv[own_keys, key_width:] = pre[:, key_width:].astype(jnp.bfloat16)
+        line_keys.start(0)
+        line_o.wait(1)
+        line_o.start(2)
+        line_keys.wait(0)
+        line_keys.start(1)
+        line_o.wait(2)
+        plane_o.start(0)
+        plane_cot.start(0)
+        plane_q.wait(1)
+        plane_q.start(2)
+        plane_o.wait(0)
+        plane_o.start(1)
+        plane_cot.wait(0)
+        plane_cot.start(1)
+        plane_q.finish()
+        saves = [pltpu.make_async_copy(full_q, out_q, there.at[0])]
+        saves.append(pltpu.make_async_copy(full_kv, out_kv, there.at[1]))
+        saves[0].start()
+        saves[1].start()
+
+        @pl.loop(0, HEADS // 2)
+        def _(step):
+            wide = pl.ds(pl.multiple_of(step * 2 * HD, 2 * HD), 2 * HD)
+            pre_q = dot(normed_ref[...], full_q[:, wide], 1, 0)
+            for one in range(2):
+                query_ref[:, pl.ds(pl.multiple_of((2 * step + one) * HD, HD), HD)] = turned(
+                    pre_q[:, one * HD : (one + 1) * HD], cos_ref[...], sin_ref[...]
+                ).astype(jnp.bfloat16)
+
+        line_keys.wait(1)
+        line_keys.start(2)
+        line_keys.wait(2)
+        value_t[...] = all_kv[:, key_width:].astype(jnp.float32).T.astype(jnp.bfloat16)
+        lse_ref[...] = jnp.zeros_like(lse_ref)
+
+        @pl.loop(0, HEADS)
+        def _(head):
+            own_cut = pl.ds(pl.multiple_of(head * HD, HD), HD)
+            key_cut = pl.ds(pl.multiple_of((head // per_group) * HD, HD), HD)
+            scores = dot(all_kv[:, key_cut], query_ref[:, own_cut], 1, 1) * score_scale + bias[...]
+            top = jnp.max(scores, axis=0, keepdims=True)
+            expo = jnp.exp(scores - top)
+            total = jnp.sum(expo, axis=0, keepdims=True)
+            lse_ref[pl.ds(head, 1), :] = top + jnp.log(total)
+            probs = (expo * (1.0 / total)).astype(jnp.bfloat16)
+            mixed_ref[:, own_cut] = dot(value_t[key_cut, :], probs, 1, 0).T.astype(jnp.bfloat16)
+
+        plane_o.wait(1)
+        plane_o.start(2)
+        plane_o.finish()
+        saves.append(pltpu.make_async_copy(full_o, out_o, there.at[2]))
+        saves[2].start()
+
+        @pl.loop(0, width // 512)
+        def _(step):
+            cut = pl.ds(pl.multiple_of(step * 512, 512), 512)
+            middle_ref[:, cut] = tok_ref[:, cut].astype(jnp.float32) + dot(
+                mixed_ref[...], full_o[:, cut], 1, 0
+            )
+
+        @pl.loop(0, tok_rows // tile)
+        def _(step):
+            cut = pl.ds(pl.multiple_of(step * tile, tile), tile)
+            routed_ref[cut, :] = rms_norm(middle_ref[cut, :], gain_rows_ref[1:2, :]).astype(jnp.bfloat16)
+
+        plane_cot.wait(1)
+        plane_cot.start(2)
+        plane_cot.finish()
+        saves.append(pltpu.make_async_copy(all_cot, out_cot, there.at[3]))
+        saves[3].start()
         for mask in range(1, planes):
             gate_copy(mask, masked(dp, mask)).wait_recv()
         for mask in range(1, planes):
             gate_copy(mask, dp).wait_send()
-
-    copies = 2 * LineGather.COPIES + 3 * PlaneGather.COPIES + planes - 1
+        for one in (line_kv, line_q, line_o, line_keys):
+            one.finish()
+        for one in saves:
+            one.wait()
+
+    f32, low = jnp.float32, jnp.bfloat16
+    copies = 4 * LineGather.COPIES + 4 * PlaneGather.COPIES + planes - 1
     return pl.pallas_call(
         kernel,
         out_shape=(
-            jax.ShapeDtypeStruct((planes * group, w_in.shape[1]), jnp.bfloat16),
-            jax.ShapeDtypeStruct((planes * group, w_out.shape[1]), jnp.bfloat16),
-            jax.ShapeDtypeStruct((planes * tokens, cotangent.shape[1]), jnp.bfloat16),
-            jax.ShapeDtypeStruct((planes * 8, tokens), jnp.float32),
+            jax.ShapeDtypeStruct((w_rows, width), low),
+            jax.ShapeDtypeStruct((w_rows, kv_width + LANES), low),
+            jax.ShapeDtypeStruct((w_rows, width), low),
+            jax.ShapeDtypeStruct((planes * tok_rows, width), low),
+            jax.ShapeDtypeStruct((planes * 8, tok_rows), f32),
+            jax.ShapeDtypeStruct((tok_rows, width), low),
+            jax.ShapeDtypeStruct((keys, kv_width), low),
+            jax.ShapeDtypeStruct((16, tok_rows), f32),
+            jax.ShapeDtypeStruct((tok_rows, width), low),
+            jax.ShapeDtypeStruct((tok_rows, width), f32),
+            jax.ShapeDtypeStruct((tok_rows, width), low),
+            jax.ShapeDtypeStruct((tok_rows, width), low),
+            jax.ShapeDtypeStruct((8, width), f32),
         ),
-        in_specs=[ANY] * 4,
-        out_specs=(ANY,) * 4,
-        scratch_shapes=[pltpu.SemaphoreType.DMA((4,))] + sems(copies),
-        compiler_params=kernel_params(0, 60),
-        name="gather_inputs",
-    )(w_in, w_out, cotangent, gates)
-
-
-def gather_line(block):
-    rows, columns = block.shape
-
-    def kernel(block_ref, all_ref, here, send, recv):
+        in_specs=[VMEM] * 11,
+        out_specs=(ANY,) * 4 + (VMEM,) * 9,
+        scratch_shapes=[
+            pltpu.VMEM((w_rows, width), low),
+            pltpu.VMEM((w_rows, kv_width + LANES), low),
+            pltpu.VMEM((w_rows, width), low),
+            pltpu.VMEM((planes * tok_rows, width), low),
+            pltpu.VMEM((keys, tok_rows), f32),
+            pltpu.VMEM((kv_width - key_width, keys), low),
+            pltpu.SemaphoreType.DMA((7,)),
+            pltpu.SemaphoreType.DMA((4,)),
+        ]
+        + sems(copies),
+        compiler_params=kernel_params(0, 63),
+        name="front",
+    )(w_query, w_key, w_value, gains, w_out, cotangent, gates, tokens, starts, cosine, sine)
+
+
+def experts(routed, all_cot, all_gate, w_gate, w_up, w_down):
+    tok_rows, width = routed.shape
+    hidden_width = w_gate.shape[1]
+    total_rows = 8 * tok_rows
+
+    def kernel(
+        routed_ref, cot_ref, gate_ref, wg_ref, wu_ref, wd_ref,
+        sums_ref, sent_ref, prod_ref,
+        w_in, w_down, x_all, y_all, hidden, grad_hidden, grad_in, sums, gate_t, stage, here, there, send, recv,
+    ):
         wires = Wires(send, recv)
-        own = pltpu.make_async_copy(
-            block_ref, all_ref.at[pl.ds(pl.multiple_of(wires.z * rows, 16), rows)], here.at[0]
-        )
+        dp = wires.dp
+        own = pltpu.make_async_copy(routed_ref, x_all.at[rows_at(dp * tok_rows, tok_rows)], here.at[0])
+        loads = [
+            pltpu.make_async_copy(cot_ref, y_all, here.at[1]),
+            pltpu.make_async_copy(wd_ref, w_down, here.at[2]),
+            pltpu.make_async_copy(wg_ref, w_in.at[:, pl.ds(0, hidden_width)], here.at[3]),
+            pltpu.make_async_copy(wu_ref, w_in.at[:, pl.ds(hidden_width, hidden_width)], here.at[4]),
+        ]
         own.start()
-        greet(wires, (), True)
-        own.wait()
-        line = LineGather(wires, all_ref, lambda b: pl.ds(pl.multiple_of(b * rows, 16), rows))
-        for step in range(LINE - 1):
-            line.start(step)
-            line.wait(step)
-        line.finish()
-
-    return pl.pallas_call(
-        kernel,
-        out_shape=jax.ShapeDtypeStruct((LINE * rows, columns), block.dtype),
-        in_specs=[VMEM],
-        out_specs=VMEM,
-        scratch_shapes=[pltpu.SemaphoreType.DMA((1,))] + sems(LineGather.COPIES),
-        compiler_params=kernel_params(1, 60),
-        name="gather_line",
-    )(block)
-
-
-def gather_plane(block):
-    rows, columns = block.shape
-
-    def kernel(block_ref, all_ref, here, send, recv):
-        wires = Wires(send, recv)
-        own = pltpu.make_async_copy(
-            block_ref, all_ref.at[pl.ds(pl.multiple_of(wires.dp * rows, 16), rows)], here.at[0]
-        )
-        own.start()
+        for one in loads:
+            one.start()
         greet(wires, (1, 2, 4), False)
         own.wait()
-        spread = PlaneGather(wires, all_ref, rows)
+        spread = PlaneGather(wires, x_all, tok_rows)
         spread.start(0)
+        gate_t[...] = gate_ref[...].T
+        for one in loads:
+            one.wait()
+
+        def gate_of(block):
+            lane = lax.broadcasted_iota(jnp.int32, gate_t.shape, 1)
+            return jnp.sum(jnp.where(lane == block * 8 + dp, gate_t[...], 0.0), axis=1, keepdims=True)
+
+        def back_hidden(block):
+            cut = rows_at(block * tok_rows, tok_rows)
+            y_all[cut, :] = (y_all[cut, :].astype(jnp.float32) * gate_of(block)).astype(jnp.bfloat16)
+            grad_hidden[cut, :] = dot(y_all[cut, :], w_down[...], 1, 1)
+
+        def through(block):
+            cut = rows_at(block * tok_rows, tok_rows)
+            acts = dot(x_all[cut, :], w_in[...], 1, 0)
+            gate_act, up_act = acts[:, :hidden_width], acts[:, hidden_width:]
+            share = jax.nn.sigmoid(gate_act)
+            silu = gate_act * share
+            hidden[cut, :] = (silu * up_act).astype(jnp.bfloat16)
+            grad = grad_hidden[cut, :]
+            grad_in[cut, :hidden_width] = (
+                grad * up_act * share * (1.0 + gate_act * (1.0 - share))
+            ).astype(jnp.bfloat16)
+            grad_in[cut, hidden_width:] = (grad * silu).astype(jnp.bfloat16)
+
+        pl.loop(0, 4)(back_hidden)
         spread.wait(0)
         spread.start(1)
+        pl.loop(4, 8)(back_hidden)
+        through(dp)
         spread.wait(1)
         spread.start(2)
         spread.finish()
-
+        for mask in range(1, 8):
+            through(masked(dp, mask))
+
+        @pl.loop(0, width // 256)
+        def _(step):
+            cut = rows_at(step * 256, 256)
+            sums[cut, :] = dot(x_all[:, cut], grad_in[...], 0, 0).astype(jnp.bfloat16)
+
+        @pl.loop(0, hidden_width // 256)
+        def _(step):
+            cut = rows_at(step * 256, 256)
+            out = rows_at(width + step * 256, 256)
+            sums[out, :] = dot(hidden[:, cut], y_all[...], 0, 0).astype(jnp.bfloat16)
+
+        save = pltpu.make_async_copy(sums, sums_ref, there.at[0])
+        save.start()
+
+        def stage_copy(slot, ref, block):
+            return pltpu.make_async_copy(
+                stage.at[slot], ref.at[rows_at(block * tok_rows, tok_rows)], there.at[1 + slot]
+            )
+
+        for block in range(8):
+            slot = block % 2
+            cut = rows_at(block * tok_rows, tok_rows)
+            if block >= 2:
+                stage_copy(slot, sent_ref, block - 2).wait()
+            stage[slot] = dot(grad_in[cut, :], w_in[...], 1, 1).astype(jnp.bfloat16)
+            stage_copy(slot, sent_ref, block).start()
+        for block in range(8):
+            slot = block % 2
+            cut = rows_at(block * tok_rows, tok_rows)
+            stage_copy(slot, sent_ref if block < 2 else prod_ref, (block - 2) % 8).wait()
+            made = dot(hidden[cut, :], w_down[...], 1, 0).astype(jnp.bfloat16).astype(jnp.float32)
+            stage[slot] = (made * gate_of(block)).astype(jnp.bfloat16)
+            stage_copy(slot, prod_ref, block).start()
+        stage_copy(0, prod_ref, 6).wait()
+        stage_copy(1, prod_ref, 7).wait()
+        save.wait()
+
+    f32, low = jnp.float32, jnp.bfloat16
     return pl.pallas_call(
         kernel,
-        out_shape=jax.ShapeDtypeStruct((8 * rows, columns), block.dtype),
-        in_specs=[VMEM],
-        out_specs=VMEM,
-        scratch_shapes=[pltpu.SemaphoreType.DMA((1,))] + sems(PlaneGather.COPIES),
-        compiler_params=kernel_params(2, 60),
-        name="gather_plane",
-    )(block)
+        out_shape=(
+            jax.ShapeDtypeStruct((width + hidden_width, width), low),
+            jax.ShapeDtypeStruct((total_rows, width), low),
+            jax.ShapeDtypeStruct((total_rows, width), low),
+        ),
+        in_specs=[VMEM, ANY, VMEM, ANY, ANY, ANY],
+        out_specs=(ANY,) * 3,
+        scratch_shapes=[
+            pltpu.VMEM((width, 2 * hidden_width), low),
+            pltpu.VMEM((hidden_width, width), low),
+            pltpu.VMEM((total_rows, width), low),
+            pltpu.VMEM((total_rows, width), low),
+            pltpu.VMEM((total_rows, hidden_width), low),
+            pltpu.VMEM((total_rows, hidden_width), f32),
+            pltpu.VMEM((total_rows, 2 * hidden_width), low),
+            pltpu.VMEM((width + hidden_width, width), low),
+            pltpu.VMEM((tok_rows, 64), f32),
+            pltpu.VMEM((2, tok_rows, width), low),
+            pltpu.SemaphoreType.DMA((5,)),
+            pltpu.SemaphoreType.DMA((3,)),
+        ]
+        + sems(PlaneGather.COPIES),
+        compiler_params=kernel_params(1, 63),
+        name="experts",
+    )(routed, all_cot, all_gate, w_gate, w_up, w_down)
 
 
 class LineSum:
@@ -855,12 +1063,6 @@
                 self._back(chunk).wait_send()
 
 
-def dot(left, right, left_dim, right_dim):
-    return lax.dot_general(
-        left, right, (((left_dim,), (right_dim,)), ((), ())), preferred_element_type=jnp.float32
-    )
-
-
 def norm_back(values, gain, grad):
     scale = lax.rsqrt(jnp.mean(values * values, axis=-1, keepdims=True) + epsilon)
     normal = values * scale
@@ -873,7 +1075,7 @@
     return values * cosine + pltpu.roll(values, HD // 2, 1) * sine
 
 
-CHUNK = 192
+CHUNK = 96
 SPLIT = 11
 
 
@@ -1023,7 +1225,7 @@
         line.start(2)
         summed.tick()
         line.add(2)
-        line.finish(kv_out)
+        line.finish((kv_out,))
         q_width = HEADS * HD
         for pair in range(KVH):
             cut = slice(pair * HD, (pair + 1) * HD)
@@ -1075,18 +1277,19 @@
     )
 
 
-def back_dense(sums_in, produced, full_in, normed, grad_pre, tokens, gains, grad_mid, gain_row, w_out_part, middle):
+def back_dense(sums_in, produced, full_q, full_kv, normed, grad_pre, tokens, gains, grad_mid, gain_row, w_out_part, middle):
     tok_rows, width = middle.shape
-    in_width = full_in.shape[1]
+    q_width = full_q.shape[1]
+    in_width = q_width + full_kv.shape[1]
     pre_width = in_width - LANES
     w_rows = width
     group, rows = w_rows // 8, w_rows // (8 * LINE)
     chunks = sums_in.shape[0] // CHUNK - SPLIT
 
     def kernel(
-        sums_ref, prod_ref, full_ref, normed_ref, pre_ref, tok_ref, gain_ref, mid_grad_ref, gain_row_ref, o_part_ref,
+        sums_ref, prod_ref, full_q_ref, full_kv_ref, normed_ref, pre_ref, tok_ref, gain_ref, mid_grad_ref, gain_row_ref, o_part_ref,
         middle_ref,
-        total_ref, layer_ref, tok_grad_ref, in_ref, out_ref,
+        total_ref, layer_ref, tok_grad_ref, wq_ref, wk_ref, wv_ref, gains_ref, out_ref,
         sums_own, sums_land, own, core_in, first_in, second_in, moe, part, d_core, d_first, d_second, in_sums,
         in_land, o_sums, o_land, normed_grad, gain_rows, here, send, recv,
     ):
@@ -1127,7 +1330,9 @@
         @pl.loop(0, width // wide)
         def _(step):
             cut = pl.ds(pl.multiple_of(step * wide, wide), wide)
-            normed_grad[:, cut] = dot(pre_ref[...], full_ref[cut, :pre_width], 1, 1)
+            normed_grad[:, cut] = dot(pre_ref[:, :q_width], full_q_ref[cut, :], 1, 1) + dot(
+                pre_ref[:, q_width:], full_kv_ref[cut, : pre_width - q_width], 1, 1
+            )
 
         gain_rows[...] = jnp.zeros_like(gain_rows)
         gain_rows[1:2, :] = gain_row_ref[0:1, :]
@@ -1190,8 +1395,8 @@
             cut = pl.ds(pl.multiple_of(step * tile, tile), tile)
             layer_ref[cut, :] = (middle_ref[cut, :] + moe[cut, :]).astype(jnp.bfloat16)
 
-        o_line.finish(out_ref)
-        in_line.finish(in_ref)
+        o_line.finish((out_ref,))
+        in_line.finish((wq_ref, wk_ref, wv_ref, gains_ref))
         summed.finish()
 
     f32, low = jnp.float32, jnp.bfloat16
@@ -1201,11 +1406,14 @@
             jax.ShapeDtypeStruct((chunks * CHUNK, sums_in.shape[1]), low),
             jax.ShapeDtypeStruct((tok_rows, width), low),
             jax.ShapeDtypeStruct((tok_rows, width), f32),
-            jax.ShapeDtypeStruct((rows, in_width), f32),
+            jax.ShapeDtypeStruct((rows, q_width), f32),
+            jax.ShapeDtypeStruct((rows, (pre_width - q_width) // 2), f32),
+            jax.ShapeDtypeStruct((rows, (pre_width - q_width) // 2), f32),
+            jax.ShapeDtypeStruct((rows, LANES), f32),
             jax.ShapeDtypeStruct((rows, width), f32),
         ),
-        in_specs=[ANY, ANY] + [VMEM] * 9,
-        out_specs=(VMEM,) * 5,
+        in_specs=[ANY, ANY] + [VMEM] * 10,
+        out_specs=(VMEM,) * 8,
         scratch_shapes=[
             pltpu.VMEM((chunks * CHUNK, sums_in.shape[1]), low),
             pltpu.VMEM((chunks * CHUNK, sums_in.shape[1]), low),
@@ -1227,7 +1435,7 @@
         compiler_params=kernel_params(4, 63),
         name="back_dense",
     )(
-        sums_in, produced, full_in, normed, grad_pre, tokens, gains, grad_mid, gain_row, w_out_part, middle
+        sums_in, produced, full_q, full_kv, normed, grad_pre, tokens, gains, grad_mid, gain_row, w_out_part, middle
     )
 
 
@@ -1250,125 +1458,34 @@
     tok_rows = tokens.shape[0]
     ctx_size = lax.axis_size("ctx")
     ctx_place = lax.axis_index("ctx")
-    group_rows = tok_rows * ctx_size
-    group_places = jnp.arange(group_rows, dtype=jnp.int32)
+    group_places = jnp.arange(tok_rows * ctx_size, dtype=jnp.int32)
     seg_all, within_all = seq_tables(lengths[0], group_places)
     offset = ctx_place * tok_rows
     own_places = offset + jnp.arange(tok_rows, dtype=jnp.int32)
-    seg_own = lax.dynamic_slice_in_dim(seg_all, offset, tok_rows)
     within_own = lax.dynamic_slice_in_dim(within_all, offset, tok_rows)
-    allowed = (seg_own[:, None] == seg_all[None, :]) & (
-        group_places[None, :] <= own_places[:, None]
-    )
     kv_columns = KVH * HD
     q_columns = HEADS * HD
     gains = jnp.pad(jnp.stack([norm_attn, norm_moe], axis=1), ((0, 0), (0, LANES - 2)))
-    w_in = jnp.concatenate([w_query, w_key, w_value, gains], axis=1)
-    experts = jnp.arange(8, dtype=jnp.int32)
+    numbers = jnp.arange(8, dtype=jnp.int32)
     gates = jnp.sum(
-        jnp.where(routes[None, :, :] == experts[:, None, None], gate_values[None], 0.0), axis=2
-    )
-    full_in, full_o, cot_all, gates_all = gather_inputs(w_in, w_out, cotangent, gates)
-    full_q = full_in[:, :q_columns]
-    full_k = full_in[:, q_columns : q_columns + kv_columns]
-    full_v = full_in[:, q_columns + kv_columns : q_columns + 2 * kv_columns]
-    both_gains = full_in[:, q_columns + 2 * kv_columns :][:, :2].astype(jnp.float32).T
-    gain_attn_f, gain_moe_f = both_gains[0], both_gains[1]
-    inputs = tokens.astype(jnp.float32)
-    normed_low = rms_norm(inputs, gain_attn_f).astype(jnp.bfloat16)
-    pre = jnp.dot(
-        normed_low, full_in[:, : q_columns + 2 * kv_columns], preferred_element_type=jnp.float32
-    )
-    query_pre = pre[:, :q_columns]
-    key_pre = pre[:, q_columns : q_columns + kv_columns]
-    value_pre = pre[:, q_columns + kv_columns :]
-    query = rotate(query_pre.reshape(tok_rows, HEADS, HD), within_own, 1.0).astype(jnp.bfloat16)
-    key_low = rotate(key_pre.reshape(tok_rows, KVH, HD), within_own, 1.0).astype(jnp.bfloat16)
-    key_low = key_low.reshape(tok_rows, kv_columns)
-    all_kv = gather_line(jnp.concatenate([key_low, value_pre.astype(jnp.bfloat16)], axis=1))
-    all_keys, all_values = all_kv[:, :kv_columns], all_kv[:, kv_columns:]
-    per_group = HEADS // KVH
-    score_scale = HD ** (-0.5)
-    query_groups = query.reshape(tok_rows, KVH, per_group, HD)
-
-    def softmax_weights(group_number):
-        keys_part = all_keys[:, group_number * HD : (group_number + 1) * HD]
-        raw = jnp.einsum(
-            "qjd,kd->jqk",
-            query_groups[:, group_number],
-            keys_part,
-            preferred_element_type=jnp.float32,
-        )
-        scores = jnp.where(allowed[None], raw * score_scale, masked_score)
-        row_top = jnp.max(scores, axis=-1, keepdims=True)
-        expo = jnp.exp(scores - row_top)
-        row_sum = jnp.sum(expo, axis=-1, keepdims=True)
-        return expo / row_sum, (row_top + jnp.log(row_sum))[:, :, 0]
-
-    mixed_parts = []
-    lse_parts = []
-    for group_number in range(KVH):
-        probs, lse_part = softmax_weights(group_number)
-        lse_parts.append(lse_part)
-        values_part = all_values[:, group_number * HD : (group_number + 1) * HD]
-        mixed_group = jnp.einsum(
-            "jqk,kd->qjd",
-            probs.astype(jnp.bfloat16),
-            values_part,
-            preferred_element_type=jnp.float32,
-        )
-        mixed_parts.append(mixed_group.reshape(tok_rows, per_group * HD))
-    mixed_low = jnp.concatenate(mixed_parts, axis=1).astype(jnp.bfloat16)
-    lse = jnp.pad(jnp.concatenate(lse_parts, axis=0), ((0, 16 - HEADS), (0, 0)))
+        jnp.where(routes[None, :, :] == numbers[:, None, None], gate_values[None], 0.0), axis=2
+    )
     half_size = HD // 2
     frequency = rope_base ** (-jnp.arange(half_size, dtype=jnp.float32) / half_size)
     angles = within_own.astype(jnp.float32)[:, None] * frequency[None, :]
     cosine = jnp.concatenate([jnp.cos(angles), jnp.cos(angles)], axis=1)
     sine = jnp.concatenate([-jnp.sin(angles), jnp.sin(angles)], axis=1)
     starts = jnp.broadcast_to((own_places - within_own)[None, :], (8, tok_rows))
-    gain_rows = jnp.pad(both_gains, ((0, 6), (0, 0)))
-    middle = inputs + jnp.dot(mixed_low, full_o, preferred_element_type=jnp.float32)
-    routed_low = rms_norm(middle, gain_moe_f).astype(jnp.bfloat16)
-
-    routed_all = gather_plane(routed_low)
-    my_expert = lax.axis_index("dp")
-    gate_mine = lax.dynamic_index_in_dim(
-        gates_all.reshape(8, 8, tok_rows), my_expert, axis=1, keepdims=False
-    ).reshape(8 * tok_rows, 1)
-    w_gate_e, w_up_e, w_down_e = w_gate[0], w_up[0], w_down[0]
-    gate_act = jnp.dot(routed_all, w_gate_e, preferred_element_type=jnp.float32)
-    up_act = jnp.dot(routed_all, w_up_e, preferred_element_type=jnp.float32)
-    hidden_low = (jax.nn.silu(gate_act) * up_act).astype(jnp.bfloat16)
-    grad_arrived = (cot_all.astype(jnp.float32) * gate_mine).astype(jnp.bfloat16)
-    grad_hidden = jnp.einsum(
-        "cd,fd->cf", grad_arrived, w_down_e, preferred_element_type=jnp.float32
-    )
-    grad_w_down = jnp.einsum(
-        "cf,cd->fd", hidden_low, grad_arrived, preferred_element_type=jnp.float32
-    )
-    glu_value, glu_pull = jax.vjp(
-        lambda gate_in, up_in: jax.nn.silu(gate_in) * up_in, gate_act, up_act
-    )
-    grad_gate, grad_up = glu_pull(grad_hidden)
-    grad_gate_low = grad_gate.astype(jnp.bfloat16)
-    grad_up_low = grad_up.astype(jnp.bfloat16)
-    grad_w_gate = jnp.einsum(
-        "cd,cf->df", routed_all, grad_gate_low, preferred_element_type=jnp.float32
-    )
-    grad_w_up = jnp.einsum(
-        "cd,cf->df", routed_all, grad_up_low, preferred_element_type=jnp.float32
-    )
-    half = grad_w_down.shape[1] // 2
-    partial_sums = jnp.concatenate(
-        [grad_w_gate, grad_w_up, grad_w_down[:, :half], grad_w_down[:, half:]], axis=0
-    ).astype(jnp.bfloat16)
-    grad_sent = (
-        jnp.einsum("cf,df->cd", grad_gate_low, w_gate_e, preferred_element_type=jnp.float32)
-        + jnp.einsum("cf,df->cd", grad_up_low, w_up_e, preferred_element_type=jnp.float32)
-    ).astype(jnp.bfloat16)
-    produced = jnp.dot(hidden_low, w_down_e, preferred_element_type=jnp.float32)
-    produced = produced.astype(jnp.bfloat16).astype(jnp.float32) * gate_mine
-    produced = produced.astype(jnp.bfloat16)
+    (
+        full_q, full_kv, full_o, all_cot, all_gate, query, all_kv, lse, mixed_low, middle, normed_low, routed_low,
+        gain_rows,
+    ) = front(
+        w_query, w_key, w_value, gains, w_out, cotangent, gates, tokens, starts, cosine, sine
+    )
+    partial_sums, grad_sent, produced = experts(
+        routed_low, all_cot, all_gate, w_gate[0], w_up[0], w_down[0]
+    )
+    half = w_gate.shape[2]
     sums_head, grad_mid, grad_pre, gain_row, w_out_part = back_attention(
         partial_sums,
         grad_sent,
@@ -1377,17 +1494,18 @@
         cotangent,
         gain_rows,
         mixed_low,
-        query.reshape(tok_rows, q_columns),
+        query,
         all_kv,
         lse,
         starts,
         cosine,
         sine,
     )
-    sums_tail, layer_out, grad_tokens, in_sums, out_sums = back_dense(
+    sums_tail, layer_out, grad_tokens, sum_q, sum_k, sum_v, sum_gains, sum_o = back_dense(
         partial_sums,
         produced,
-        full_in,
+        full_q,
+        full_kv,
         normed_low,
         grad_pre,
         tokens,
@@ -1397,23 +1515,23 @@
         w_out_part,
         middle,
     )
-    expert_sums = jnp.concatenate([sums_head, sums_tail], axis=0).astype(jnp.float32)
-    width = D
-    edge = q_columns + 2 * kv_columns
+    in_tail = D - sums_head.shape[0]
+
+    def whole(columns):
+        return jnp.concatenate([sums_head[:, columns], sums_tail[:in_tail, columns]], axis=0)
+
     return (
         layer_out,
         grad_tokens,
-        in_sums[:, edge],
-        in_sums[:, :q_columns],
-        in_sums[:, q_columns : q_columns + kv_columns],
-        in_sums[:, q_columns + kv_columns : edge],
-        out_sums,
-        in_sums[:, edge + 1],
-        expert_sums[None, :width],
-        expert_sums[None, width : 2 * width],
-        jnp.concatenate(
-            [expert_sums[None, 2 * width : 2 * width + half], expert_sums[None, 2 * width + half :]], axis=2
-        ),
+        sum_gains[:, 0],
+        sum_q,
+        sum_k,
+        sum_v,
+        sum_o,
+        sum_gains[:, 1],
+        whole(slice(0, half)).astype(jnp.float32)[None],
+        whole(slice(half, 2 * half)).astype(jnp.float32)[None],
+        sums_tail[in_tail:].astype(jnp.float32)[None],
     )
 
 

time: 675 us -> 482 us (0.71)
  matrix products: 99.7 us -> 0 us
  other arithmetic: 58 us -> 14.8 us
  local copies, waits for them, and re-layouts: 42.3 us -> 9.19 us
  Pallas kernels: 465 us -> 453 us
    dot_general x15 -> x0, matrix products: 99.7 us -> none  [the longest x1 12.4 us: on_plane_device(): gate_act = jnp.dot(routed_all, w_gate_e, preferred_element_type=jnp.float32)]
    concatenate x9 -> x0, other arithmetic: 35.7 us -> none  [the longest x1 25.7 us: on_plane_device(): jnp.concatenate([grad_w_gate, grad_w_up, grad_w_down[:, :half], grad_w_do...]
    pallas_call x3 -> x2, Pallas kernels: 197 us -> 185 us  [the longest x1 106 us: front(): pl.pallas_call(kernel, out_shape=(jax.ShapeDtypeStruct((w_rows, width), l...]
    pallas_call x1 -> x0, local copies, waits for them, and re-layouts: 9.83 us -> none  [gather_inputs(): pl.pallas_call(kernel, out_shape=(jax.ShapeDtypeStruct((planes * group, w...]
    slice x9 -> x1, local copies, waits for them, and re-layouts: 10 us -> 1.51 us  [on_plane_device(): sum_gains[:, 1]]
    broadcast_in_dim x1 -> x0, local copies, waits for them, and re-layouts: 8.25 us -> none  [on_plane_device(): expert_sums[None, width:2 * width]]
where the time goes in v3:
time: 482 us; the launch traced here: 478 us
  Pallas kernels  453 us (94%)
  other arithmetic  14.8 us (3%)
  local copies, waits for them, and re-layouts  9.19 us (2%)
    pallas_call x1, Pallas kernels, back_dense(): pl.pallas_call(kernel, out_shape=(jax.ShapeDtypeStruct((chunks * CHUNK, s...  142 us
    pallas_call x1, Pallas kernels, back_attention(): pl.pallas_call(kernel, out_shape=(jax.ShapeDtypeStruct((chunks * CHUNK, s...  125 us
    pallas_call x1, Pallas kernels, front(): pl.pallas_call(kernel, out_shape=(jax.ShapeDtypeStruct((w_rows, width), l...  106 us
    pallas_call x1, Pallas kernels, experts(): pl.pallas_call(kernel, out_shape=(jax.ShapeDtypeStruct((width + hidden_wi...  79.6 us

profile of v3, /device:TPU:0, one launch (start us, length us, event | category | flops | bytes accessed | tf_op | source)
XLA Modules:
  0.0 477.8 jit_solution(14170351133529134790)
XLA Ops:
  0.6 0.7 pad_maximum_fusion.2
  1.3 0.8 reduce-window.8
  2.2 0.7 select_reduce_fusion.1
  3.0 0.6 broadcast_in_dim.52.starts_ref
  3.6 1.3 select_reduce_fusion.gate_ref
  5.0 0.6 pad.4.gains_ref
  5.6 0.5 fusion
  6.2 0.8 pad_maximum_fusion
  7.0 105.6 %front.1 = (bf16[1536,1536]{1,0:T(8,128)(2,1)}, bf16[1536,640]{1,0:T(8,128)(2,1)}, bf16[1536,1536]{1,0:T(8,128)(2,1)}, bf16[2048,1536]{1,0:T(8,128)(2,1)}, f32[6...) custom-call(bf16[48,1536]{1,0:T(8,128)(2,1)} %wq_ref.1, ...), custom_call_target="tpu_custom_call" | custom-call | tf_op jit(solution)/shard_map/front/pallas_call | solution.py:818
  112.6 79.6 %experts.1 = (bf16[2304,1536]{1,0:T(8,128)(2,1)}, bf16[2048,1536]{1,0:T(8,128)(2,1)}, bf16[2048,1536]{1,0:T(8,128)(2,1)}) custom-call(bf16[256,1536]{1,0:T(8,128)(2,1)} %get-tuple-element.40.routed_ref, bf16[2048,1536]{1,0:T(8,128)(2,1)} %get-tuple-element.41.cot_ref, f32[64,256]{1,0:T(8,128)} %get-tuple-element.42.gate_ref, bf16[1536,768]{1,0:T(8,128)(2,1)} %bitcast.19, ...), custom_call_target="tpu_custom_call" | custom-call | tf_op jit(solution)/shard_map/experts/pallas_call | solution.py:954
  192.2 125.3 %back_attention.1 = (bf16[1056,1536]{1,0:T(8,128)(2,1)}, f32[256,1536]{1,0:T(8,128)}, bf16[256,2048]{1,0:T(8,128)(2,1)}, f32[8,1536]{1,0:T(8,128)}, bf16[192,1536]{1,0:T(8,128)(2,1)}) custom-call(bf16[2304,1536]{1,0:T(8,128)(2,1)} %get-tuple-element.43.sums_ref, bf16[2048,1536]{1,0:T(8,128)(2,1)} %get-tuple-element.48.sent_ref, ...), custom_call_target="tpu_custom_call" | custom-call | tf_op jit(solution)/shard_map/back_attention/pallas_call | solution.py:1239
  317.6 142.1 %back_dense.1 = (bf16[1248,1536]{1,0:T(8,128)(2,1)}, bf16[256,1536]{1,0:T(8,128)(2,1)}, f32[256,1536]{1,0:T(8,128)}, f32[48,1536]{1,0:T(8,128)}, f32[48,256]{1,0...) custom-call(bf16[2304,1536]{1,0:T(8,128)(2,1)} %get-tuple-element.43.sums_ref, ...), custom_call_target="tpu_custom_call" | custom-call | tf_op jit(solution)/shard_map/back_dense/pallas_call | solution.py:1403
  459.7 1.5 slice_reduce_fusion
  461.2 1.4 slice_bitcast_fusion.2
  462.7 4.6 bitcast_convert_fusion
  467.3 0.2 slice_bitcast_fusion
  467.5 2.5 maximum_convert_fusion.1
  470.1 2.5 maximum_convert_fusion
  472.6 0.9 copy.43
  473.5 1.1 copy.44
  474.7 0.7 copy.45
  475.4 0.6 copy.46
  476.0 0.6 copy.47
  476.6 0.7 copy.48
  (18 shorter events, 0.2 us)
Async XLA Ops:
  462.7 4.7 copy-start
  470.1 2.6 copy-start.2
  470.1 3.5 copy-start.1
  472.6 2.0 copy-start.4
  472.6 2.8 copy-start.6
  472.6 3.4 copy-start.5
  472.6 4.0 copy-start.3

commit v4 on v3

--- a/solution.py
+++ b/solution.py
@@ -418,14 +418,12 @@
 
 
 class PlaneGather:
-    CHIP = (
-        ((2, 0, 0), (4, 0, 1)),
-        ((4, 0, 0), (4, 2, 0), (2, 0, 1), (2, 4, 1)),
-    )
+    CHIP = (((2, 0, 0), (4, 0, 1)), ((4, 0, 0), (2, 0, 1)), ((4, 2, 0), (2, 4, 1)))
     CORE = (
         ((1, 0, 2),),
         ((1, 2, 0), (1, 4, 1)),
-        ((1, 4, 0), (1, 6, 0), (1, 2, 1), (1, 6, 1)),
+        ((1, 4, 0), (1, 2, 1)),
+        ((1, 6, 0), (1, 6, 1)),
     )
     COPIES = 13
 
@@ -436,6 +434,7 @@
         for stage in self.CHIP + self.CORE:
             for one in stage:
                 self.number[one] = first + len(self.number)
+        self.core_left = [0, 1, 2, 3]
 
     def _copy(self, one, from_me):
         to, whose, half = one
@@ -447,18 +446,28 @@
         part = self.ref.at[pl.ds(pl.multiple_of(begin, 16), size)]
         return self.wires.copy(part, part, self.number[one], dp=masked(dp, to))
 
-    def start(self, stage):
+    def start(self, stage, far=True):
         for one in (self.CHIP[stage] if stage < 2 else ()) + self.CORE[stage]:
+            self._copy(one, True).start()
+        if stage == 1 and far:
+            self.start_far()
+
+    def start_far(self):
+        for one in self.CHIP[2]:
             self._copy(one, True).start()
 
     def wait(self, stage):
         for one in self.CHIP[stage]:
             self._copy(one, False).wait_recv()
 
+    def wait_core(self, stage):
+        self.core_left.remove(stage)
+        for one in self.CORE[stage]:
+            self._copy(one, False).wait_recv()
+
     def finish(self):
-        for stage in self.CORE:
-            for one in stage:
-                self._copy(one, False).wait_recv()
+        for stage in list(self.core_left):
+            self.wait_core(stage)
         for one in self.number:
             self._copy(one, True).wait_send()
 
@@ -517,11 +526,14 @@
         self._far(number).wait()
         add_rows(self.core_in, row, self.core_in, row, self.first_in, in_row, self.half)
 
+    def start_core(self, slot):
+        self._core(slot).start()
+
     def step(self, number):
         g, h = self.group, self.half
         if number == 0:
             for slot in (3, 2, 1, 0):
-                self._core(slot).start()
+                self.start_core(slot)
         elif number == 1:
             self._sum_core(3)
             self._far(0).start()
@@ -557,45 +569,52 @@
 
 class LineReduce:
     COPIES = 2 * (LINE - 1) * LINE
-
-    def __init__(self, wires, part, rows, landing):
-        self.wires, self.part, self.rows, self.landing = wires, part, rows, landing
+    EVENTS = ((0, 0), (0, 1), (1, 0), (0, 2), (1, 1), (2, 0))
+
+    def __init__(self, wires, part, rows, landing, ways=(1, -1)):
+        self.wires, self.part, self.rows, self.landing, self.ways = wires, part, rows, landing, ways
         self.first = wires.take(self.COPIES)
 
-    def _copy(self, way, hop, block, z):
-        number = ((0 if way == 1 else 1) * (LINE - 1) + hop) * LINE + block
+    def _place(self, way, hop, nearer):
+        return (LINE - 1 - nearer, hop) if way == 1 else (nearer, LINE - 1 - hop)
+
+    def _copy(self, way, hop, nearer, z):
+        side = self.ways.index(way)
+        block, _ = self._place(way, hop, nearer)
         return self.wires.copy(
             self.part.at[pl.ds(block * self.rows, self.rows)],
-            self.landing.at[pl.ds(((0 if way == 1 else 1) * LINE + block) * self.rows, self.rows)],
-            self.first + number,
+            self.landing.at[pl.ds((side * LINE + block) * self.rows, self.rows)],
+            self.first + (side * (LINE - 1) + hop) * LINE + nearer,
             z=z,
         )
 
-    def _moves(self, hop):
-        for way in (1, -1):
-            source = hop if way == 1 else LINE - 1 - hop
-            for block in range(LINE - 1, hop, -1) if way == 1 else range(0, LINE - 1 - hop):
-                yield way, block, source
-
-    def start(self, hop):
+    def _send(self, way, hop, nearer):
         z = self.wires.z
-        for way, block, source in self._moves(hop):
-
-            @pl.when(z == source)
-            def _():
-                self._copy(way, hop, block, z + way).start()
-
-    def add(self, hop):
+
+        @pl.when(z == self._place(way, hop, nearer)[1])
+        def _():
+            self._copy(way, hop, nearer, z + way).start()
+
+    def begin(self):
+        for nearer in range(LINE - 1):
+            for way in self.ways:
+                self._send(way, 0, nearer)
+
+    def event(self, number):
+        hop, nearer = self.EVENTS[number]
         z, rows = self.wires.z, self.rows
-        for way, block, source in self._moves(hop):
+        for way in self.ways:
+            block, source = self._place(way, hop, nearer)
 
             @pl.when(z == source + way)
             def _():
-                self._copy(way, hop, block, z).wait_recv()
-                place = ((0 if way == 1 else 1) * LINE + block) * rows
+                self._copy(way, hop, nearer, z).wait_recv()
+                landed = (self.ways.index(way) * LINE + block) * rows
                 add_rows(
-                    self.part, block * rows, self.part, block * rows, self.landing, place, rows
+                    self.part, block * rows, self.part, block * rows, self.landing, landed, rows
                 )
+                if nearer < LINE - 2 - hop:
+                    self._copy(way, hop + 1, nearer, z + way).start()
 
     def finish(self, outs):
         z, rows = self.wires.z, self.rows
@@ -610,16 +629,16 @@
                 ].astype(out.dtype)
                 begin += out.shape[1]
 
-        for hop in range(LINE - 1):
-            for way, block, source in self._moves(hop):
-
-                @pl.when(z == source)
+        for hop, nearer in self.EVENTS:
+            for way in self.ways:
+
+                @pl.when(z == self._place(way, hop, nearer)[1])
                 def _():
-                    self._copy(way, hop, block, z + way).wait_send()
+                    self._copy(way, hop, nearer, z + way).wait_send()
 
     @staticmethod
-    def scratch(rows, columns):
-        return pltpu.VMEM((2 * LINE * rows, columns), jnp.bfloat16)
+    def scratch(rows, columns, ways=2):
+        return pltpu.VMEM((ways * LINE * rows, columns), jnp.bfloat16)
 
 
 def sems(count):
@@ -692,30 +711,42 @@
             part = all_gate.at[pl.ds(pl.multiple_of(owner * 8, 8), 8)]
             return wires.copy(part, part, first + mask - 1, dp=masked(dp, mask))
 
-        for step in range(LINE - 1):
-            line_kv.start(step)
-            line_q.start(step)
-            if step == 0:
-                for mask in range(1, planes):
-                    gate_copy(mask, dp).start()
-                key_place = lax.broadcasted_iota(jnp.int32, (keys, tok_rows), 0)
-                query_place = lax.broadcasted_iota(jnp.int32, (keys, tok_rows), 1) + z * tok_rows
-                allowed = (key_place >= starts_ref[0:1, :]) & (key_place <= query_place)
-                bias[...] = jnp.where(allowed, 0.0, masked_score)
-            line_kv.wait(step)
-            if step == LINE - 2:
-                plane_kv.start(0)
-            line_q.wait(step)
+        line_kv.start(0)
+        line_q.start(0)
+        plane_cot.start(0)
+        for mask in range(1, planes):
+            gate_copy(mask, dp).start()
+        key_place = lax.broadcasted_iota(jnp.int32, (keys, tok_rows), 0)
+        query_place = lax.broadcasted_iota(jnp.int32, (keys, tok_rows), 1) + z * tok_rows
+        allowed = (key_place >= starts_ref[0:1, :]) & (key_place <= query_place)
+        bias[...] = jnp.where(allowed, 0.0, masked_score)
+        line_kv.wait(0)
+        line_kv.start(1)
+        line_q.wait(0)
+        line_q.start(1)
+        plane_cot.wait(0)
+        plane_cot.start(1, far=False)
+        line_kv.wait(1)
+        line_kv.start(2)
+        line_q.wait(1)
+        line_q.start(2)
+        line_kv.wait(2)
+        plane_kv.start(0)
+        line_q.wait(2)
         plane_q.start(0)
+        line_o.start(0)
+        plane_cot.wait(1)
+        plane_cot.start(2)
         plane_kv.wait(0)
         plane_kv.start(1)
-        line_o.start(0)
-        plane_kv.wait(1)
-        plane_kv.start(2)
         plane_q.wait(0)
         plane_q.start(1)
         line_o.wait(0)
         line_o.start(1)
+        plane_kv.wait(1)
+        plane_kv.start(2)
+        plane_kv.wait(2)
+        plane_kv.start(3)
         plane_kv.finish()
 
         gain_rows_ref[...] = full_kv[:, kv_width:].astype(jnp.float32).T[:8, :]
@@ -741,13 +772,12 @@
         line_keys.start(1)
         line_o.wait(2)
         plane_o.start(0)
-        plane_cot.start(0)
         plane_q.wait(1)
         plane_q.start(2)
-        plane_o.wait(0)
-        plane_o.start(1)
-        plane_cot.wait(0)
-        plane_cot.start(1)
+        line_keys.wait(1)
+        line_keys.start(2)
+        plane_q.wait(2)
+        plane_q.start(3)
         plane_q.finish()
         saves = [pltpu.make_async_copy(full_q, out_q, there.at[0])]
         saves.append(pltpu.make_async_copy(full_kv, out_kv, there.at[1]))
@@ -763,14 +793,11 @@
                     pre_q[:, one * HD : (one + 1) * HD], cos_ref[...], sin_ref[...]
                 ).astype(jnp.bfloat16)
 
-        line_keys.wait(1)
-        line_keys.start(2)
         line_keys.wait(2)
         value_t[...] = all_kv[:, key_width:].astype(jnp.float32).T.astype(jnp.bfloat16)
         lse_ref[...] = jnp.zeros_like(lse_ref)
 
-        @pl.loop(0, HEADS)
-        def _(head):
+        def attend(head):
             own_cut = pl.ds(pl.multiple_of(head * HD, HD), HD)
             key_cut = pl.ds(pl.multiple_of((head // per_group) * HD, HD), HD)
             scores = dot(all_kv[:, key_cut], query_ref[:, own_cut], 1, 1) * score_scale + bias[...]
@@ -781,8 +808,15 @@
             probs = (expo * (1.0 / total)).astype(jnp.bfloat16)
             mixed_ref[:, own_cut] = dot(value_t[key_cut, :], probs, 1, 0).T.astype(jnp.bfloat16)
 
+        pl.loop(0, 2)(attend)
+        plane_o.wait(0)
+        plane_o.start(1)
+        plane_cot.start_far()
+        pl.loop(2, HEADS)(attend)
         plane_o.wait(1)
         plane_o.start(2)
+        plane_o.wait(2)
+        plane_o.start(3)
         plane_o.finish()
         saves.append(pltpu.make_async_copy(full_o, out_o, there.at[2]))
         saves[2].start()
@@ -799,8 +833,8 @@
             cut = pl.ds(pl.multiple_of(step * tile, tile), tile)
             routed_ref[cut, :] = rms_norm(middle_ref[cut, :], gain_rows_ref[1:2, :]).astype(jnp.bfloat16)
 
-        plane_cot.wait(1)
-        plane_cot.start(2)
+        plane_cot.wait(2)
+        plane_cot.start(3)
         plane_cot.finish()
         saves.append(pltpu.make_async_copy(all_cot, out_cot, there.at[3]))
         saves[3].start()
@@ -855,42 +889,55 @@
     hidden_width = w_gate.shape[1]
     total_rows = 8 * tok_rows
 
+    sum_rows = width + hidden_width
+    chunks = WITH_EXPERTS
+
     def kernel(
         routed_ref, cot_ref, gate_ref, wg_ref, wu_ref, wd_ref,
-        sums_ref, sent_ref, prod_ref,
-        w_in, w_down, x_all, y_all, hidden, grad_hidden, grad_in, sums, gate_t, stage, here, there, send, recv,
+        sums_ref, prod_ref, total_ref, routed_grad_ref,
+        w_in, w_down, x_all, y_all, hidden, grad_hidden, grad_in, sums, sums_land, gate_t, core_in, first_in,
+        second_in, here, there, send, recv,
     ):
         wires = Wires(send, recv)
         dp = wires.dp
         own = pltpu.make_async_copy(routed_ref, x_all.at[rows_at(dp * tok_rows, tok_rows)], here.at[0])
         loads = [
-            pltpu.make_async_copy(cot_ref, y_all, here.at[1]),
-            pltpu.make_async_copy(wd_ref, w_down, here.at[2]),
+            pltpu.make_async_copy(wd_ref, w_down, here.at[1]),
+            pltpu.make_async_copy(cot_ref, y_all, here.at[2]),
             pltpu.make_async_copy(wg_ref, w_in.at[:, pl.ds(0, hidden_width)], here.at[3]),
             pltpu.make_async_copy(wu_ref, w_in.at[:, pl.ds(hidden_width, hidden_width)], here.at[4]),
         ]
         own.start()
         for one in loads:
             one.start()
-        greet(wires, (1, 2, 4), False)
+        greet(wires, (1, 2, 4), True)
         own.wait()
         spread = PlaneGather(wires, x_all, tok_rows)
+        plane = PlaneReduce(
+            wires, x_all, tok_rows, x_all, lambda slot: rows_begin(masked(dp, 2 * slot)), core_in, first_in, second_in,
+            routed_grad_ref,
+        )
+        summed = LineSum(wires, sums, total_ref, sums_land, CHUNK, chunks)
         spread.start(0)
         gate_t[...] = gate_ref[...].T
-        for one in loads:
-            one.wait()
+
+        def rows_begin(block):
+            return pl.multiple_of(block * tok_rows, 16)
+
+        def cut_of(block):
+            return pl.ds(rows_begin(block), tok_rows)
 
         def gate_of(block):
             lane = lax.broadcasted_iota(jnp.int32, gate_t.shape, 1)
             return jnp.sum(jnp.where(lane == block * 8 + dp, gate_t[...], 0.0), axis=1, keepdims=True)
 
         def back_hidden(block):
-            cut = rows_at(block * tok_rows, tok_rows)
+            cut = cut_of(block)
             y_all[cut, :] = (y_all[cut, :].astype(jnp.float32) * gate_of(block)).astype(jnp.bfloat16)
             grad_hidden[cut, :] = dot(y_all[cut, :], w_down[...], 1, 1)
 
-        def through(block):
-            cut = rows_at(block * tok_rows, tok_rows)
+        def through(mask):
+            cut = cut_of(masked(dp, mask))
             acts = dot(x_all[cut, :], w_in[...], 1, 0)
             gate_act, up_act = acts[:, :hidden_width], acts[:, hidden_width:]
             share = jax.nn.sigmoid(gate_act)
@@ -902,64 +949,104 @@
             ).astype(jnp.bfloat16)
             grad_in[cut, hidden_width:] = (grad * silu).astype(jnp.bfloat16)
 
+        loads[0].wait()
+        loads[1].wait()
         pl.loop(0, 4)(back_hidden)
         spread.wait(0)
         spread.start(1)
         pl.loop(4, 8)(back_hidden)
-        through(dp)
+        loads[2].wait()
+        loads[3].wait()
+        through(0)
+        spread.wait_core(0)
+        through(1)
         spread.wait(1)
         spread.start(2)
+        through(2)
+        through(4)
+        spread.wait_core(1)
+        spread.wait_core(2)
+        through(3)
+        through(5)
+        spread.wait(2)
+        spread.start(3)
+        through(6)
+        spread.wait_core(3)
+        through(7)
         spread.finish()
-        for mask in range(1, 8):
-            through(masked(dp, mask))
-
-        @pl.loop(0, width // 256)
-        def _(step):
+
+        def weights_in(step):
             cut = rows_at(step * 256, 256)
             sums[cut, :] = dot(x_all[:, cut], grad_in[...], 0, 0).astype(jnp.bfloat16)
 
-        @pl.loop(0, hidden_width // 256)
-        def _(step):
+        def weights_down(step):
             cut = rows_at(step * 256, 256)
             out = rows_at(width + step * 256, 256)
             sums[out, :] = dot(hidden[:, cut], y_all[...], 0, 0).astype(jnp.bfloat16)
 
-        save = pltpu.make_async_copy(sums, sums_ref, there.at[0])
+        def save_sums(begin, end, number):
+            rows = pl.ds(begin, end - begin)
+            return pltpu.make_async_copy(sums.at[rows], sums_ref.at[rows], there.at[number])
+
+        pl.loop(0, 2)(weights_in)
+        summed.begin()
+        pl.loop(2, 4)(weights_in)
+        pl.loop(4, 6)(weights_in)
+        summed.tick()
+        pl.loop(0, 3)(weights_down)
+        summed.tick()
+        save = save_sums(chunks * CHUNK, sum_rows, 0)
         save.start()
 
-        def stage_copy(slot, ref, block):
+        def input_grads(side):
+            for slot in (3, 2, 1, 0):
+                cut = cut_of(masked(dp, 2 * slot + side))
+                x_all[cut, :] = dot(grad_in[cut, :], w_in[...], 1, 1).astype(jnp.bfloat16)
+                if side:
+                    plane.start_core(slot)
+
+        input_grads(1)
+        summed.tick()
+        input_grads(0)
+        summed.tick()
+        plane.step(1)
+        plane.step(2)
+        summed.tick()
+
+        def save_made(block):
             return pltpu.make_async_copy(
-                stage.at[slot], ref.at[rows_at(block * tok_rows, tok_rows)], there.at[1 + slot]
+                y_all.at[cut_of(block)], prod_ref.at[cut_of(block)], there.at[1 + block]
             )
 
+        def make(block):
+            made = dot(hidden[cut_of(block), :], w_down[...], 1, 0).astype(jnp.bfloat16).astype(jnp.float32)
+            y_all[cut_of(block), :] = (made * gate_of(block)).astype(jnp.bfloat16)
+            save_made(block).start()
+
+        pl.loop(0, 4)(make)
+        summed.tick()
+        pl.loop(4, 8)(make)
+        plane.step(3)
+        summed.tick(2)
+        plane.step(4)
+        summed.tick(2)
+        plane.step(5)
+        summed.finish()
         for block in range(8):
-            slot = block % 2
-            cut = rows_at(block * tok_rows, tok_rows)
-            if block >= 2:
-                stage_copy(slot, sent_ref, block - 2).wait()
-            stage[slot] = dot(grad_in[cut, :], w_in[...], 1, 1).astype(jnp.bfloat16)
-            stage_copy(slot, sent_ref, block).start()
-        for block in range(8):
-            slot = block % 2
-            cut = rows_at(block * tok_rows, tok_rows)
-            stage_copy(slot, sent_ref if block < 2 else prod_ref, (block - 2) % 8).wait()
-            made = dot(hidden[cut, :], w_down[...], 1, 0).astype(jnp.bfloat16).astype(jnp.float32)
-            stage[slot] = (made * gate_of(block)).astype(jnp.bfloat16)
-            stage_copy(slot, prod_ref, block).start()
-        stage_copy(0, prod_ref, 6).wait()
-        stage_copy(1, prod_ref, 7).wait()
+            save_made(block).wait()
         save.wait()
 
     f32, low = jnp.float32, jnp.bfloat16
     return pl.pallas_call(
         kernel,
         out_shape=(
-            jax.ShapeDtypeStruct((width + hidden_width, width), low),
+            jax.ShapeDtypeStruct((sum_rows, width), low),
             jax.ShapeDtypeStruct((total_rows, width), low),
-            jax.ShapeDtypeStruct((total_rows, width), low),
+            jax.ShapeDtypeStruct((chunks * CHUNK, width), low),
+            jax.ShapeDtypeStruct((tok_rows, width), f32),
         ),
         in_specs=[VMEM, ANY, VMEM, ANY, ANY, ANY],
-        out_specs=(ANY,) * 3,
+        out_specs=(ANY, ANY, VMEM, VMEM),
         scratch_shapes=[
             pltpu.VMEM((width, 2 * hidden_width), low),
             pltpu.VMEM((hidden_width, width), low),
@@ -968,16 +1055,22 @@
             pltpu.VMEM((total_rows, hidden_width), low),
             pltpu.VMEM((total_rows, hidden_width), f32),
             pltpu.VMEM((total_rows, 2 * hidden_width), low),
-            pltpu.VMEM((width + hidden_width, width), low),
+            pltpu.VMEM((sum_rows, width), low),
+            pltpu.VMEM((chunks * CHUNK, width), low),
             pltpu.VMEM((tok_rows, 64), f32),
-            pltpu.VMEM((2, tok_rows, width), low),
-            pltpu.SemaphoreType.DMA((5,)),
-            pltpu.SemaphoreType.DMA((3,)),
         ]
-        + sems(PlaneGather.COPIES),
+        + PlaneReduce.scratch(tok_rows, width)
+        + [pltpu.SemaphoreType.DMA((5,)), pltpu.SemaphoreType.DMA((9,))]
+        + sems(PlaneGather.COPIES + PlaneReduce.COPIES + 3 * chunks),
         compiler_params=kernel_params(1, 63),
         name="experts",
     )(routed, all_cot, all_gate, w_gate, w_up, w_down)
+
+
+CHUNK = 64
+AHEAD = 4
+WITH_EXPERTS = 9
+WITH_ATTENTION = 7
 
 
 class LineSum:
@@ -1015,7 +1108,7 @@
     def begin(self):
         @pl.when(self.outer)
         def _():
-            for chunk in range(min(2, self.chunks)):
+            for chunk in range(min(AHEAD, self.chunks)):
                 self._in(chunk).start()
 
     def tick(self, count=1):
@@ -1030,8 +1123,8 @@
             @pl.when(self.outer)
             def _():
                 self._in(chunk).wait_send()
-                if chunk + 2 < self.chunks:
-                    self._in(chunk + 2).start()
+                if chunk + AHEAD < self.chunks:
+                    self._in(chunk + AHEAD).start()
 
         @pl.when(self.inner)
         def _():
@@ -1075,14 +1168,10 @@
     return values * cosine + pltpu.roll(values, HD // 2, 1) * sine
 
 
-CHUNK = 96
-SPLIT = 11
-
-
 def back_attention(
     sums_in,
-    grad_sent,
     full_o,
+    routed_grad,
     middle,
     cotangent,
     gain_moe,
@@ -1098,41 +1187,30 @@
     keys, kv_width = all_kv.shape
     w_rows = width
     group = w_rows // 8
-    chunks = SPLIT
+    skipped, chunks = WITH_EXPERTS, WITH_ATTENTION
 
     def kernel(
-        sums_ref, sent_ref, full_o_ref, middle_ref, cot_ref, gain_ref, mixed_ref, query_ref, kv_ref, lse_ref,
+        sums_ref, full_o_hbm, routed_grad_ref, middle_ref, cot_ref, gain_ref, mixed_ref, query_ref, kv_ref, lse_ref,
         starts_ref, cos_ref, sin_ref,
         total_ref, grad_mid_ref, grad_pre_ref, gain_row_ref, w_out_ref,
-        sums_own, sums_land, own, core_in, first_in, second_in, routed_grad, attn_low, mixed_grad, part_o, o_core,
+        sums_own, sums_land, full_o_ref, attn_low, mixed_grad, part_o, o_core,
         o_first, o_second, bias, key_t, kv_grad, kv_part, kv_land, kv_out, here, send, recv,
     ):
         wires = Wires(send, recv)
         dp, z = wires.dp, wires.z
-        loads = [pltpu.make_async_copy(sums_ref.at[pl.ds(0, chunks * CHUNK)], sums_own, here.at[0])]
-        for slot in range(4):
-            row = pl.multiple_of(masked(dp, 2 * slot) * tok_rows, 16)
-            loads.append(
-                pltpu.make_async_copy(
-                    sent_ref.at[pl.ds(row, tok_rows)],
-                    own.at[pl.ds(slot * tok_rows, tok_rows)],
-                    here.at[1 + slot],
-                )
-            )
+        loads = [
+            pltpu.make_async_copy(sums_ref.at[pl.ds(skipped * CHUNK, chunks * CHUNK)], sums_own, here.at[0]),
+            pltpu.make_async_copy(full_o_hbm, full_o_ref, here.at[1]),
+        ]
         for one in loads:
             one.start()
         greet(wires, (1, 2, 4), True)
         summed = LineSum(wires, sums_own, total_ref, sums_land, CHUNK, chunks)
-        plane = PlaneReduce(
-            wires, sent_ref, tok_rows, own, lambda slot: slot * tok_rows, core_in, first_in, second_in,
-            routed_grad,
-        )
         dense = PlaneReduce(
             wires, part_o, group, part_o, lambda slot: pl.multiple_of(masked(dp, 2 * slot) * group, 16),
             o_core, o_first, o_second, w_out_ref,
         )
-        line = LineReduce(wires, kv_part, tok_rows, kv_land)
-        plane.step(0)
+        line = LineReduce(wires, kv_part, tok_rows, kv_land, ways=(-1,))
         loads[0].wait()
         summed.begin()
         key_place = lax.broadcasted_iota(jnp.int32, (keys, tok_rows), 0)
@@ -1141,17 +1219,6 @@
         bias[...] = jnp.where(allowed, 0.0, masked_score)
         key_t[...] = kv_ref[:, : kv_width // 2].astype(jnp.float32).T.astype(jnp.bfloat16)
         kv_grad[...] = jnp.zeros_like(kv_grad)
-        for one in loads[1:]:
-            one.wait()
-        plane.step(1)
-        plane.step(2)
-        summed.tick()
-        summed.tick()
-        plane.step(3)
-        summed.tick()
-        plane.step(4)
-        summed.tick()
-        plane.step(5)
 
         tile = 32
         gain_row_ref[...] = jnp.zeros_like(gain_row_ref)
@@ -1159,12 +1226,14 @@
         @pl.loop(0, tok_rows // tile)
         def _(step):
             cut = pl.ds(pl.multiple_of(step * tile, tile), tile)
-            to_middle, terms = norm_back(middle_ref[cut, :], gain_ref[1:2, :], routed_grad[cut, :])
+            to_middle, terms = norm_back(middle_ref[cut, :], gain_ref[1:2, :], routed_grad_ref[cut, :])
             to_middle = cot_ref[cut, :].astype(jnp.float32) + to_middle
             grad_mid_ref[cut, :] = to_middle
             attn_low[cut, :] = to_middle.astype(jnp.bfloat16)
             gain_row_ref[0:1, :] += jnp.sum(terms, axis=0, keepdims=True)
 
+        summed.tick()
+        loads[1].wait()
         wide = 512
 
         @pl.loop(0, width // wide)
@@ -1204,27 +1273,28 @@
                 )
 
         heads(0, 3)
+        summed.tick()
         dense.step(1)
         dense.step(2)
-        summed.tick()
         heads(3, 6)
-        dense.step(3)
         summed.tick()
         heads(6, 9)
-        dense.step(4)
         summed.tick()
         heads(9, 12)
         kv_part[...] = kv_grad[...].astype(jnp.bfloat16)
-        line.start(0)
+        line.begin()
+        summed.tick()
+        dense.step(3)
+        summed.tick()
+        line.event(0)
+        summed.tick()
+        dense.step(4)
+        line.event(1)
+        line.event(2)
+        line.event(3)
+        line.event(4)
         dense.step(5)
-        summed.tick()
-        line.add(0)
-        line.start(1)
-        summed.tick()
-        line.add(1)
-        line.start(2)
-        summed.tick()
-        line.add(2)
+        line.event(5)
         line.finish((kv_out,))
         q_width = HEADS * HD
         for pair in range(KVH):
@@ -1250,11 +1320,7 @@
         scratch_shapes=[
             pltpu.VMEM((chunks * CHUNK, sums_in.shape[1]), low),
             pltpu.VMEM((chunks * CHUNK, sums_in.shape[1]), low),
-            pltpu.VMEM((4 * tok_rows, width), low),
-        ]
-        + PlaneReduce.scratch(tok_rows, width)
-        + [
-            pltpu.VMEM((tok_rows, width), f32),
+            pltpu.VMEM((w_rows, width), low),
             pltpu.VMEM((tok_rows, width), low),
             pltpu.VMEM((tok_rows, width), low),
             pltpu.VMEM((w_rows, width), low),
@@ -1265,15 +1331,15 @@
             pltpu.VMEM((kv_width // 2, keys), low),
             pltpu.VMEM((keys, kv_width), f32),
             pltpu.VMEM((keys, kv_width), low),
-            LineReduce.scratch(tok_rows, kv_width),
+            LineReduce.scratch(tok_rows, kv_width, 1),
             pltpu.VMEM((tok_rows, kv_width), f32),
-            pltpu.SemaphoreType.DMA((5,)),
+            pltpu.SemaphoreType.DMA((2,)),
         ]
-        + sems(3 * chunks + 2 * PlaneReduce.COPIES + LineReduce.COPIES),
+        + sems(3 * chunks + PlaneReduce.COPIES + LineReduce.COPIES),
         compiler_params=kernel_params(3, 63),
         name="back_attention",
     )(
-        sums_in, grad_sent, full_o, middle, cotangent, gain_moe, mixed, query, all_kv, lse, starts, cosine, sine
+        sums_in, full_o, routed_grad, middle, cotangent, gain_moe, mixed, query, all_kv, lse, starts, cosine, sine
     )
 
 
@@ -1284,7 +1350,8 @@
     pre_width = in_width - LANES
     w_rows = width
     group, rows = w_rows // 8, w_rows // (8 * LINE)
-    chunks = sums_in.shape[0] // CHUNK - SPLIT
+    skipped = WITH_EXPERTS + WITH_ATTENTION
+    chunks = sums_in.shape[0] // CHUNK - skipped
 
     def kernel(
         sums_ref, prod_ref, full_q_ref, full_kv_ref, normed_ref, pre_ref, tok_ref, gain_ref, mid_grad_ref, gain_row_ref, o_part_ref,
@@ -1297,7 +1364,7 @@
         dp, z = wires.dp, wires.z
         loads = [
             pltpu.make_async_copy(
-                sums_ref.at[pl.ds(SPLIT * CHUNK, chunks * CHUNK)], sums_own, here.at[0]
+                sums_ref.at[pl.ds(skipped * CHUNK, chunks * CHUNK)], sums_own, here.at[0]
             )
         ]
         for slot in range(4):
@@ -1322,9 +1389,10 @@
         )
         o_line = LineReduce(wires, o_sums, rows, o_land)
         in_line = LineReduce(wires, in_sums, rows, in_land)
+        o_sums[...] = o_part_ref[...]
+        o_line.begin()
         loads[0].wait()
         summed.begin()
-        o_sums[...] = o_part_ref[...]
         wide = 512
 
         @pl.loop(0, width // wide)
@@ -1334,6 +1402,7 @@
                 pre_ref[:, q_width:], full_kv_ref[cut, : pre_width - q_width], 1, 1
             )
 
+        summed.tick()
         gain_rows[...] = jnp.zeros_like(gain_rows)
         gain_rows[1:2, :] = gain_row_ref[0:1, :]
         tile = 32
@@ -1347,6 +1416,8 @@
             tok_grad_ref[cut, :] = mid_grad_ref[cut, :] + to_tokens
             gain_rows[0:1, :] += jnp.sum(terms, axis=0, keepdims=True)
 
+        summed.tick()
+        o_line.event(0)
         part[:, pre_width:] = gain_rows[...].T.astype(jnp.bfloat16)
 
         @pl.loop(0, w_rows // 256)
@@ -1355,40 +1426,42 @@
             part[cut, :pre_width] = dot(normed_ref[:, cut], pre_ref[...], 0, 0).astype(jnp.bfloat16)
 
         dense.step(0)
-        summed.tick()
+        o_line.event(1)
+        o_line.event(2)
+        summed.tick(2)
         dense.step(1)
+        o_line.event(3)
+        summed.tick()
         dense.step(2)
-        summed.tick()
+        o_line.event(4)
+        summed.tick()
+        o_line.event(5)
         for one in loads[1:]:
             one.wait()
+        plane.step(0)
+        summed.tick(2)
+        plane.step(1)
         summed.tick()
         dense.step(3)
-        plane.step(0)
-        summed.tick()
+        plane.step(2)
+        summed.tick(2)
         dense.step(4)
-        o_line.start(0)
-        summed.tick()
         dense.step(5)
-        in_line.start(0)
-        plane.step(1)
-        plane.step(2)
-        o_line.add(0)
-        o_line.start(1)
-        summed.tick()
-        in_line.add(0)
-        in_line.start(1)
+        in_line.begin()
+        summed.tick()
+        in_line.event(0)
+        summed.tick()
         plane.step(3)
-        summed.tick()
-        o_line.add(1)
-        o_line.start(2)
-        summed.tick()
-        in_line.add(1)
-        in_line.start(2)
+        in_line.event(1)
+        in_line.event(2)
+        summed.tick(2)
+        in_line.event(3)
+        in_line.event(4)
         plane.step(4)
-        summed.tick()
-        o_line.add(2)
-        in_line.add(2)
+        summed.tick(2)
+        in_line.event(5)
         plane.step(5)
+        summed.tick(2)
 
         @pl.loop(0, tok_rows // tile)
         def _(step):
@@ -1482,14 +1555,14 @@
     ) = front(
         w_query, w_key, w_value, gains, w_out, cotangent, gates, tokens, starts, cosine, sine
     )
-    partial_sums, grad_sent, produced = experts(
+    partial_sums, produced, sums_first, routed_grad = experts(
         routed_low, all_cot, all_gate, w_gate[0], w_up[0], w_down[0]
     )
     half = w_gate.shape[2]
-    sums_head, grad_mid, grad_pre, gain_row, w_out_part = back_attention(
+    sums_second, grad_mid, grad_pre, gain_row, w_out_part = back_attention(
         partial_sums,
-        grad_sent,
         full_o,
+        routed_grad,
         middle,
         cotangent,
         gain_rows,
@@ -1515,10 +1588,12 @@
         w_out_part,
         middle,
     )
-    in_tail = D - sums_head.shape[0]
+    in_tail = D - sums_first.shape[0] - sums_second.shape[0]
 
     def whole(columns):
-        return jnp.concatenate([sums_head[:, columns], sums_tail[:in_tail, columns]], axis=0)
+        return jnp.concatenate(
+            [sums_first[:, columns], sums_second[:, columns], sums_tail[:in_tail, columns]], axis=0
+        )
 
     return (
         layer_out,

time: 482 us -> 430 us (0.89)
  Pallas kernels: 453 us -> 401 us
    pallas_call x1, Pallas kernels: 125 us -> 61.9 us  [back_attention(): pl.pallas_call(kernel, out_shape=(jax.ShapeDtypeStruct((chunks * CHUNK, s...]
    pallas_call x1, Pallas kernels: 79.6 us -> 99.9 us  [experts(): pl.pallas_call(kernel, out_shape=(jax.ShapeDtypeStruct((sum_rows, width),...]
    pallas_call x1, Pallas kernels: 106 us -> 101 us  [front(): pl.pallas_call(kernel, out_shape=(jax.ShapeDtypeStruct((w_rows, width), l...]
where the time goes in v4:
time: 430 us; the launch traced here: 425 us
  Pallas kernels  401 us (93%)
  other arithmetic  12.9 us (3%)
  local copies, waits for them, and re-layouts  10.6 us (2%)
    pallas_call x1, Pallas kernels, back_dense(): pl.pallas_call(kernel, out_shape=(jax.ShapeDtypeStruct((chunks * CHUNK, s...  138 us
    pallas_call x1, Pallas kernels, front(): pl.pallas_call(kernel, out_shape=(jax.ShapeDtypeStruct((w_rows, width), l...  101 us
    pallas_call x1, Pallas kernels, experts(): pl.pallas_call(kernel, out_shape=(jax.ShapeDtypeStruct((sum_rows, width),...  99.9 us
    pallas_call x1, Pallas kernels, back_attention(): pl.pallas_call(kernel, out_shape=(jax.ShapeDtypeStruct((chunks * CHUNK, s...  61.9 us

profile of v4, /device:TPU:0, one launch (start us, length us, event | category | flops | bytes accessed | tf_op | source)
XLA Modules:
  0.0 425.3 jit_solution(8583546341024431424)
XLA Ops:
  0.6 0.7 pad_maximum_fusion.2
  1.3 0.8 reduce-window.8
  2.2 0.7 select_reduce_fusion.1
  3.0 0.6 broadcast_in_dim.52.starts_ref
  3.6 1.3 select_reduce_fusion.gate_ref
  5.0 0.6 pad.4.gains_ref
  5.6 0.5 fusion
  6.2 0.8 pad_maximum_fusion
  7.0 100.8 %front.1 = (bf16[1536,1536]{1,0:T(8,128)(2,1)}, bf16[1536,640]{1,0:T(8,128)(2,1)}, bf16[1536,1536]{1,0:T(8,128)(2,1)}, bf16[2048,1536]{1,0:T(8,128)(2,1)}, f32[6...) custom-call(bf16[48,1536]{1,0:T(8,128)(2,1)} %wq_ref.1, ...), custom_call_target="tpu_custom_call" | custom-call | tf_op jit(solution)/shard_map/front/pallas_call | solution.py:852
  107.8 99.9 %experts.1 = (bf16[2304,1536]{1,0:T(8,128)(2,1)}, bf16[2048,1536]{1,0:T(8,128)(2,1)}, bf16[576,1536]{1,0:T(8,128)(2,1)}, f32[256,1536]{1,0:T(8,128)}) custom-call(bf16[256,1536]{1,0:T(8,128)(2,1)} %get-tuple-element.41.routed_ref, bf16[2048,1536]{1,0:T(8,128)(2,1)} %get-tuple-element.42.cot_ref, f32[64,256]{1,0:T(8,128)} %get-tuple-element.43.gate_ref, ...), custom_call_target="tpu_custom_call" | custom-call | tf_op jit(solution)/shard_map/experts/pallas_call | solution.py:1040
  207.7 61.9 %back_attention.1 = (bf16[448,1536]{1,0:T(8,128)(2,1)}, f32[256,1536]{1,0:T(8,128)}, bf16[256,2048]{1,0:T(8,128)(2,1)}, f32[8,1536]{1,0:T(8,128)}, bf16[192,1536]{1,0:T(8,128)(2,1)}) custom-call(bf16[2304,1536]{1,0:T(8,128)(2,1)} %get-tuple-element.44.sums_ref, bf16[1536,1536]{1,0:T(8,128)(2,1)} %get-tuple-element.49.full_o_hbm, ...), custom_call_target="tpu_custom_call" | custom-call | tf_op jit(solution)/shard_map/back_attention/pallas_call | solution.py:1309
  269.6 138.0 %back_dense.1 = (bf16[1280,1536]{1,0:T(8,128)(2,1)}, bf16[256,1536]{1,0:T(8,128)(2,1)}, f32[256,1536]{1,0:T(8,128)}, f32[48,1536]{1,0:T(8,128)}, f32[48,256]{1,0...) custom-call(bf16[2304,1536]{1,0:T(8,128)(2,1)} %get-tuple-element.44.sums_ref, ...), custom_call_target="tpu_custom_call" | custom-call | tf_op jit(solution)/shard_map/back_dense/pallas_call | solution.py:1476
  407.6 1.6 slice_reduce_fusion
  409.2 1.4 slice_bitcast_fusion.4
  410.6 1.5 slice_bitcast_fusion.2
  412.1 2.8 bitcast_convert_fusion
  415.1 2.5 maximum_convert_fusion.1
  417.6 2.5 maximum_convert_fusion
  420.2 0.9 copy.43
  421.1 1.1 copy.44
  422.2 0.7 copy.45
  422.9 0.6 copy.46
  423.6 0.6 copy.47
  424.2 0.7 copy.48
  (21 shorter events, 0.3 us)
Async XLA Ops:
  407.6 4.5 %copy-start = (bf16[1280,1536]{1,0:T(8,128)(2,1)S(1)}, bf16[1280,1536]{1,0:T(8,128)(2,1)}, u32[]{:S(2)}) copy-start(bf16[1280,1536]{1,0:T(8,128)(2,1)} %get-tuple-element.70) | copy-start | bytes 11796484
  412.1 2.8 copy-start.1
  417.6 2.6 copy-start.3
  417.6 3.5 copy-start.2
  420.2 2.0 copy-start.5
  420.2 2.8 copy-start.7
  420.2 3.4 copy-start.6
  420.2 4.0 copy-start.4

commit v5 on v4

--- a/solution.py
+++ b/solution.py
@@ -712,42 +712,36 @@
             return wires.copy(part, part, first + mask - 1, dp=masked(dp, mask))
 
         line_kv.start(0)
-        line_q.start(0)
         plane_cot.start(0)
         for mask in range(1, planes):
             gate_copy(mask, dp).start()
+        line_kv.wait(0)
+        line_kv.start(1)
         key_place = lax.broadcasted_iota(jnp.int32, (keys, tok_rows), 0)
         query_place = lax.broadcasted_iota(jnp.int32, (keys, tok_rows), 1) + z * tok_rows
         allowed = (key_place >= starts_ref[0:1, :]) & (key_place <= query_place)
         bias[...] = jnp.where(allowed, 0.0, masked_score)
-        line_kv.wait(0)
-        line_kv.start(1)
+        line_kv.wait(1)
+        line_kv.start(2)
+        line_q.start(0)
+        line_kv.wait(2)
+        plane_kv.start(0)
+        plane_cot.wait(0)
         line_q.wait(0)
         line_q.start(1)
-        plane_cot.wait(0)
+        plane_kv.wait(0)
+        plane_kv.start(1)
         plane_cot.start(1, far=False)
-        line_kv.wait(1)
-        line_kv.start(2)
         line_q.wait(1)
         line_q.start(2)
-        line_kv.wait(2)
-        plane_kv.start(0)
-        line_q.wait(2)
-        plane_q.start(0)
         line_o.start(0)
-        plane_cot.wait(1)
-        plane_cot.start(2)
-        plane_kv.wait(0)
-        plane_kv.start(1)
-        plane_q.wait(0)
-        plane_q.start(1)
-        line_o.wait(0)
-        line_o.start(1)
         plane_kv.wait(1)
         plane_kv.start(2)
         plane_kv.wait(2)
         plane_kv.start(3)
         plane_kv.finish()
+        line_q.wait(2)
+        plane_q.start(0)
 
         gain_rows_ref[...] = full_kv[:, kv_width:].astype(jnp.float32).T[:8, :]
         tile = 32
@@ -766,16 +760,22 @@
             all_kv[own_keys, cut] = turned(pre[:, cut], cos_ref[...], sin_ref[...]).astype(jnp.bfloat16)
         all_kv[own_keys, key_width:] = pre[:, key_width:].astype(jnp.bfloat16)
         line_keys.start(0)
+        line_o.wait(0)
+        line_o.start(1)
+        plane_q.wait(0)
+        plane_q.start(1)
+        plane_cot.wait(1)
+        plane_cot.start(2)
+        line_keys.wait(0)
+        line_keys.start(1)
         line_o.wait(1)
         line_o.start(2)
-        line_keys.wait(0)
-        line_keys.start(1)
+        line_keys.wait(1)
+        line_keys.start(2)
         line_o.wait(2)
         plane_o.start(0)
         plane_q.wait(1)
         plane_q.start(2)
-        line_keys.wait(1)
-        line_keys.start(2)
         plane_q.wait(2)
         plane_q.start(3)
         plane_q.finish()
@@ -793,6 +793,9 @@
                     pre_q[:, one * HD : (one + 1) * HD], cos_ref[...], sin_ref[...]
                 ).astype(jnp.bfloat16)
 
+        plane_o.wait(0)
+        plane_o.start(1)
+        plane_cot.start_far()
         line_keys.wait(2)
         value_t[...] = all_kv[:, key_width:].astype(jnp.float32).T.astype(jnp.bfloat16)
         lse_ref[...] = jnp.zeros_like(lse_ref)
@@ -808,11 +811,7 @@
             probs = (expo * (1.0 / total)).astype(jnp.bfloat16)
             mixed_ref[:, own_cut] = dot(value_t[key_cut, :], probs, 1, 0).T.astype(jnp.bfloat16)
 
-        pl.loop(0, 2)(attend)
-        plane_o.wait(0)
-        plane_o.start(1)
-        plane_cot.start_far()
-        pl.loop(2, HEADS)(attend)
+        pl.loop(0, HEADS)(attend)
         plane_o.wait(1)
         plane_o.start(2)
         plane_o.wait(2)
@@ -884,48 +883,211 @@
     )(w_query, w_key, w_value, gains, w_out, cotangent, gates, tokens, starts, cosine, sine)
 
 
-def experts(routed, all_cot, all_gate, w_gate, w_up, w_down):
+CHUNK = 64
+AHEAD = 4
+CARRIED = 2
+RING = 4
+BEFORE_DENSE = 16
+
+
+class LineSum:
+    def __init__(self, wires, own, out, landing, rows, chunks, came=False, goes_on=False):
+        self.wires, self.own, self.out, self.landing = wires, own, out, landing
+        self.rows, self.chunks, self.came, self.goes_on = rows, chunks, came, goes_on
+        self.all = chunks + (CARRIED if goes_on else 0)
+        self.begun = CARRIED if came else 0
+        self.now = self.begun
+        self.first = wires.take(3 * self.all)
+        z = wires.z
+        self.inner = (z == 1) | (z == 2)
+        self.outer = (z == 0) | (z == 3)
+        self.end = 3 * (z - 1)
+        self.near = 1 + z // 3
+        self.peer = 3 - z
+
+    def _cut(self, ref, chunk):
+        return ref.at[pl.ds(pl.multiple_of(chunk * self.rows, 16), self.rows)]
+
+    def _in(self, chunk):
+        return self.wires.copy(
+            self._cut(self.own, chunk), self._cut(self.out, chunk), self.first + chunk, z=self.near
+        )
+
+    def _across(self, chunk):
+        number = self.first + self.all + chunk
+        return self.wires.copy(
+            self._cut(self.own, chunk), self._cut(self.landing, lax.rem(chunk, RING)), number, z=self.peer
+        )
+
+    def _back(self, chunk, ref=None):
+        number = self.first + 2 * self.all + chunk
+        return self.wires.copy(
+            self._cut(self.out if ref is None else ref, chunk), self._cut(self.out, chunk), number, z=self.end
+        )
+
+    def begin(self):
+        @pl.when(self.outer)
+        def _():
+            for chunk in range(self.begun, min(self.begun + AHEAD, self.all)):
+                self._in(chunk).start()
+
+        if self.came:
+
+            @pl.when(self.inner)
+            def _():
+                self._across(1).start()
+                self._back(0, self.own).start()
+                self.out[pl.ds(0, self.rows), :] = self.own[pl.ds(0, self.rows), :]
+
+    def tick(self, count=1):
+        for _ in range(count):
+            if self.now < self.all + (0 if self.goes_on else 1):
+                self._tick(self.now)
+            self.now += 1
+
+    def _tick(self, chunk):
+        if chunk < self.all:
+
+            @pl.when(self.outer)
+            def _():
+                self._in(chunk).wait_send()
+                if chunk + AHEAD < self.all:
+                    self._in(chunk + AHEAD).start()
+
+        @pl.when(self.inner)
+        def _():
+            if chunk < self.all:
+                row = chunk * self.rows
+                self._in(chunk).wait_recv()
+                add_rows(self.own, row, self.own, row, self.out, row, self.rows)
+                if chunk <= self.chunks:
+                    self._across(chunk).start()
+            if chunk >= 1:
+                row = (chunk - 1) * self.rows
+                landed = (chunk - 1) % RING * self.rows
+                self._across(chunk - 1).wait_recv()
+                if chunk - 1 < self.chunks:
+                    add_rows(self.out, row, self.own, row, self.landing, landed, self.rows)
+                    self._back(chunk - 1).start()
+                else:
+                    self._across(chunk - 1).wait_send()
+                    add_rows(self.own, row, self.own, row, self.landing, landed, self.rows)
+
+    def finish(self):
+        self.tick(max(0, self.all + (0 if self.goes_on else 1) - self.now))
+
+        @pl.when(self.outer)
+        def _():
+            @pl.loop(0, self.chunks)
+            def _(chunk):
+                self._back(chunk).wait_recv()
+
+        @pl.when(self.inner)
+        def _():
+            @pl.loop(1 if self.came else 0, self.chunks)
+            def _(chunk):
+                self._across(chunk).wait_send()
+
+            @pl.loop(0, self.chunks)
+            def _(chunk):
+                self._back(chunk).wait_send()
+
+
+def norm_back(values, gain, grad):
+    scale = lax.rsqrt(jnp.mean(values * values, axis=-1, keepdims=True) + epsilon)
+    normal = values * scale
+    inner = grad * gain
+    to_values = scale * (inner - normal * jnp.mean(inner * normal, axis=-1, keepdims=True))
+    return to_values, grad * normal
+
+
+def turned(values, cosine, sine):
+    return values * cosine + pltpu.roll(values, HD // 2, 1) * sine
+
+
+def experts_attention(
+    routed,
+    all_cot,
+    all_gate,
+    w_gate,
+    w_up,
+    w_down,
+    full_o,
+    middle,
+    cotangent,
+    gain_rows,
+    mixed,
+    query,
+    all_kv,
+    lse,
+    starts,
+    cosine,
+    sine,
+):
     tok_rows, width = routed.shape
     hidden_width = w_gate.shape[1]
+    keys, kv_width = all_kv.shape
     total_rows = 8 * tok_rows
-
     sum_rows = width + hidden_width
-    chunks = WITH_EXPERTS
+    group = width // 8
+    chunks = BEFORE_DENSE
+    score_scale = HD ** (-0.5)
+    per_group = HEADS // KVH
+    q_width = HEADS * HD
 
     def kernel(
-        routed_ref, cot_ref, gate_ref, wg_ref, wu_ref, wd_ref,
-        sums_ref, prod_ref, total_ref, routed_grad_ref,
-        w_in, w_down, x_all, y_all, hidden, grad_hidden, grad_in, sums, sums_land, gate_t, core_in, first_in,
-        second_in, here, there, send, recv,
+        routed_ref, all_cot_ref, gate_ref, wg_ref, wu_ref, wd_ref, full_o_hbm, middle_hbm, cot_hbm, gain_ref, mixed_hbm,
+        query_hbm, kv_hbm, lse_ref, starts_ref, cos_ref, sin_ref,
+        sums_ref, prod_ref, total_ref, grad_mid_hbm, grad_pre_ref, gain_row_ref, w_out_ref,
+        w_in, w_down, x_all, y_all, hidden, grad_hidden, grad_in, sums, sums_land, gate_t, core_in, first_in, second_in,
+        routed_grad, middle_ref, key_t, kv_land, here, there, freed, send, recv,
     ):
         wires = Wires(send, recv)
-        dp = wires.dp
-        own = pltpu.make_async_copy(routed_ref, x_all.at[rows_at(dp * tok_rows, tok_rows)], here.at[0])
+        dp, z = wires.dp, wires.z
+
+        def rows_begin(block):
+            return pl.multiple_of(block * tok_rows, 16)
+
+        def cut_of(block):
+            return pl.ds(rows_begin(block), tok_rows)
+
+        full_o_ref = w_in
+        part_o = y_all.at[pl.ds(0, width)]
+        query_ref, mixed_ref, cot_ref, attn_low, mixed_grad = [grad_in.at[pl.ds(i * tok_rows, tok_rows)] for i in range(5)]
+        kv_ref = hidden.at[pl.ds(0, keys), pl.ds(0, kv_width)]
+        kv_part = hidden.at[pl.ds(keys, keys), pl.ds(0, kv_width)]
+        kv_grad = grad_hidden.at[pl.ds(0, keys), pl.ds(0, kv_width)]
+        bias = grad_hidden.at[pl.ds(keys, keys), pl.ds(0, tok_rows)]
+        kv_out = grad_hidden.at[pl.ds(keys, tok_rows), pl.ds(tok_rows, kv_width)]
+
         loads = [
-            pltpu.make_async_copy(wd_ref, w_down, here.at[1]),
-            pltpu.make_async_copy(cot_ref, y_all, here.at[2]),
-            pltpu.make_async_copy(wg_ref, w_in.at[:, pl.ds(0, hidden_width)], here.at[3]),
-            pltpu.make_async_copy(wu_ref, w_in.at[:, pl.ds(hidden_width, hidden_width)], here.at[4]),
+            (routed_ref, x_all.at[cut_of(dp)]),
+            (wd_ref, w_down),
+            (all_cot_ref, y_all),
+            (wg_ref, w_in.at[:, pl.ds(0, hidden_width)]),
+            (wu_ref, w_in.at[:, pl.ds(hidden_width, hidden_width)]),
+            (middle_hbm, middle_ref),
         ]
-        own.start()
+        later = [(full_o_hbm, full_o_ref), (query_hbm, query_ref), (mixed_hbm, mixed_ref), (cot_hbm, cot_ref), (kv_hbm, kv_ref)]
+        loads = [pltpu.make_async_copy(a, b, here.at[i]) for i, (a, b) in enumerate(loads + later)]
+        loads, later = loads[: len(loads) - len(later)], loads[len(loads) - len(later) :]
         for one in loads:
             one.start()
         greet(wires, (1, 2, 4), True)
-        own.wait()
+        loads[0].wait()
         spread = PlaneGather(wires, x_all, tok_rows)
         plane = PlaneReduce(
-            wires, x_all, tok_rows, x_all, lambda slot: rows_begin(masked(dp, 2 * slot)), core_in, first_in, second_in,
-            routed_grad_ref,
+            wires, y_all, tok_rows, y_all, lambda slot: rows_begin(masked(dp, 2 * slot)), core_in, first_in, second_in,
+            routed_grad,
         )
-        summed = LineSum(wires, sums, total_ref, sums_land, CHUNK, chunks)
+        summed = LineSum(wires, sums, total_ref, sums_land, CHUNK, chunks, goes_on=True)
+        dense = PlaneReduce(
+            wires, part_o, group, part_o, lambda slot: pl.multiple_of(masked(dp, 2 * slot) * group, 16),
+            core_in, first_in, second_in, w_out_ref,
+        )
+        line = LineReduce(wires, kv_part, tok_rows, kv_land, ways=(-1,))
         spread.start(0)
         gate_t[...] = gate_ref[...].T
-
-        def rows_begin(block):
-            return pl.multiple_of(block * tok_rows, 16)
-
-        def cut_of(block):
-            return pl.ds(rows_begin(block), tok_rows)
 
         def gate_of(block):
             lane = lax.broadcasted_iota(jnp.int32, gate_t.shape, 1)
@@ -949,14 +1111,14 @@
             ).astype(jnp.bfloat16)
             grad_in[cut, hidden_width:] = (grad * silu).astype(jnp.bfloat16)
 
-        loads[0].wait()
         loads[1].wait()
+        loads[2].wait()
         pl.loop(0, 4)(back_hidden)
         spread.wait(0)
         spread.start(1)
         pl.loop(4, 8)(back_hidden)
-        loads[2].wait()
         loads[3].wait()
+        loads[4].wait()
         through(0)
         spread.wait_core(0)
         through(1)
@@ -973,35 +1135,29 @@
         through(6)
         spread.wait_core(3)
         through(7)
-        spread.finish()
+
+        def weights_down(step):
+            cut = rows_at(step * 256, 256)
+            sums[cut, :] = dot(hidden[:, cut], y_all[...], 0, 0).astype(jnp.bfloat16)
 
         def weights_in(step):
             cut = rows_at(step * 256, 256)
-            sums[cut, :] = dot(x_all[:, cut], grad_in[...], 0, 0).astype(jnp.bfloat16)
-
-        def weights_down(step):
-            cut = rows_at(step * 256, 256)
-            out = rows_at(width + step * 256, 256)
-            sums[out, :] = dot(hidden[:, cut], y_all[...], 0, 0).astype(jnp.bfloat16)
+            out = rows_at(hidden_width + step * 256, 256)
+            sums[out, :] = dot(x_all[:, cut], grad_in[...], 0, 0).astype(jnp.bfloat16)
 
         def save_sums(begin, end, number):
             rows = pl.ds(begin, end - begin)
             return pltpu.make_async_copy(sums.at[rows], sums_ref.at[rows], there.at[number])
 
-        pl.loop(0, 2)(weights_in)
+        pl.loop(0, 1)(weights_down)
         summed.begin()
-        pl.loop(2, 4)(weights_in)
-        pl.loop(4, 6)(weights_in)
-        summed.tick()
-        pl.loop(0, 3)(weights_down)
-        summed.tick()
-        save = save_sums(chunks * CHUNK, sum_rows, 0)
-        save.start()
+        pl.loop(1, 3)(weights_down)
+        spread.finish()
 
         def input_grads(side):
             for slot in (3, 2, 1, 0):
                 cut = cut_of(masked(dp, 2 * slot + side))
-                x_all[cut, :] = dot(grad_in[cut, :], w_in[...], 1, 1).astype(jnp.bfloat16)
+                y_all[cut, :] = dot(grad_in[cut, :], w_in[...], 1, 1).astype(jnp.bfloat16)
                 if side:
                     plane.start_core(slot)
 
@@ -1009,231 +1165,68 @@
         summed.tick()
         input_grads(0)
         summed.tick()
+        later[0].start()
         plane.step(1)
         plane.step(2)
         summed.tick()
+        pl.loop(0, 2)(weights_in)
+        summed.tick()
+        pl.loop(2, 4)(weights_in)
+        summed.tick()
+        plane.step(3)
+        pl.loop(4, 6)(weights_in)
+        summed.tick()
+        for one in later[1:4]:
+            one.start()
+        saved = (chunks + CARRIED) * CHUNK
+        save = save_sums(saved, sum_rows, 0)
+        save.start()
 
         def save_made(block):
             return pltpu.make_async_copy(
-                y_all.at[cut_of(block)], prod_ref.at[cut_of(block)], there.at[1 + block]
+                x_all.at[cut_of(block)], prod_ref.at[cut_of(block)], there.at[3 + block]
             )
 
         def make(block):
             made = dot(hidden[cut_of(block), :], w_down[...], 1, 0).astype(jnp.bfloat16).astype(jnp.float32)
-            y_all[cut_of(block), :] = (made * gate_of(block)).astype(jnp.bfloat16)
+            x_all[cut_of(block), :] = (made * gate_of(block)).astype(jnp.bfloat16)
             save_made(block).start()
 
         pl.loop(0, 4)(make)
         summed.tick()
         pl.loop(4, 8)(make)
-        plane.step(3)
-        summed.tick(2)
+        later[4].start()
         plane.step(4)
-        summed.tick(2)
-        plane.step(5)
-        summed.finish()
-        for block in range(8):
-            save_made(block).wait()
-        save.wait()
-
-    f32, low = jnp.float32, jnp.bfloat16
-    return pl.pallas_call(
-        kernel,
-        out_shape=(
-            jax.ShapeDtypeStruct((sum_rows, width), low),
-            jax.ShapeDtypeStruct((total_rows, width), low),
-            jax.ShapeDtypeStruct((chunks * CHUNK, width), low),
-            jax.ShapeDtypeStruct((tok_rows, width), f32),
-        ),
-        in_specs=[VMEM, ANY, VMEM, ANY, ANY, ANY],
-        out_specs=(ANY, ANY, VMEM, VMEM),
-        scratch_shapes=[
-            pltpu.VMEM((width, 2 * hidden_width), low),
-            pltpu.VMEM((hidden_width, width), low),
-            pltpu.VMEM((total_rows, width), low),
-            pltpu.VMEM((total_rows, width), low),
-            pltpu.VMEM((total_rows, hidden_width), low),
-            pltpu.VMEM((total_rows, hidden_width), f32),
-            pltpu.VMEM((total_rows, 2 * hidden_width), low),
-            pltpu.VMEM((sum_rows, width), low),
-            pltpu.VMEM((chunks * CHUNK, width), low),
-            pltpu.VMEM((tok_rows, 64), f32),
-        ]
-        + PlaneReduce.scratch(tok_rows, width)
-        + [pltpu.SemaphoreType.DMA((5,)), pltpu.SemaphoreType.DMA((9,))]
-        + sems(PlaneGather.COPIES + PlaneReduce.COPIES + 3 * chunks),
-        compiler_params=kernel_params(1, 63),
-        name="experts",
-    )(routed, all_cot, all_gate, w_gate, w_up, w_down)
-
-
-CHUNK = 64
-AHEAD = 4
-WITH_EXPERTS = 9
-WITH_ATTENTION = 7
-
-
-class LineSum:
-    def __init__(self, wires, own, out, landing, rows, chunks):
-        self.wires, self.own, self.out, self.landing = wires, own, out, landing
-        self.rows, self.chunks, self.now = rows, chunks, 0
-        self.first = wires.take(3 * chunks)
-        z = wires.z
-        self.inner = (z == 1) | (z == 2)
-        self.outer = (z == 0) | (z == 3)
-        self.end = 3 * (z - 1)
-        self.near = 1 + z // 3
-        self.peer = 3 - z
-
-    def _cut(self, ref, chunk):
-        return ref.at[pl.ds(pl.multiple_of(chunk * self.rows, 16), self.rows)]
-
-    def _in(self, chunk):
-        return self.wires.copy(
-            self._cut(self.own, chunk), self._cut(self.out, chunk), self.first + chunk, z=self.near
-        )
-
-    def _across(self, chunk):
-        number = self.first + self.chunks + chunk
-        return self.wires.copy(
-            self._cut(self.own, chunk), self._cut(self.landing, chunk), number, z=self.peer
-        )
-
-    def _back(self, chunk):
-        number = self.first + 2 * self.chunks + chunk
-        return self.wires.copy(
-            self._cut(self.out, chunk), self._cut(self.out, chunk), number, z=self.end
-        )
-
-    def begin(self):
-        @pl.when(self.outer)
-        def _():
-            for chunk in range(min(AHEAD, self.chunks)):
-                self._in(chunk).start()
-
-    def tick(self, count=1):
-        for _ in range(count):
-            if self.now <= self.chunks:
-                self._tick(self.now)
-            self.now += 1
-
-    def _tick(self, chunk):
-        if chunk < self.chunks:
-
-            @pl.when(self.outer)
-            def _():
-                self._in(chunk).wait_send()
-                if chunk + AHEAD < self.chunks:
-                    self._in(chunk + AHEAD).start()
-
-        @pl.when(self.inner)
-        def _():
-            if chunk < self.chunks:
-                row = chunk * self.rows
-                self._in(chunk).wait_recv()
-                add_rows(self.own, row, self.own, row, self.out, row, self.rows)
-                self._across(chunk).start()
-            if chunk >= 1:
-                row = (chunk - 1) * self.rows
-                self._across(chunk - 1).wait_recv()
-                add_rows(self.out, row, self.own, row, self.landing, row, self.rows)
-                self._back(chunk - 1).start()
-
-    def finish(self):
-        self.tick(max(0, self.chunks + 1 - self.now))
-
-        @pl.when(self.outer)
-        def _():
-            @pl.loop(0, self.chunks)
-            def _(chunk):
-                self._back(chunk).wait_recv()
-
-        @pl.when(self.inner)
-        def _():
-            @pl.loop(0, self.chunks)
-            def _(chunk):
-                self._across(chunk).wait_send()
-                self._back(chunk).wait_send()
-
-
-def norm_back(values, gain, grad):
-    scale = lax.rsqrt(jnp.mean(values * values, axis=-1, keepdims=True) + epsilon)
-    normal = values * scale
-    inner = grad * gain
-    to_values = scale * (inner - normal * jnp.mean(inner * normal, axis=-1, keepdims=True))
-    return to_values, grad * normal
-
-
-def turned(values, cosine, sine):
-    return values * cosine + pltpu.roll(values, HD // 2, 1) * sine
-
-
-def back_attention(
-    sums_in,
-    full_o,
-    routed_grad,
-    middle,
-    cotangent,
-    gain_moe,
-    mixed,
-    query,
-    all_kv,
-    lse,
-    starts,
-    cosine,
-    sine,
-):
-    tok_rows, width = middle.shape
-    keys, kv_width = all_kv.shape
-    w_rows = width
-    group = w_rows // 8
-    skipped, chunks = WITH_EXPERTS, WITH_ATTENTION
-
-    def kernel(
-        sums_ref, full_o_hbm, routed_grad_ref, middle_ref, cot_ref, gain_ref, mixed_ref, query_ref, kv_ref, lse_ref,
-        starts_ref, cos_ref, sin_ref,
-        total_ref, grad_mid_ref, grad_pre_ref, gain_row_ref, w_out_ref,
-        sums_own, sums_land, full_o_ref, attn_low, mixed_grad, part_o, o_core,
-        o_first, o_second, bias, key_t, kv_grad, kv_part, kv_land, kv_out, here, send, recv,
-    ):
-        wires = Wires(send, recv)
-        dp, z = wires.dp, wires.z
-        loads = [
-            pltpu.make_async_copy(sums_ref.at[pl.ds(skipped * CHUNK, chunks * CHUNK)], sums_own, here.at[0]),
-            pltpu.make_async_copy(full_o_hbm, full_o_ref, here.at[1]),
-        ]
-        for one in loads:
-            one.start()
-        greet(wires, (1, 2, 4), True)
-        summed = LineSum(wires, sums_own, total_ref, sums_land, CHUNK, chunks)
-        dense = PlaneReduce(
-            wires, part_o, group, part_o, lambda slot: pl.multiple_of(masked(dp, 2 * slot) * group, 16),
-            o_core, o_first, o_second, w_out_ref,
-        )
-        line = LineReduce(wires, kv_part, tok_rows, kv_land, ways=(-1,))
-        loads[0].wait()
-        summed.begin()
+        summed.tick()
         key_place = lax.broadcasted_iota(jnp.int32, (keys, tok_rows), 0)
         query_place = lax.broadcasted_iota(jnp.int32, (keys, tok_rows), 1) + z * tok_rows
         allowed = (key_place >= starts_ref[0:1, :]) & (key_place <= query_place)
         bias[...] = jnp.where(allowed, 0.0, masked_score)
+        kv_grad[...] = jnp.zeros_like(kv_grad)
+        gain_row_ref[...] = jnp.zeros_like(gain_row_ref)
+        loads[5].wait()
+        for one in later:
+            one.wait()
         key_t[...] = kv_ref[:, : kv_width // 2].astype(jnp.float32).T.astype(jnp.bfloat16)
-        kv_grad[...] = jnp.zeros_like(kv_grad)
+        summed.tick()
+        plane.step(5)
+        for mask in (1, 2, 4):
+            pl.semaphore_signal(freed, inc=1, device_id=(masked(dp, mask), z), device_id_type=MESH)
 
         tile = 32
-        gain_row_ref[...] = jnp.zeros_like(gain_row_ref)
 
         @pl.loop(0, tok_rows // tile)
         def _(step):
             cut = pl.ds(pl.multiple_of(step * tile, tile), tile)
-            to_middle, terms = norm_back(middle_ref[cut, :], gain_ref[1:2, :], routed_grad_ref[cut, :])
+            to_middle, terms = norm_back(middle_ref[cut, :], gain_ref[1:2, :], routed_grad[cut, :])
             to_middle = cot_ref[cut, :].astype(jnp.float32) + to_middle
-            grad_mid_ref[cut, :] = to_middle
+            middle_ref[cut, :] = to_middle
             attn_low[cut, :] = to_middle.astype(jnp.bfloat16)
             gain_row_ref[0:1, :] += jnp.sum(terms, axis=0, keepdims=True)
 
-        summed.tick()
-        loads[1].wait()
+        save_mid = pltpu.make_async_copy(middle_ref, grad_mid_hbm, there.at[1])
+        save_mid.start()
+        summed.tick()
         wide = 512
 
         @pl.loop(0, width // wide)
@@ -1246,10 +1239,9 @@
             cut = pl.ds(pl.multiple_of(step * 256, 256), 256)
             part_o[cut, :] = dot(mixed_ref[:, cut], attn_low[...], 0, 0).astype(jnp.bfloat16)
 
+        pl.semaphore_wait(freed, 3)
         dense.step(0)
         summed.tick()
-        score_scale = HD ** (-0.5)
-        per_group = HEADS // KVH
 
         def heads(first, last):
             @pl.loop(first, last)
@@ -1291,12 +1283,15 @@
         dense.step(4)
         line.event(1)
         line.event(2)
+        summed.tick()
         line.event(3)
         line.event(4)
         dense.step(5)
+        summed.tick(max(0, summed.all - summed.now))
+        save_last = save_sums(chunks * CHUNK, saved, 2)
+        save_last.start()
         line.event(5)
         line.finish((kv_out,))
-        q_width = HEADS * HD
         for pair in range(KVH):
             cut = slice(pair * HD, (pair + 1) * HD)
             grad_pre_ref[:, q_width + pair * HD : q_width + (pair + 1) * HD] = turned(
@@ -1304,42 +1299,55 @@
             ).astype(jnp.bfloat16)
         grad_pre_ref[:, q_width + kv_width // 2 :] = kv_out[:, kv_width // 2 :].astype(jnp.bfloat16)
         summed.finish()
+        for block in range(8):
+            save_made(block).wait()
+        for one in (save, save_mid, save_last):
+            one.wait()
 
     f32, low = jnp.float32, jnp.bfloat16
     return pl.pallas_call(
         kernel,
         out_shape=(
-            jax.ShapeDtypeStruct((chunks * CHUNK, sums_in.shape[1]), low),
+            jax.ShapeDtypeStruct((sum_rows, width), low),
+            jax.ShapeDtypeStruct((total_rows, width), low),
+            jax.ShapeDtypeStruct(((chunks + CARRIED) * CHUNK, width), low),
             jax.ShapeDtypeStruct((tok_rows, width), f32),
             jax.ShapeDtypeStruct((tok_rows, width + kv_width), low),
             jax.ShapeDtypeStruct((8, width), f32),
             jax.ShapeDtypeStruct((group, width), low),
         ),
-        in_specs=[ANY, ANY] + [VMEM] * 11,
-        out_specs=(VMEM,) * 5,
+        in_specs=[ANY, ANY, VMEM] + [ANY] * 6 + [VMEM] + [ANY] * 3 + [VMEM] * 4,
+        out_specs=(ANY, ANY, VMEM, ANY, VMEM, VMEM, VMEM),
         scratch_shapes=[
-            pltpu.VMEM((chunks * CHUNK, sums_in.shape[1]), low),
-            pltpu.VMEM((chunks * CHUNK, sums_in.shape[1]), low),
-            pltpu.VMEM((w_rows, width), low),
-            pltpu.VMEM((tok_rows, width), low),
-            pltpu.VMEM((tok_rows, width), low),
-            pltpu.VMEM((w_rows, width), low),
+            pltpu.VMEM((width, 2 * hidden_width), low),
+            pltpu.VMEM((hidden_width, width), low),
+            pltpu.VMEM((total_rows, width), low),
+            pltpu.VMEM((total_rows, width), low),
+            pltpu.VMEM((total_rows, hidden_width), low),
+            pltpu.VMEM((total_rows, hidden_width), f32),
+            pltpu.VMEM((total_rows, 2 * hidden_width), low),
+            pltpu.VMEM((sum_rows, width), low),
+            pltpu.VMEM((RING * CHUNK, width), low),
+            pltpu.VMEM((tok_rows, 64), f32),
         ]
-        + PlaneReduce.scratch(group, width)
+        + PlaneReduce.scratch(tok_rows, width)
         + [
-            pltpu.VMEM((keys, tok_rows), f32),
+            pltpu.VMEM((tok_rows, width), f32),
+            pltpu.VMEM((tok_rows, width), f32),
             pltpu.VMEM((kv_width // 2, keys), low),
-            pltpu.VMEM((keys, kv_width), f32),
-            pltpu.VMEM((keys, kv_width), low),
             LineReduce.scratch(tok_rows, kv_width, 1),
-            pltpu.VMEM((tok_rows, kv_width), f32),
-            pltpu.SemaphoreType.DMA((2,)),
+            pltpu.SemaphoreType.DMA((11,)),
+            pltpu.SemaphoreType.DMA((11,)),
+            pltpu.SemaphoreType.REGULAR,
         ]
-        + sems(3 * chunks + PlaneReduce.COPIES + LineReduce.COPIES),
-        compiler_params=kernel_params(3, 63),
-        name="back_attention",
+        + sems(
+            PlaneGather.COPIES + 2 * PlaneReduce.COPIES + 3 * (chunks + CARRIED) + LineReduce.COPIES
+        ),
+        compiler_params=kernel_params(1, 63),
+        name="experts_attention",
     )(
-        sums_in, full_o, routed_grad, middle, cotangent, gain_moe, mixed, query, all_kv, lse, starts, cosine, sine
+        routed, all_cot, all_gate, w_gate, w_up, w_down, full_o, middle, cotangent, gain_rows, mixed, query, all_kv,
+        lse, starts, cosine, sine,
     )
 
 
@@ -1350,36 +1358,50 @@
     pre_width = in_width - LANES
     w_rows = width
     group, rows = w_rows // 8, w_rows // (8 * LINE)
-    skipped = WITH_EXPERTS + WITH_ATTENTION
+    skipped = BEFORE_DENSE
     chunks = sums_in.shape[0] // CHUNK - skipped
 
     def kernel(
-        sums_ref, prod_ref, full_q_ref, full_kv_ref, normed_ref, pre_ref, tok_ref, gain_ref, mid_grad_ref, gain_row_ref, o_part_ref,
-        middle_ref,
+        sums_ref, prod_ref, full_q_hbm, full_kv_hbm, normed_hbm, pre_hbm, tok_hbm, gain_ref, mid_grad_hbm,
+        gain_row_ref, o_part_hbm, middle_hbm,
         total_ref, layer_ref, tok_grad_ref, wq_ref, wk_ref, wv_ref, gains_ref, out_ref,
-        sums_own, sums_land, own, core_in, first_in, second_in, moe, part, d_core, d_first, d_second, in_sums,
+        sums_own, sums_land, full_q_ref, full_kv_ref, normed_ref, pre_ref, tok_ref, mid_grad_ref, middle_ref, own, core_in, first_in, second_in, moe, part, d_core, d_first, d_second, in_sums,
         in_land, o_sums, o_land, normed_grad, gain_rows, here, send, recv,
     ):
         wires = Wires(send, recv)
         dp, z = wires.dp, wires.z
+        early = (CARRIED + AHEAD) * CHUNK
+        begin = skipped * CHUNK
         loads = [
+            pltpu.make_async_copy(sums_ref.at[pl.ds(begin, early)], sums_own.at[pl.ds(0, early)], here.at[0]),
             pltpu.make_async_copy(
-                sums_ref.at[pl.ds(skipped * CHUNK, chunks * CHUNK)], sums_own, here.at[0]
-            )
+                sums_ref.at[pl.ds(begin + early, chunks * CHUNK - early)],
+                sums_own.at[pl.ds(early, chunks * CHUNK - early)],
+                here.at[1],
+            ),
+            pltpu.make_async_copy(o_part_hbm, o_sums, here.at[2]),
+            pltpu.make_async_copy(pre_hbm, pre_ref, here.at[3]),
+            pltpu.make_async_copy(full_q_hbm, full_q_ref, here.at[4]),
+            pltpu.make_async_copy(full_kv_hbm, full_kv_ref, here.at[5]),
+            pltpu.make_async_copy(tok_hbm, tok_ref, here.at[6]),
+            pltpu.make_async_copy(mid_grad_hbm, mid_grad_ref, here.at[7]),
+            pltpu.make_async_copy(normed_hbm, normed_ref, here.at[8]),
+            pltpu.make_async_copy(middle_hbm, middle_ref, here.at[9]),
         ]
+        first_loads = len(loads)
         for slot in range(4):
             row = pl.multiple_of(masked(dp, 2 * slot) * tok_rows, 16)
             loads.append(
                 pltpu.make_async_copy(
                     prod_ref.at[pl.ds(row, tok_rows)],
                     own.at[pl.ds(slot * tok_rows, tok_rows)],
-                    here.at[1 + slot],
+                    here.at[first_loads + slot],
                 )
             )
         for one in loads:
             one.start()
         greet(wires, (1, 2, 4), True)
-        summed = LineSum(wires, sums_own, total_ref, sums_land, CHUNK, chunks)
+        summed = LineSum(wires, sums_own, total_ref, sums_land, CHUNK, chunks, came=True)
         dense = PlaneReduce(
             wires, part, group, part, lambda slot: pl.multiple_of(masked(dp, 2 * slot) * group, 16),
             d_core, d_first, d_second, in_sums,
@@ -1389,10 +1411,13 @@
         )
         o_line = LineReduce(wires, o_sums, rows, o_land)
         in_line = LineReduce(wires, in_sums, rows, in_land)
-        o_sums[...] = o_part_ref[...]
-        o_line.begin()
         loads[0].wait()
         summed.begin()
+        loads[1].wait()
+        loads[2].wait()
+        o_line.begin()
+        for one in loads[3:first_loads]:
+            one.wait()
         wide = 512
 
         @pl.loop(0, width // wide)
@@ -1436,7 +1461,7 @@
         o_line.event(4)
         summed.tick()
         o_line.event(5)
-        for one in loads[1:]:
+        for one in loads[first_loads:]:
             one.wait()
         plane.step(0)
         summed.tick(2)
@@ -1485,11 +1510,18 @@
             jax.ShapeDtypeStruct((rows, LANES), f32),
             jax.ShapeDtypeStruct((rows, width), f32),
         ),
-        in_specs=[ANY, ANY] + [VMEM] * 10,
+        in_specs=[ANY] * 7 + [VMEM, ANY, VMEM, ANY, ANY],
         out_specs=(VMEM,) * 8,
         scratch_shapes=[
-            pltpu.VMEM((chunks * CHUNK, sums_in.shape[1]), low),
-            pltpu.VMEM((chunks * CHUNK, sums_in.shape[1]), low),
+            pltpu.VMEM((chunks * CHUNK, width), low),
+            pltpu.VMEM((RING * CHUNK, width), low),
+            pltpu.VMEM(full_q.shape, low),
+            pltpu.VMEM(full_kv.shape, low),
+            pltpu.VMEM((tok_rows, width), low),
+            pltpu.VMEM((tok_rows, pre_width), low),
+            pltpu.VMEM((tok_rows, width), low),
+            pltpu.VMEM((tok_rows, width), f32),
+            pltpu.VMEM((tok_rows, width), f32),
             pltpu.VMEM((4 * tok_rows, width), low),
         ]
         + PlaneReduce.scratch(tok_rows, width)
@@ -1502,7 +1534,7 @@
             LineReduce.scratch(rows, width),
             pltpu.VMEM((tok_rows, width), f32),
             pltpu.VMEM((LANES, width), f32),
-            pltpu.SemaphoreType.DMA((5,)),
+            pltpu.SemaphoreType.DMA((14,)),
         ]
         + sems(3 * chunks + 2 * PlaneReduce.COPIES + 2 * LineReduce.COPIES),
         compiler_params=kernel_params(4, 63),
@@ -1555,14 +1587,14 @@
     ) = front(
         w_query, w_key, w_value, gains, w_out, cotangent, gates, tokens, starts, cosine, sine
     )
-    partial_sums, produced, sums_first, routed_grad = experts(
-        routed_low, all_cot, all_gate, w_gate[0], w_up[0], w_down[0]
-    )
-    half = w_gate.shape[2]
-    sums_second, grad_mid, grad_pre, gain_row, w_out_part = back_attention(
-        partial_sums,
+    partial_sums, produced, sums_head, grad_mid, grad_pre, gain_row, w_out_part = experts_attention(
+        routed_low,
+        all_cot,
+        all_gate,
+        w_gate[0],
+        w_up[0],
+        w_down[0],
         full_o,
-        routed_grad,
         middle,
         cotangent,
         gain_rows,
@@ -1574,6 +1606,7 @@
         cosine,
         sine,
     )
+    half = w_gate.shape[2]
     sums_tail, layer_out, grad_tokens, sum_q, sum_k, sum_v, sum_gains, sum_o = back_dense(
         partial_sums,
         produced,
@@ -1588,12 +1621,10 @@
         w_out_part,
         middle,
     )
-    in_tail = D - sums_first.shape[0] - sums_second.shape[0]
+    head = BEFORE_DENSE * CHUNK
 
     def whole(columns):
-        return jnp.concatenate(
-            [sums_first[:, columns], sums_second[:, columns], sums_tail[:in_tail, columns]], axis=0
-        )
+        return jnp.concatenate([sums_head[half:head, columns], sums_tail[:, columns]], axis=0)
 
     return (
         layer_out,
@@ -1606,7 +1637,7 @@
         sum_gains[:, 1],
         whole(slice(0, half)).astype(jnp.float32)[None],
         whole(slice(half, 2 * half)).astype(jnp.float32)[None],
-        sums_tail[in_tail:].astype(jnp.float32)[None],
+        sums_head[:half].astype(jnp.float32)[None],
     )
 
 

time: 430 us -> 392 us (0.912)
  Pallas kernels: 401 us -> 363 us
    pallas_call x2 -> x1, Pallas kernels: 162 us -> 144 us  [experts_attention(): pl.pallas_call(kernel, out_shape=(jax.ShapeDtypeStruct((sum_rows, width),...]
    pallas_call x1, Pallas kernels: 138 us -> 125 us  [back_dense(): pl.pallas_call(kernel, out_shape=(jax.ShapeDtypeStruct((chunks * CHUNK, s...]
    pallas_call x1, Pallas kernels: 101 us -> 93.4 us  [front(): pl.pallas_call(kernel, out_shape=(jax.ShapeDtypeStruct((w_rows, width), l...]
where the time goes in v5:
time: 392 us; the launch traced here: 387 us
  Pallas kernels  363 us (93%)
  other arithmetic  14.8 us (4%)
  local copies, waits for them, and re-layouts  8.97 us (2%)
    pallas_call x1, Pallas kernels, experts_attention(): pl.pallas_call(kernel, out_shape=(jax.ShapeDtypeStruct((sum_rows, width),...  144 us
    pallas_call x1, Pallas kernels, back_dense(): pl.pallas_call(kernel, out_shape=(jax.ShapeDtypeStruct((chunks * CHUNK, s...  125 us
    pallas_call x1, Pallas kernels, front(): pl.pallas_call(kernel, out_shape=(jax.ShapeDtypeStruct((w_rows, width), l...  93.4 us

profile of v5, /device:TPU:0, one launch (start us, length us, event | category | flops | bytes accessed | tf_op | source)
XLA Modules:
  0.0 387.4 jit_solution(11504891857694649796)
XLA Ops:
  0.6 0.7 pad_maximum_fusion.2
  1.3 0.8 reduce-window.8
  2.2 0.7 select_reduce_fusion.1
  3.0 0.6 broadcast_in_dim.52.starts_ref
  3.6 1.3 select_reduce_fusion.gate_ref
  4.9 0.1 copy.36
  5.0 0.6 pad.4.gains_ref
  5.6 0.5 fusion
  6.2 0.8 pad_maximum_fusion
  7.0 93.4 %front.1 = (bf16[1536,1536]{1,0:T(8,128)(2,1)}, bf16[1536,640]{1,0:T(8,128)(2,1)}, bf16[1536,1536]{1,0:T(8,128)(2,1)}, bf16[2048,1536]{1,0:T(8,128)(2,1)}, f32[6...) custom-call(bf16[48,1536]{1,0:T(8,128)(2,1)} %wq_ref.1, ...), custom_call_target="tpu_custom_call" | custom-call | tf_op jit(solution)/shard_map/front/pallas_call | solution.py:851
  100.4 143.7 %experts_attention.1 = (bf16[2304,1536]{1,0:T(8,128)(2,1)}, bf16[2048,1536]{1,0:T(8,128)(2,1)}, bf16[1152,1536]{1,0:T(8,128)(2,1)}, f32[256,1536]{1,0:T(8,128)},...) custom-call(bf16[256,1536]{1,0:T(8,128)(2,1)} %get-tuple-element.39.routed_ref, ...), custom_call_target="tpu_custom_call" | custom-call | tf_op jit(solution)/shard_map/experts_attention/pallas_call | solution.py:1308
  244.2 125.4 %back_dense.1 = (bf16[1280,1536]{1,0:T(8,128)(2,1)}, bf16[256,1536]{1,0:T(8,128)(2,1)}, f32[256,1536]{1,0:T(8,128)}, f32[48,1536]{1,0:T(8,128)}, f32[48,256]{1,0...) custom-call(bf16[2304,1536]{1,0:T(8,128)(2,1)} %get-tuple-element.49.sums_ref, ...), custom_call_target="tpu_custom_call" | custom-call | tf_op jit(solution)/shard_map/back_dense/pallas_call | solution.py:1501
  369.5 1.5 slice_reduce_fusion
  371.1 1.2 slice_bitcast_fusion.2
  372.2 4.6 %bitcast_convert_fusion = f32[1,768,1536]{2,1,0:T(8,128)} fusion(bf16[1152,1536]{1,0:T(8,128)(2,1)} %get-tuple-element.65), kind=kLoop, calls=%fused_computation.2 | loop fusion | flops 1179648 | bytes 7077888 | tf_op jit(solution)/shard_map/broadcast_in_dim | solution.py:1640
  376.9 0.3 slice_bitcast_fusion
  377.1 2.5 maximum_convert_fusion.1
  379.7 2.5 maximum_convert_fusion
  382.3 0.9 copy.43
  383.1 1.1 copy.44
  384.3 0.7 copy.45
  385.0 0.6 copy.46
  385.6 0.6 copy.47
  386.3 0.7 copy.48
  (17 shorter events, 0.1 us)
Async XLA Ops:
  372.2 4.7 %copy-start = (bf16[1280,1536]{1,0:T(8,128)(2,1)S(1)}, bf16[1280,1536]{1,0:T(8,128)(2,1)}, u32[]{:S(2)}) copy-start(bf16[1280,1536]{1,0:T(8,128)(2,1)} %get-tuple-element.66) | copy-start | bytes 11796484
  379.7 2.6 copy-start.2
  379.7 3.5 copy-start.1
  382.2 2.0 copy-start.4
  382.2 2.8 copy-start.6
  382.2 3.4 copy-start.5
  382.3 4.0 %copy-start.3 = (f32[48,1536]{1,0:T(8,128)S(1)}, f32[48,1536]{1,0:T(8,128)}, u32[]{:S(2)}) copy-start(f32[48,1536]{1,0:T(8,128)} %get-tuple-element.97) | copy-start | bytes 884740

commit v6 on v5

--- a/solution.py
+++ b/solution.py
@@ -452,6 +452,9 @@
         if stage == 1 and far:
             self.start_far()
 
+    def start_one(self, number):
+        self._copy((self.CHIP[0] + self.CORE[0])[number], True).start()
+
     def start_far(self):
         for one in self.CHIP[2]:
             self._copy(one, True).start()
@@ -552,6 +555,9 @@
         elif number == 4:
             self._sum_far(2, 0, 0)
             self._sum_far(3, h, 2 * h)
+        elif self.out is None:
+            self._far(4).wait()
+            self._far(5).wait()
         else:
             self._far(4).wait()
             add_rows(self.out, 0, self.core_in, 0, self.second_in, 0, h)
@@ -638,7 +644,7 @@
 
     @staticmethod
     def scratch(rows, columns, ways=2):
-        return pltpu.VMEM((ways * LINE * rows, columns), jnp.bfloat16)
+        return pltpu.VMEM(((ways * LINE - 1) * rows, columns), jnp.bfloat16)
 
 
 def sems(count):
@@ -661,39 +667,205 @@
     return pl.ds(pl.multiple_of(begin, 16), size)
 
 
-def front(w_query, w_key, w_value, gains, w_out, cotangent, gates, tokens, starts, cosine, sine):
+CHUNK = 64
+AHEAD = 4
+CARRIED = 2
+RING = 4
+BEFORE_DENSE = 16
+
+
+class LineSum:
+    def __init__(self, wires, own, out, landing, rows, chunks, came=False, goes_on=False):
+        self.wires, self.own, self.out, self.landing = wires, own, out, landing
+        self.rows, self.chunks, self.came, self.goes_on = rows, chunks, came, goes_on
+        self.all = chunks + (CARRIED if goes_on else 0)
+        self.begun = CARRIED if came else 0
+        self.now = self.begun
+        self.first = wires.take(3 * self.all)
+        z = wires.z
+        self.inner = (z == 1) | (z == 2)
+        self.outer = (z == 0) | (z == 3)
+        self.end = 3 * (z - 1)
+        self.near = 1 + z // 3
+        self.peer = 3 - z
+
+    def _cut(self, ref, chunk):
+        return ref.at[pl.ds(pl.multiple_of(chunk * self.rows, 16), self.rows)]
+
+    def _in(self, chunk):
+        return self.wires.copy(
+            self._cut(self.own, chunk), self._cut(self.out, chunk), self.first + chunk, z=self.near
+        )
+
+    def _across(self, chunk):
+        number = self.first + self.all + chunk
+        return self.wires.copy(
+            self._cut(self.own, chunk), self._cut(self.landing, lax.rem(chunk, RING)), number, z=self.peer
+        )
+
+    def _back(self, chunk, ref=None):
+        number = self.first + 2 * self.all + chunk
+        return self.wires.copy(
+            self._cut(self.out if ref is None else ref, chunk), self._cut(self.out, chunk), number, z=self.end
+        )
+
+    def begin(self):
+        @pl.when(self.outer)
+        def _():
+            for chunk in range(self.begun, min(self.begun + AHEAD, self.all)):
+                self._in(chunk).start()
+
+        if self.came:
+
+            @pl.when(self.inner)
+            def _():
+                self._across(1).start()
+                self._back(0, self.own).start()
+                self.out[pl.ds(0, self.rows), :] = self.own[pl.ds(0, self.rows), :]
+
+    def tick(self, count=1):
+        for _ in range(count):
+            if self.now < self.all + (0 if self.goes_on else 1):
+                self._tick(self.now)
+            self.now += 1
+
+    def _tick(self, chunk):
+        if chunk < self.all:
+
+            @pl.when(self.outer)
+            def _():
+                self._in(chunk).wait_send()
+                if chunk + AHEAD < self.all:
+                    self._in(chunk + AHEAD).start()
+
+        @pl.when(self.inner)
+        def _():
+            if chunk < self.all:
+                row = chunk * self.rows
+                self._in(chunk).wait_recv()
+                add_rows(self.own, row, self.own, row, self.out, row, self.rows)
+                if chunk <= self.chunks:
+                    self._across(chunk).start()
+            if chunk >= 1:
+                row = (chunk - 1) * self.rows
+                landed = (chunk - 1) % RING * self.rows
+                self._across(chunk - 1).wait_recv()
+                if chunk - 1 < self.chunks:
+                    add_rows(self.out, row, self.own, row, self.landing, landed, self.rows)
+                    self._back(chunk - 1).start()
+                else:
+                    self._across(chunk - 1).wait_send()
+                    add_rows(self.own, row, self.own, row, self.landing, landed, self.rows)
+
+    def finish(self):
+        self.tick(max(0, self.all + (0 if self.goes_on else 1) - self.now))
+
+        @pl.when(self.outer)
+        def _():
+            @pl.loop(0, self.chunks)
+            def _(chunk):
+                self._back(chunk).wait_recv()
+
+        @pl.when(self.inner)
+        def _():
+            @pl.loop(1 if self.came else 0, self.chunks)
+            def _(chunk):
+                self._across(chunk).wait_send()
+
+            @pl.loop(0, self.chunks)
+            def _(chunk):
+                self._back(chunk).wait_send()
+
+
+def norm_back(values, gain, grad):
+    scale = lax.rsqrt(jnp.mean(values * values, axis=-1, keepdims=True) + epsilon)
+    normal = values * scale
+    inner = grad * gain
+    to_values = scale * (inner - normal * jnp.mean(inner * normal, axis=-1, keepdims=True))
+    return to_values, grad * normal
+
+
+def turned(values, cosine, sine):
+    return values * cosine + pltpu.roll(values, HD // 2, 1) * sine
+
+
+def up_to_attention_back(
+    w_query, w_key, w_value, gains, w_out, tokens, cotangent, gates, w_gate, w_up, w_down, starts, cosine, sine
+):
     rows, width = w_query.shape
-    kv_width = w_key.shape[1] + w_value.shape[1]
     key_width = w_key.shape[1]
+    kv_width = key_width + w_value.shape[1]
     tok_rows = tokens.shape[0]
     keys = LINE * tok_rows
     planes = 8
     group = LINE * rows
-    w_rows = planes * group
+    hidden_width = w_gate.shape[1]
+    total_rows = planes * tok_rows
+    sum_rows = width + hidden_width
+    chunks = BEFORE_DENSE
     score_scale = HD ** (-0.5)
     per_group = HEADS // KVH
+    q_width = HEADS * HD
 
     def kernel(
-        wq_ref, wk_ref, wv_ref, gains_ref, wo_ref, cot_ref, gate_ref, tok_ref, starts_ref, cos_ref, sin_ref,
-        out_q, out_kv, out_o, out_cot, all_gate, query_ref, all_kv, lse_ref, mixed_ref, middle_ref, normed_ref,
-        routed_ref, gain_rows_ref,
-        full_q, full_kv, full_o, all_cot, bias, value_t, here, there, send, recv,
+        wq_ref, wk_ref, wv_ref, gains_ref, wo_ref, tok_hbm, cot_hbm, gate_ref, wg_ref, wu_ref, wd_ref, starts_ref, cos_ref,
+        sin_ref,
+        out_q, out_kv, out_o, query_hbm, mixed_hbm, normed_hbm, middle_hbm, gain_rows_ref, sums_ref, prod_ref, total_ref,
+        grad_mid_hbm, grad_pre_ref, gain_row_ref, w_out_ref,
+        w_in, w_down, x_all, y_all, hidden, grad_hidden, grad_in, sums, sums_land, all_gate, gate_t, all_kv, lse_ref,
+        core_in, first_in, second_in, middle_ref, kv_land, here, there, freed, send, recv,
     ):
         wires = Wires(send, recv)
         dp, z = wires.dp, wires.z
+
+        def rows_begin(block):
+            return pl.multiple_of(block * tok_rows, 16)
+
+        def cut_of(block):
+            return pl.ds(rows_begin(block), tok_rows)
+
+        def gate_rows(block):
+            return pl.ds(pl.multiple_of(block * planes, planes), planes)
+
+        full_q = w_in
+        full_kv = hidden.at[pl.ds(0, width), pl.ds(0, kv_width + LANES)]
+        full_o = sums.at[pl.ds(0, width)]
+        all_cot = y_all
+        query_ref, mixed_ref, tok_ref, normed_ref, cot_ref = [
+            grad_in.at[pl.ds(i * tok_rows, tok_rows)] for i in range(5)
+        ]
+        value_t = key_t = grad_in.at[pl.ds(5 * tok_rows, kv_width // 2), pl.ds(0, keys)]
+        bias = grad_hidden.at[pl.ds(keys, keys), pl.ds(0, tok_rows)]
+        full_o_ref = w_in
+        part_o = y_all.at[pl.ds(0, width)]
+        attn_low, mixed_grad = tok_ref, normed_ref
+        kv_part = hidden.at[pl.ds(keys, keys), pl.ds(0, kv_width)]
+        kv_grad = grad_hidden.at[pl.ds(0, keys), pl.ds(0, kv_width)]
+        kv_out = grad_hidden.at[pl.ds(keys, tok_rows), pl.ds(tok_rows, kv_width)]
+
         own = rows_at((dp * LINE + z) * rows, rows)
-        locals_ = [
+        moves = [
             (wk_ref, full_kv.at[own, pl.ds(0, key_width)]),
             (wv_ref, full_kv.at[own, pl.ds(key_width, kv_width - key_width)]),
             (gains_ref, full_kv.at[own, pl.ds(kv_width, LANES)]),
+            (cot_hbm, all_cot.at[cut_of(dp)]),
+            (gate_ref, all_gate.at[gate_rows(dp)]),
             (wq_ref, full_q.at[own]),
             (wo_ref, full_o.at[own]),
-            (cot_ref, all_cot.at[rows_at(dp * tok_rows, tok_rows)]),
-            (gate_ref, all_gate.at[pl.ds(pl.multiple_of(dp * 8, 8), 8)]),
+            (tok_hbm, tok_ref),
+            (wd_ref, w_down),
+            (wg_ref, w_in.at[:, pl.ds(0, hidden_width)]),
+            (wu_ref, w_in.at[:, pl.ds(hidden_width, hidden_width)]),
+            (out_o, full_o_ref),
+            (query_hbm, query_ref),
+            (mixed_hbm, mixed_ref),
+            (cot_hbm, cot_ref),
         ]
-        locals_ = [pltpu.make_async_copy(a, b, here.at[i]) for i, (a, b) in enumerate(locals_)]
+        moves = [pltpu.make_async_copy(a, b, here.at[i]) for i, (a, b) in enumerate(moves)]
+        locals_, load_down, load_in, later = moves[:8], moves[8], moves[9:11], moves[11:]
         for one in locals_:
             one.start()
+        load_down.start()
         greet(wires, range(1, planes), True)
         for one in locals_:
             one.wait()
@@ -705,11 +877,28 @@
         plane_kv, plane_q, plane_o = [PlaneGather(wires, r, group) for r in (full_kv, full_q, full_o)]
         plane_cot = PlaneGather(wires, all_cot, tok_rows)
         line_keys = LineGather(wires, all_kv, lambda block: rows_at(block * tok_rows, tok_rows))
+        spread = PlaneGather(wires, x_all, tok_rows)
+        plane = PlaneReduce(
+            wires, y_all, tok_rows, y_all, lambda slot: rows_begin(masked(dp, 2 * slot)), core_in, first_in, second_in,
+            None,
+        )
+        summed = LineSum(wires, sums, total_ref, sums_land, CHUNK, chunks, goes_on=True)
+        dense = PlaneReduce(
+            wires, part_o, group, part_o, lambda slot: pl.multiple_of(masked(dp, 2 * slot) * group, 16),
+            core_in, first_in, second_in, w_out_ref,
+        )
+        line = LineReduce(wires, kv_part, tok_rows, kv_land, ways=(-1,))
         first = wires.take(planes - 1)
 
         def gate_copy(mask, owner):
-            part = all_gate.at[pl.ds(pl.multiple_of(owner * 8, 8), 8)]
+            part = all_gate.at[gate_rows(owner)]
             return wires.copy(part, part, first + mask - 1, dp=masked(dp, mask))
+
+        def set_bias():
+            key_place = lax.broadcasted_iota(jnp.int32, (keys, tok_rows), 0)
+            query_place = lax.broadcasted_iota(jnp.int32, (keys, tok_rows), 1) + z * tok_rows
+            allowed = (key_place >= starts_ref[0:1, :]) & (key_place <= query_place)
+            bias[...] = jnp.where(allowed, 0.0, masked_score)
 
         line_kv.start(0)
         plane_cot.start(0)
@@ -717,10 +906,7 @@
             gate_copy(mask, dp).start()
         line_kv.wait(0)
         line_kv.start(1)
-        key_place = lax.broadcasted_iota(jnp.int32, (keys, tok_rows), 0)
-        query_place = lax.broadcasted_iota(jnp.int32, (keys, tok_rows), 1) + z * tok_rows
-        allowed = (key_place >= starts_ref[0:1, :]) & (key_place <= query_place)
-        bias[...] = jnp.where(allowed, 0.0, masked_score)
+        set_bias()
         line_kv.wait(1)
         line_kv.start(2)
         line_q.start(0)
@@ -779,8 +965,20 @@
         plane_q.wait(2)
         plane_q.start(3)
         plane_q.finish()
-        saves = [pltpu.make_async_copy(full_q, out_q, there.at[0])]
-        saves.append(pltpu.make_async_copy(full_kv, out_kv, there.at[1]))
+        line_kv.finish()
+        line_q.finish()
+        saves = [
+            (full_q, out_q),
+            (full_kv, out_kv),
+            (normed_ref, normed_hbm),
+            (query_ref, query_hbm),
+            (full_o, out_o),
+            (mixed_ref, mixed_hbm),
+            (middle_ref, middle_hbm),
+        ]
+        saves = [pltpu.make_async_copy(a, b, there.at[11 + i]) for i, (a, b) in enumerate(saves)]
+        save_q, saves = saves[0], saves[1:]
+        save_q.start()
         saves[0].start()
         saves[1].start()
 
@@ -793,9 +991,12 @@
                     pre_q[:, one * HD : (one + 1) * HD], cos_ref[...], sin_ref[...]
                 ).astype(jnp.bfloat16)
 
+        saves[2].start()
         plane_o.wait(0)
         plane_o.start(1)
-        plane_cot.start_far()
+        save_q.wait()
+        for one in load_in:
+            one.start()
         line_keys.wait(2)
         value_t[...] = all_kv[:, key_width:].astype(jnp.float32).T.astype(jnp.bfloat16)
         lse_ref[...] = jnp.zeros_like(lse_ref)
@@ -811,283 +1012,46 @@
             probs = (expo * (1.0 / total)).astype(jnp.bfloat16)
             mixed_ref[:, own_cut] = dot(value_t[key_cut, :], probs, 1, 0).T.astype(jnp.bfloat16)
 
-        pl.loop(0, HEADS)(attend)
+        pl.loop(0, HEADS // 2)(attend)
+        plane_cot.start_far()
+        pl.loop(HEADS // 2, HEADS)(attend)
         plane_o.wait(1)
         plane_o.start(2)
         plane_o.wait(2)
         plane_o.start(3)
         plane_o.finish()
-        saves.append(pltpu.make_async_copy(full_o, out_o, there.at[2]))
-        saves[2].start()
-
-        @pl.loop(0, width // 512)
-        def _(step):
-            cut = pl.ds(pl.multiple_of(step * 512, 512), 512)
-            middle_ref[:, cut] = tok_ref[:, cut].astype(jnp.float32) + dot(
-                mixed_ref[...], full_o[:, cut], 1, 0
-            )
-
-        @pl.loop(0, tok_rows // tile)
-        def _(step):
-            cut = pl.ds(pl.multiple_of(step * tile, tile), tile)
-            routed_ref[cut, :] = rms_norm(middle_ref[cut, :], gain_rows_ref[1:2, :]).astype(jnp.bfloat16)
-
+        line_o.finish()
+        saves[3].start()
+        saves[4].start()
+
+        half_rows = tok_rows // 2
+        for half in range(2):
+            half_cut = pl.ds(half * half_rows, half_rows)
+
+            @pl.loop(0, width // 512)
+            def _(step):
+                cut = pl.ds(pl.multiple_of(step * 512, 512), 512)
+                middle_ref[half_cut, cut] = tok_ref[half_cut, cut].astype(jnp.float32) + dot(
+                    mixed_ref[half_cut, :], full_o[:, cut], 1, 0
+                )
+
+            @pl.loop(0, half_rows // tile)
+            def _(step):
+                begin = half * half_rows + step * tile
+                cut = pl.ds(pl.multiple_of(begin, tile), tile)
+                x_all[pl.ds(pl.multiple_of(dp * tok_rows + begin, tile), tile), :] = rms_norm(
+                    middle_ref[cut, :], gain_rows_ref[1:2, :]
+                ).astype(jnp.bfloat16)
+
+            spread.start_one(half)
+        spread.start_one(2)
+        saves[5].start()
         plane_cot.wait(2)
         plane_cot.start(3)
         plane_cot.finish()
-        saves.append(pltpu.make_async_copy(all_cot, out_cot, there.at[3]))
-        saves[3].start()
         for mask in range(1, planes):
             gate_copy(mask, masked(dp, mask)).wait_recv()
-        for mask in range(1, planes):
-            gate_copy(mask, dp).wait_send()
-        for one in (line_kv, line_q, line_o, line_keys):
-            one.finish()
-        for one in saves:
-            one.wait()
-
-    f32, low = jnp.float32, jnp.bfloat16
-    copies = 4 * LineGather.COPIES + 4 * PlaneGather.COPIES + planes - 1
-    return pl.pallas_call(
-        kernel,
-        out_shape=(
-            jax.ShapeDtypeStruct((w_rows, width), low),
-            jax.ShapeDtypeStruct((w_rows, kv_width + LANES), low),
-            jax.ShapeDtypeStruct((w_rows, width), low),
-            jax.ShapeDtypeStruct((planes * tok_rows, width), low),
-            jax.ShapeDtypeStruct((planes * 8, tok_rows), f32),
-            jax.ShapeDtypeStruct((tok_rows, width), low),
-            jax.ShapeDtypeStruct((keys, kv_width), low),
-            jax.ShapeDtypeStruct((16, tok_rows), f32),
-            jax.ShapeDtypeStruct((tok_rows, width), low),
-            jax.ShapeDtypeStruct((tok_rows, width), f32),
-            jax.ShapeDtypeStruct((tok_rows, width), low),
-            jax.ShapeDtypeStruct((tok_rows, width), low),
-            jax.ShapeDtypeStruct((8, width), f32),
-        ),
-        in_specs=[VMEM] * 11,
-        out_specs=(ANY,) * 4 + (VMEM,) * 9,
-        scratch_shapes=[
-            pltpu.VMEM((w_rows, width), low),
-            pltpu.VMEM((w_rows, kv_width + LANES), low),
-            pltpu.VMEM((w_rows, width), low),
-            pltpu.VMEM((planes * tok_rows, width), low),
-            pltpu.VMEM((keys, tok_rows), f32),
-            pltpu.VMEM((kv_width - key_width, keys), low),
-            pltpu.SemaphoreType.DMA((7,)),
-            pltpu.SemaphoreType.DMA((4,)),
-        ]
-        + sems(copies),
-        compiler_params=kernel_params(0, 63),
-        name="front",
-    )(w_query, w_key, w_value, gains, w_out, cotangent, gates, tokens, starts, cosine, sine)
-
-
-CHUNK = 64
-AHEAD = 4
-CARRIED = 2
-RING = 4
-BEFORE_DENSE = 16
-
-
-class LineSum:
-    def __init__(self, wires, own, out, landing, rows, chunks, came=False, goes_on=False):
-        self.wires, self.own, self.out, self.landing = wires, own, out, landing
-        self.rows, self.chunks, self.came, self.goes_on = rows, chunks, came, goes_on
-        self.all = chunks + (CARRIED if goes_on else 0)
-        self.begun = CARRIED if came else 0
-        self.now = self.begun
-        self.first = wires.take(3 * self.all)
-        z = wires.z
-        self.inner = (z == 1) | (z == 2)
-        self.outer = (z == 0) | (z == 3)
-        self.end = 3 * (z - 1)
-        self.near = 1 + z // 3
-        self.peer = 3 - z
-
-    def _cut(self, ref, chunk):
-        return ref.at[pl.ds(pl.multiple_of(chunk * self.rows, 16), self.rows)]
-
-    def _in(self, chunk):
-        return self.wires.copy(
-            self._cut(self.own, chunk), self._cut(self.out, chunk), self.first + chunk, z=self.near
-        )
-
-    def _across(self, chunk):
-        number = self.first + self.all + chunk
-        return self.wires.copy(
-            self._cut(self.own, chunk), self._cut(self.landing, lax.rem(chunk, RING)), number, z=self.peer
-        )
-
-    def _back(self, chunk, ref=None):
-        number = self.first + 2 * self.all + chunk
-        return self.wires.copy(
-            self._cut(self.out if ref is None else ref, chunk), self._cut(self.out, chunk), number, z=self.end
-        )
-
-    def begin(self):
-        @pl.when(self.outer)
-        def _():
-            for chunk in range(self.begun, min(self.begun + AHEAD, self.all)):
-                self._in(chunk).start()
-
-        if self.came:
-
-            @pl.when(self.inner)
-            def _():
-                self._across(1).start()
-                self._back(0, self.own).start()
-                self.out[pl.ds(0, self.rows), :] = self.own[pl.ds(0, self.rows), :]
-
-    def tick(self, count=1):
-        for _ in range(count):
-            if self.now < self.all + (0 if self.goes_on else 1):
-                self._tick(self.now)
-            self.now += 1
-
-    def _tick(self, chunk):
-        if chunk < self.all:
-
-            @pl.when(self.outer)
-            def _():
-                self._in(chunk).wait_send()
-                if chunk + AHEAD < self.all:
-                    self._in(chunk + AHEAD).start()
-
-        @pl.when(self.inner)
-        def _():
-            if chunk < self.all:
-                row = chunk * self.rows
-                self._in(chunk).wait_recv()
-                add_rows(self.own, row, self.own, row, self.out, row, self.rows)
-                if chunk <= self.chunks:
-                    self._across(chunk).start()
-            if chunk >= 1:
-                row = (chunk - 1) * self.rows
-                landed = (chunk - 1) % RING * self.rows
-                self._across(chunk - 1).wait_recv()
-                if chunk - 1 < self.chunks:
-                    add_rows(self.out, row, self.own, row, self.landing, landed, self.rows)
-                    self._back(chunk - 1).start()
-                else:
-                    self._across(chunk - 1).wait_send()
-                    add_rows(self.own, row, self.own, row, self.landing, landed, self.rows)
-
-    def finish(self):
-        self.tick(max(0, self.all + (0 if self.goes_on else 1) - self.now))
-
-        @pl.when(self.outer)
-        def _():
-            @pl.loop(0, self.chunks)
-            def _(chunk):
-                self._back(chunk).wait_recv()
-
-        @pl.when(self.inner)
-        def _():
-            @pl.loop(1 if self.came else 0, self.chunks)
-            def _(chunk):
-                self._across(chunk).wait_send()
-
-            @pl.loop(0, self.chunks)
-            def _(chunk):
-                self._back(chunk).wait_send()
-
-
-def norm_back(values, gain, grad):
-    scale = lax.rsqrt(jnp.mean(values * values, axis=-1, keepdims=True) + epsilon)
-    normal = values * scale
-    inner = grad * gain
-    to_values = scale * (inner - normal * jnp.mean(inner * normal, axis=-1, keepdims=True))
-    return to_values, grad * normal
-
-
-def turned(values, cosine, sine):
-    return values * cosine + pltpu.roll(values, HD // 2, 1) * sine
-
-
-def experts_attention(
-    routed,
-    all_cot,
-    all_gate,
-    w_gate,
-    w_up,
-    w_down,
-    full_o,
-    middle,
-    cotangent,
-    gain_rows,
-    mixed,
-    query,
-    all_kv,
-    lse,
-    starts,
-    cosine,
-    sine,
-):
-    tok_rows, width = routed.shape
-    hidden_width = w_gate.shape[1]
-    keys, kv_width = all_kv.shape
-    total_rows = 8 * tok_rows
-    sum_rows = width + hidden_width
-    group = width // 8
-    chunks = BEFORE_DENSE
-    score_scale = HD ** (-0.5)
-    per_group = HEADS // KVH
-    q_width = HEADS * HD
-
-    def kernel(
-        routed_ref, all_cot_ref, gate_ref, wg_ref, wu_ref, wd_ref, full_o_hbm, middle_hbm, cot_hbm, gain_ref, mixed_hbm,
-        query_hbm, kv_hbm, lse_ref, starts_ref, cos_ref, sin_ref,
-        sums_ref, prod_ref, total_ref, grad_mid_hbm, grad_pre_ref, gain_row_ref, w_out_ref,
-        w_in, w_down, x_all, y_all, hidden, grad_hidden, grad_in, sums, sums_land, gate_t, core_in, first_in, second_in,
-        routed_grad, middle_ref, key_t, kv_land, here, there, freed, send, recv,
-    ):
-        wires = Wires(send, recv)
-        dp, z = wires.dp, wires.z
-
-        def rows_begin(block):
-            return pl.multiple_of(block * tok_rows, 16)
-
-        def cut_of(block):
-            return pl.ds(rows_begin(block), tok_rows)
-
-        full_o_ref = w_in
-        part_o = y_all.at[pl.ds(0, width)]
-        query_ref, mixed_ref, cot_ref, attn_low, mixed_grad = [grad_in.at[pl.ds(i * tok_rows, tok_rows)] for i in range(5)]
-        kv_ref = hidden.at[pl.ds(0, keys), pl.ds(0, kv_width)]
-        kv_part = hidden.at[pl.ds(keys, keys), pl.ds(0, kv_width)]
-        kv_grad = grad_hidden.at[pl.ds(0, keys), pl.ds(0, kv_width)]
-        bias = grad_hidden.at[pl.ds(keys, keys), pl.ds(0, tok_rows)]
-        kv_out = grad_hidden.at[pl.ds(keys, tok_rows), pl.ds(tok_rows, kv_width)]
-
-        loads = [
-            (routed_ref, x_all.at[cut_of(dp)]),
-            (wd_ref, w_down),
-            (all_cot_ref, y_all),
-            (wg_ref, w_in.at[:, pl.ds(0, hidden_width)]),
-            (wu_ref, w_in.at[:, pl.ds(hidden_width, hidden_width)]),
-            (middle_hbm, middle_ref),
-        ]
-        later = [(full_o_hbm, full_o_ref), (query_hbm, query_ref), (mixed_hbm, mixed_ref), (cot_hbm, cot_ref), (kv_hbm, kv_ref)]
-        loads = [pltpu.make_async_copy(a, b, here.at[i]) for i, (a, b) in enumerate(loads + later)]
-        loads, later = loads[: len(loads) - len(later)], loads[len(loads) - len(later) :]
-        for one in loads:
-            one.start()
-        greet(wires, (1, 2, 4), True)
-        loads[0].wait()
-        spread = PlaneGather(wires, x_all, tok_rows)
-        plane = PlaneReduce(
-            wires, y_all, tok_rows, y_all, lambda slot: rows_begin(masked(dp, 2 * slot)), core_in, first_in, second_in,
-            routed_grad,
-        )
-        summed = LineSum(wires, sums, total_ref, sums_land, CHUNK, chunks, goes_on=True)
-        dense = PlaneReduce(
-            wires, part_o, group, part_o, lambda slot: pl.multiple_of(masked(dp, 2 * slot) * group, 16),
-            core_in, first_in, second_in, w_out_ref,
-        )
-        line = LineReduce(wires, kv_part, tok_rows, kv_land, ways=(-1,))
-        spread.start(0)
-        gate_t[...] = gate_ref[...].T
+        gate_t[...] = all_gate[...].T
 
         def gate_of(block):
             lane = lax.broadcasted_iota(jnp.int32, gate_t.shape, 1)
@@ -1111,14 +1075,13 @@
             ).astype(jnp.bfloat16)
             grad_in[cut, hidden_width:] = (grad * silu).astype(jnp.bfloat16)
 
-        loads[1].wait()
-        loads[2].wait()
+        load_down.wait()
         pl.loop(0, 4)(back_hidden)
         spread.wait(0)
         spread.start(1)
         pl.loop(4, 8)(back_hidden)
-        loads[3].wait()
-        loads[4].wait()
+        for one in load_in + saves:
+            one.wait()
         through(0)
         spread.wait_core(0)
         through(1)
@@ -1176,7 +1139,7 @@
         plane.step(3)
         pl.loop(4, 6)(weights_in)
         summed.tick()
-        for one in later[1:4]:
+        for one in later[1:]:
             one.start()
         saved = (chunks + CARRIED) * CHUNK
         save = save_sums(saved, sum_rows, 0)
@@ -1195,35 +1158,31 @@
         pl.loop(0, 4)(make)
         summed.tick()
         pl.loop(4, 8)(make)
-        later[4].start()
         plane.step(4)
         summed.tick()
-        key_place = lax.broadcasted_iota(jnp.int32, (keys, tok_rows), 0)
-        query_place = lax.broadcasted_iota(jnp.int32, (keys, tok_rows), 1) + z * tok_rows
-        allowed = (key_place >= starts_ref[0:1, :]) & (key_place <= query_place)
-        bias[...] = jnp.where(allowed, 0.0, masked_score)
+        set_bias()
         kv_grad[...] = jnp.zeros_like(kv_grad)
         gain_row_ref[...] = jnp.zeros_like(gain_row_ref)
-        loads[5].wait()
         for one in later:
             one.wait()
-        key_t[...] = kv_ref[:, : kv_width // 2].astype(jnp.float32).T.astype(jnp.bfloat16)
+        key_t[...] = all_kv[:, : kv_width // 2].astype(jnp.float32).T.astype(jnp.bfloat16)
         summed.tick()
         plane.step(5)
-        for mask in (1, 2, 4):
-            pl.semaphore_signal(freed, inc=1, device_id=(masked(dp, mask), z), device_id_type=MESH)
 
         tile = 32
 
         @pl.loop(0, tok_rows // tile)
         def _(step):
             cut = pl.ds(pl.multiple_of(step * tile, tile), tile)
-            to_middle, terms = norm_back(middle_ref[cut, :], gain_ref[1:2, :], routed_grad[cut, :])
+            routed_grad = core_in[cut, :].astype(jnp.float32) + second_in[cut, :].astype(jnp.float32)
+            to_middle, terms = norm_back(middle_ref[cut, :], gain_rows_ref[1:2, :], routed_grad)
             to_middle = cot_ref[cut, :].astype(jnp.float32) + to_middle
             middle_ref[cut, :] = to_middle
             attn_low[cut, :] = to_middle.astype(jnp.bfloat16)
             gain_row_ref[0:1, :] += jnp.sum(terms, axis=0, keepdims=True)
 
+        for mask in (1, 2, 4):
+            pl.semaphore_signal(freed, inc=1, device_id=(masked(dp, mask), z), device_id_type=MESH)
         save_mid = pltpu.make_async_copy(middle_ref, grad_mid_hbm, there.at[1])
         save_mid.start()
         summed.tick()
@@ -1251,7 +1210,7 @@
                 key_cut = pl.ds(pl.multiple_of(pair * HD, HD), HD)
                 value_cut = pl.ds(pl.multiple_of((KVH + pair) * HD, HD), HD)
                 q, do = query_ref[:, own_cut], mixed_grad[:, own_cut]
-                k, v = kv_ref[:, key_cut], kv_ref[:, value_cut]
+                k, v = all_kv[:, key_cut], all_kv[:, value_cut]
                 scores = dot(k, q, 1, 1) * score_scale + bias[...]
                 probs = jnp.exp(scores - lse_ref[pl.ds(head, 1), :])
                 grad_probs = dot(v, do, 1, 1)
@@ -1303,11 +1262,24 @@
             save_made(block).wait()
         for one in (save, save_mid, save_last):
             one.wait()
+        line_keys.finish()
+        for mask in range(1, planes):
+            gate_copy(mask, dp).wait_send()
 
     f32, low = jnp.float32, jnp.bfloat16
+    copies = 4 * LineGather.COPIES + 5 * PlaneGather.COPIES + planes - 1
+    copies += 2 * PlaneReduce.COPIES + 3 * (chunks + CARRIED) + LineReduce.COPIES
     return pl.pallas_call(
         kernel,
         out_shape=(
+            jax.ShapeDtypeStruct((width, width), low),
+            jax.ShapeDtypeStruct((width, kv_width + LANES), low),
+            jax.ShapeDtypeStruct((width, width), low),
+            jax.ShapeDtypeStruct((tok_rows, width), low),
+            jax.ShapeDtypeStruct((tok_rows, width), low),
+            jax.ShapeDtypeStruct((tok_rows, width), low),
+            jax.ShapeDtypeStruct((tok_rows, width), f32),
+            jax.ShapeDtypeStruct((8, width), f32),
             jax.ShapeDtypeStruct((sum_rows, width), low),
             jax.ShapeDtypeStruct((total_rows, width), low),
             jax.ShapeDtypeStruct(((chunks + CARRIED) * CHUNK, width), low),
@@ -1316,8 +1288,8 @@
             jax.ShapeDtypeStruct((8, width), f32),
             jax.ShapeDtypeStruct((group, width), low),
         ),
-        in_specs=[ANY, ANY, VMEM] + [ANY] * 6 + [VMEM] + [ANY] * 3 + [VMEM] * 4,
-        out_specs=(ANY, ANY, VMEM, ANY, VMEM, VMEM, VMEM),
+        in_specs=[ANY] * 11 + [VMEM] * 3,
+        out_specs=(ANY,) * 7 + (VMEM, ANY, ANY, VMEM, ANY, VMEM, VMEM, VMEM),
         scratch_shapes=[
             pltpu.VMEM((width, 2 * hidden_width), low),
             pltpu.VMEM((hidden_width, width), low),
@@ -1328,26 +1300,24 @@
             pltpu.VMEM((total_rows, 2 * hidden_width), low),
             pltpu.VMEM((sum_rows, width), low),
             pltpu.VMEM((RING * CHUNK, width), low),
-            pltpu.VMEM((tok_rows, 64), f32),
+            pltpu.VMEM((planes * planes, tok_rows), f32),
+            pltpu.VMEM((tok_rows, planes * planes), f32),
+            pltpu.VMEM((keys, kv_width), low),
+            pltpu.VMEM((16, tok_rows), f32),
         ]
         + PlaneReduce.scratch(tok_rows, width)
         + [
             pltpu.VMEM((tok_rows, width), f32),
-            pltpu.VMEM((tok_rows, width), f32),
-            pltpu.VMEM((kv_width // 2, keys), low),
             LineReduce.scratch(tok_rows, kv_width, 1),
-            pltpu.SemaphoreType.DMA((11,)),
-            pltpu.SemaphoreType.DMA((11,)),
+            pltpu.SemaphoreType.DMA((15,)),
+            pltpu.SemaphoreType.DMA((18,)),
             pltpu.SemaphoreType.REGULAR,
         ]
-        + sems(
-            PlaneGather.COPIES + 2 * PlaneReduce.COPIES + 3 * (chunks + CARRIED) + LineReduce.COPIES
-        ),
+        + sems(copies),
         compiler_params=kernel_params(1, 63),
-        name="experts_attention",
+        name="up_to_attention_back",
     )(
-        routed, all_cot, all_gate, w_gate, w_up, w_down, full_o, middle, cotangent, gain_rows, mixed, query, all_kv,
-        lse, starts, cosine, sine,
+        w_query, w_key, w_value, gains, w_out, tokens, cotangent, gates, w_gate, w_up, w_down, starts, cosine, sine
     )
 
 
@@ -1582,28 +1552,10 @@
     sine = jnp.concatenate([-jnp.sin(angles), jnp.sin(angles)], axis=1)
     starts = jnp.broadcast_to((own_places - within_own)[None, :], (8, tok_rows))
     (
-        full_q, full_kv, full_o, all_cot, all_gate, query, all_kv, lse, mixed_low, middle, normed_low, routed_low,
-        gain_rows,
-    ) = front(
-        w_query, w_key, w_value, gains, w_out, cotangent, gates, tokens, starts, cosine, sine
-    )
-    partial_sums, produced, sums_head, grad_mid, grad_pre, gain_row, w_out_part = experts_attention(
-        routed_low,
-        all_cot,
-        all_gate,
-        w_gate[0],
-        w_up[0],
-        w_down[0],
-        full_o,
-        middle,
-        cotangent,
-        gain_rows,
-        mixed_low,
-        query,
-        all_kv,
-        lse,
-        starts,
-        cosine,
+        full_q, full_kv, _, _, _, normed_low, middle, gain_rows, partial_sums, produced, sums_head, grad_mid, grad_pre,
+        gain_row, w_out_part,
+    ) = up_to_attention_back(
+        w_query, w_key, w_value, gains, w_out, tokens, cotangent, gates, w_gate[0], w_up[0], w_down[0], starts, cosine,
         sine,
     )
     half = w_gate.shape[2]

time: 392 us -> 379 us (0.967)
  Pallas kernels: 363 us -> 350 us
    pallas_call x2 -> x1, Pallas kernels: 237 us -> 225 us  [up_to_attention_back(): pl.pallas_call(kernel, out_shape=(jax.ShapeDtypeStruct((width, width), lo...]
where the time goes in v6:
time: 379 us; the launch traced here: 374 us
  Pallas kernels  350 us (92%)
  other arithmetic  14.8 us (4%)
  local copies, waits for them, and re-layouts  8.97 us (2%)
    pallas_call x1, Pallas kernels, up_to_attention_back(): pl.pallas_call(kernel, out_shape=(jax.ShapeDtypeStruct((width, width), lo...  225 us
    pallas_call x1, Pallas kernels, back_dense(): pl.pallas_call(kernel, out_shape=(jax.ShapeDtypeStruct((chunks * CHUNK, s...  125 us

profile of v6, /device:TPU:0, one launch (start us, length us, event | category | flops | bytes accessed | tf_op | source)
XLA Modules:
  0.0 374.2 jit_solution(14366898031609812102)
XLA Ops:
  0.6 0.7 pad_maximum_fusion.2
  1.3 0.8 reduce-window.8
  2.2 0.7 select_reduce_fusion.1
  2.9 0.1 dynamic-slice_convert_fusion
  3.0 0.6 broadcast_in_dim.52.starts_ref
  3.6 1.3 select_reduce_fusion.gate_ref
  4.9 0.1 copy.36
  5.0 0.6 pad.4.gains_ref
  5.6 0.5 fusion
  6.2 0.8 pad_maximum_fusion
  7.0 224.6 %up_to_attention_back.1 = (bf16[1536,1536]{1,0:T(8,128)(2,1)}, bf16[1536,640]{1,0:T(8,128)(2,1)}, bf16[1536,1536]{1,0:T(8,128)(2,1)}, bf16[256,1536]{1,0:T(8,128...) custom-call(bf16[48,1536]{1,0:T(8,128)(2,1)} %wq_ref.1, ...), custom_call_target="tpu_custom_call" | custom-call | tf_op jit(solution)/shard_map/up_to_attention_back/pallas_call | solution.py:1272
  231.6 125.0 %back_dense.1 = (bf16[1280,1536]{1,0:T(8,128)(2,1)}, bf16[256,1536]{1,0:T(8,128)(2,1)}, f32[256,1536]{1,0:T(8,128)}, f32[48,1536]{1,0:T(8,128)}, f32[48,256]{1,0...) custom-call(bf16[2304,1536]{1,0:T(8,128)(2,1)} %get-tuple-element.31.sums_ref, ...), custom_call_target="tpu_custom_call" | custom-call | tf_op jit(solution)/shard_map/back_dense/pallas_call | solution.py:1471
  356.6 1.5 slice_reduce_fusion
  358.2 1.2 slice_bitcast_fusion.2
  359.3 4.6 %bitcast_convert_fusion = f32[1,768,1536]{2,1,0:T(8,128)} fusion(bf16[1152,1536]{1,0:T(8,128)(2,1)} %get-tuple-element.49), kind=kLoop, calls=%fused_computation.2 | loop fusion | flops 1179648 | bytes 7077888 | tf_op jit(solution)/shard_map/broadcast_in_dim | solution.py:1592
  364.0 0.3 slice_bitcast_fusion
  364.2 2.5 maximum_convert_fusion.1
  366.8 2.5 maximum_convert_fusion
  369.4 0.9 copy.43
  370.2 1.1 copy.44
  371.4 0.7 copy.45
  372.1 0.6 copy.46
  372.7 0.6 copy.47
  373.4 0.7 copy.48
  (16 shorter events, 0.0 us)
Async XLA Ops:
  359.3 4.7 %copy-start = (bf16[1280,1536]{1,0:T(8,128)(2,1)S(1)}, bf16[1280,1536]{1,0:T(8,128)(2,1)}, u32[]{:S(2)}) copy-start(bf16[1280,1536]{1,0:T(8,128)(2,1)} %get-tuple-element.50) | copy-start | bytes 11796484
  366.8 2.6 copy-start.2
  366.8 3.5 copy-start.1
  369.3 2.0 copy-start.4
  369.3 2.8 copy-start.6
  369.3 3.4 copy-start.5
  369.3 4.0 %copy-start.3 = (f32[48,1536]{1,0:T(8,128)S(1)}, f32[48,1536]{1,0:T(8,128)}, u32[]{:S(2)}) copy-start(f32[48,1536]{1,0:T(8,128)} %get-tuple-element.81) | copy-start | bytes 884740

commit v7 on v6

--- a/solution.py
+++ b/solution.py
@@ -668,17 +668,19 @@
 
 
 CHUNK = 64
-AHEAD = 4
+AHEAD = 3
 CARRIED = 2
 RING = 4
-BEFORE_DENSE = 16
+FIRST_CHUNKS = (CHUNK,) * 22
+LAST_CHUNKS = (CHUNK,) * 16
 
 
 class LineSum:
-    def __init__(self, wires, own, out, landing, rows, chunks, came=False, goes_on=False):
+    def __init__(self, wires, own, out, landing, sizes, came=False, goes_on=False):
         self.wires, self.own, self.out, self.landing = wires, own, out, landing
-        self.rows, self.chunks, self.came, self.goes_on = rows, chunks, came, goes_on
-        self.all = chunks + (CARRIED if goes_on else 0)
+        self.sizes, self.came, self.goes_on = sizes, came, goes_on
+        self.all = len(sizes)
+        self.chunks = self.all - (CARRIED if goes_on else 0)
         self.begun = CARRIED if came else 0
         self.now = self.begun
         self.first = wires.take(3 * self.all)
@@ -689,8 +691,14 @@
         self.near = 1 + z // 3
         self.peer = 3 - z
 
+    def _row(self, chunk):
+        return sum(self.sizes[:chunk])
+
     def _cut(self, ref, chunk):
-        return ref.at[pl.ds(pl.multiple_of(chunk * self.rows, 16), self.rows)]
+        return ref.at[pl.ds(self._row(chunk), self.sizes[chunk])]
+
+    def _slot(self, chunk):
+        return chunk % RING * CHUNK
 
     def _in(self, chunk):
         return self.wires.copy(
@@ -698,9 +706,9 @@
         )
 
     def _across(self, chunk):
-        number = self.first + self.all + chunk
+        landed = self.landing.at[pl.ds(self._slot(chunk), self.sizes[chunk])]
         return self.wires.copy(
-            self._cut(self.own, chunk), self._cut(self.landing, lax.rem(chunk, RING)), number, z=self.peer
+            self._cut(self.own, chunk), landed, self.first + self.all + chunk, z=self.peer
         )
 
     def _back(self, chunk, ref=None):
@@ -721,7 +729,7 @@
             def _():
                 self._across(1).start()
                 self._back(0, self.own).start()
-                self.out[pl.ds(0, self.rows), :] = self.own[pl.ds(0, self.rows), :]
+                self.out[pl.ds(0, self.sizes[0]), :] = self.own[pl.ds(0, self.sizes[0]), :]
 
     def tick(self, count=1):
         for _ in range(count):
@@ -741,39 +749,35 @@
         @pl.when(self.inner)
         def _():
             if chunk < self.all:
-                row = chunk * self.rows
+                row = self._row(chunk)
                 self._in(chunk).wait_recv()
-                add_rows(self.own, row, self.own, row, self.out, row, self.rows)
+                add_rows(self.own, row, self.own, row, self.out, row, self.sizes[chunk])
                 if chunk <= self.chunks:
                     self._across(chunk).start()
             if chunk >= 1:
-                row = (chunk - 1) * self.rows
-                landed = (chunk - 1) % RING * self.rows
-                self._across(chunk - 1).wait_recv()
-                if chunk - 1 < self.chunks:
-                    add_rows(self.out, row, self.own, row, self.landing, landed, self.rows)
-                    self._back(chunk - 1).start()
+                last = chunk - 1
+                row, landed, rows = self._row(last), self._slot(last), self.sizes[last]
+                self._across(last).wait_recv()
+                if last < self.chunks:
+                    add_rows(self.out, row, self.own, row, self.landing, landed, rows)
+                    self._back(last).start()
                 else:
-                    self._across(chunk - 1).wait_send()
-                    add_rows(self.own, row, self.own, row, self.landing, landed, self.rows)
+                    self._across(last).wait_send()
+                    add_rows(self.own, row, self.own, row, self.landing, landed, rows)
 
     def finish(self):
         self.tick(max(0, self.all + (0 if self.goes_on else 1) - self.now))
 
         @pl.when(self.outer)
         def _():
-            @pl.loop(0, self.chunks)
-            def _(chunk):
+            for chunk in range(self.chunks):
                 self._back(chunk).wait_recv()
 
         @pl.when(self.inner)
         def _():
-            @pl.loop(1 if self.came else 0, self.chunks)
-            def _(chunk):
+            for chunk in range(1 if self.came else 0, self.chunks):
                 self._across(chunk).wait_send()
-
-            @pl.loop(0, self.chunks)
-            def _(chunk):
+            for chunk in range(self.chunks):
                 self._back(chunk).wait_send()
 
 
@@ -802,7 +806,7 @@
     hidden_width = w_gate.shape[1]
     total_rows = planes * tok_rows
     sum_rows = width + hidden_width
-    chunks = BEFORE_DENSE
+    sent_rows, done_rows = sum(FIRST_CHUNKS), sum(FIRST_CHUNKS[:-CARRIED])
     score_scale = HD ** (-0.5)
     per_group = HEADS // KVH
     q_width = HEADS * HD
@@ -882,7 +886,7 @@
             wires, y_all, tok_rows, y_all, lambda slot: rows_begin(masked(dp, 2 * slot)), core_in, first_in, second_in,
             None,
         )
-        summed = LineSum(wires, sums, total_ref, sums_land, CHUNK, chunks, goes_on=True)
+        summed = LineSum(wires, sums, total_ref, sums_land, FIRST_CHUNKS, goes_on=True)
         dense = PlaneReduce(
             wires, part_o, group, part_o, lambda slot: pl.multiple_of(masked(dp, 2 * slot) * group, 16),
             core_in, first_in, second_in, w_out_ref,
@@ -1141,8 +1145,7 @@
         summed.tick()
         for one in later[1:]:
             one.start()
-        saved = (chunks + CARRIED) * CHUNK
-        save = save_sums(saved, sum_rows, 0)
+        save = save_sums(sent_rows, sum_rows, 0)
         save.start()
 
         def save_made(block):
@@ -1247,7 +1250,7 @@
         line.event(4)
         dense.step(5)
         summed.tick(max(0, summed.all - summed.now))
-        save_last = save_sums(chunks * CHUNK, saved, 2)
+        save_last = save_sums(done_rows, sent_rows, 2)
         save_last.start()
         line.event(5)
         line.finish((kv_out,))
@@ -1268,7 +1271,7 @@
 
     f32, low = jnp.float32, jnp.bfloat16
     copies = 4 * LineGather.COPIES + 5 * PlaneGather.COPIES + planes - 1
-    copies += 2 * PlaneReduce.COPIES + 3 * (chunks + CARRIED) + LineReduce.COPIES
+    copies += 2 * PlaneReduce.COPIES + 3 * len(FIRST_CHUNKS) + LineReduce.COPIES
     return pl.pallas_call(
         kernel,
         out_shape=(
@@ -1282,7 +1285,7 @@
             jax.ShapeDtypeStruct((8, width), f32),
             jax.ShapeDtypeStruct((sum_rows, width), low),
             jax.ShapeDtypeStruct((total_rows, width), low),
-            jax.ShapeDtypeStruct(((chunks + CARRIED) * CHUNK, width), low),
+            jax.ShapeDtypeStruct((sent_rows, width), low),
             jax.ShapeDtypeStruct((tok_rows, width), f32),
             jax.ShapeDtypeStruct((tok_rows, width + kv_width), low),
             jax.ShapeDtypeStruct((8, width), f32),
@@ -1328,8 +1331,7 @@
     pre_width = in_width - LANES
     w_rows = width
     group, rows = w_rows // 8, w_rows // (8 * LINE)
-    skipped = BEFORE_DENSE
-    chunks = sums_in.shape[0] // CHUNK - skipped
+    skipped, sum_rows = sum(FIRST_CHUNKS[:-CARRIED]), sum(LAST_CHUNKS)
 
     def kernel(
         sums_ref, prod_ref, full_q_hbm, full_kv_hbm, normed_hbm, pre_hbm, tok_hbm, gain_ref, mid_grad_hbm,
@@ -1341,12 +1343,11 @@
         wires = Wires(send, recv)
         dp, z = wires.dp, wires.z
         early = (CARRIED + AHEAD) * CHUNK
-        begin = skipped * CHUNK
         loads = [
-            pltpu.make_async_copy(sums_ref.at[pl.ds(begin, early)], sums_own.at[pl.ds(0, early)], here.at[0]),
+            pltpu.make_async_copy(sums_ref.at[pl.ds(skipped, early)], sums_own.at[pl.ds(0, early)], here.at[0]),
             pltpu.make_async_copy(
-                sums_ref.at[pl.ds(begin + early, chunks * CHUNK - early)],
-                sums_own.at[pl.ds(early, chunks * CHUNK - early)],
+                sums_ref.at[pl.ds(skipped + early, sum_rows - early)],
+                sums_own.at[pl.ds(early, sum_rows - early)],
                 here.at[1],
             ),
             pltpu.make_async_copy(o_part_hbm, o_sums, here.at[2]),
@@ -1371,7 +1372,7 @@
         for one in loads:
             one.start()
         greet(wires, (1, 2, 4), True)
-        summed = LineSum(wires, sums_own, total_ref, sums_land, CHUNK, chunks, came=True)
+        summed = LineSum(wires, sums_own, total_ref, sums_land, LAST_CHUNKS, came=True)
         dense = PlaneReduce(
             wires, part, group, part, lambda slot: pl.multiple_of(masked(dp, 2 * slot) * group, 16),
             d_core, d_first, d_second, in_sums,
@@ -1471,7 +1472,7 @@
     return pl.pallas_call(
         kernel,
         out_shape=(
-            jax.ShapeDtypeStruct((chunks * CHUNK, sums_in.shape[1]), low),
+            jax.ShapeDtypeStruct((sum_rows, width), low),
             jax.ShapeDtypeStruct((tok_rows, width), low),
             jax.ShapeDtypeStruct((tok_rows, width), f32),
             jax.ShapeDtypeStruct((rows, q_width), f32),
@@ -1483,7 +1484,7 @@
         in_specs=[ANY] * 7 + [VMEM, ANY, VMEM, ANY, ANY],
         out_specs=(VMEM,) * 8,
         scratch_shapes=[
-            pltpu.VMEM((chunks * CHUNK, width), low),
+            pltpu.VMEM((sum_rows, width), low),
             pltpu.VMEM((RING * CHUNK, width), low),
             pltpu.VMEM(full_q.shape, low),
             pltpu.VMEM(full_kv.shape, low),
@@ -1506,12 +1507,90 @@
             pltpu.VMEM((LANES, width), f32),
             pltpu.SemaphoreType.DMA((14,)),
         ]
-        + sems(3 * chunks + 2 * PlaneReduce.COPIES + 2 * LineReduce.COPIES),
+        + sems(3 * len(LAST_CHUNKS) + 2 * PlaneReduce.COPIES + 2 * LineReduce.COPIES),
         compiler_params=kernel_params(4, 63),
         name="back_dense",
     )(
         sums_in, produced, full_q, full_kv, normed, grad_pre, tokens, gains, grad_mid, gain_row, w_out_part, middle
     )
+
+
+def hand_over(sums_head, sums_tail, gains, *others):
+    done, width = sum(FIRST_CHUNKS[:-CARRIED]), sums_head.shape[1]
+    hidden_width = width // 2
+    rows = 256
+    head_steps, tail_steps = done // rows, sums_tail.shape[0] // rows
+    down_steps = hidden_width // rows
+    steps = head_steps + tail_steps
+    count = len(others)
+
+    def kernel(*refs):
+        head_ref, tail_ref, gains_ref = refs[:3]
+        down_ref, gate_ref, up_ref, attn_ref, moe_ref = refs[3 + count : 8 + count]
+        step = pl.program_id(0)
+        for source, target in zip(refs[3 : 3 + count], refs[8 + count :]):
+            target[...] = source[...]
+
+        @pl.when(step == 0)
+        def _():
+            turned_gains = gains_ref[...].T
+            attn_ref[...] = turned_gains[0, :]
+            moe_ref[...] = turned_gains[1, :]
+
+        def put(values):
+            @pl.when(step < down_steps)
+            def _():
+                down_ref[0] = values
+
+            @pl.when(step >= down_steps)
+            def _():
+                gate_ref[0] = values[:, :hidden_width]
+                up_ref[0] = values[:, hidden_width:]
+
+        @pl.when(step < head_steps)
+        def _():
+            put(head_ref[...].astype(jnp.float32))
+
+        @pl.when(step >= head_steps)
+        def _():
+            put(tail_ref[...].astype(jnp.float32))
+
+    def by_rows(one):
+        if one.shape[0] % (8 * 16):
+            return pl.BlockSpec(one.shape, lambda i: (0, 0))
+        return pl.BlockSpec((one.shape[0] // 8, one.shape[1]), lambda i: (jnp.minimum(i, 7), 0))
+
+    f32 = jnp.float32
+    in_shape = (1, rows, hidden_width)
+    copied = [by_rows(one) for one in others]
+    return pl.pallas_call(
+        kernel,
+        grid=(steps,),
+        out_shape=(
+            jax.ShapeDtypeStruct((1, hidden_width, width), f32),
+            jax.ShapeDtypeStruct((1, width, hidden_width), f32),
+            jax.ShapeDtypeStruct((1, width, hidden_width), f32),
+            jax.ShapeDtypeStruct((gains.shape[0],), f32),
+            jax.ShapeDtypeStruct((gains.shape[0],), f32),
+        )
+        + tuple(jax.ShapeDtypeStruct(one.shape, one.dtype) for one in others),
+        in_specs=[
+            pl.BlockSpec((rows, width), lambda i: (jnp.minimum(i, head_steps - 1), 0)),
+            pl.BlockSpec((rows, width), lambda i: (jnp.maximum(i - head_steps, 0), 0)),
+            pl.BlockSpec(gains.shape, lambda i: (0, 0)),
+        ]
+        + copied,
+        out_specs=(
+            pl.BlockSpec((1, rows, width), lambda i: (0, jnp.minimum(i, down_steps - 1), 0)),
+            pl.BlockSpec(in_shape, lambda i: (0, jnp.maximum(i - down_steps, 0), 0)),
+            pl.BlockSpec(in_shape, lambda i: (0, jnp.maximum(i - down_steps, 0), 0)),
+            pl.BlockSpec((gains.shape[0],), lambda i: (0,)),
+            pl.BlockSpec((gains.shape[0],), lambda i: (0,)),
+        )
+        + tuple(copied),
+        compiler_params=pltpu.CompilerParams(vmem_limit_bytes=63 * MIB),
+        name="hand_over",
+    )(sums_head, sums_tail, gains, *others)
 
 
 def on_plane_device(
@@ -1558,7 +1637,6 @@
         w_query, w_key, w_value, gains, w_out, tokens, cotangent, gates, w_gate[0], w_up[0], w_down[0], starts, cosine,
         sine,
     )
-    half = w_gate.shape[2]
     sums_tail, layer_out, grad_tokens, sum_q, sum_k, sum_v, sum_gains, sum_o = back_dense(
         partial_sums,
         produced,
@@ -1573,23 +1651,11 @@
         w_out_part,
         middle,
     )
-    head = BEFORE_DENSE * CHUNK
-
-    def whole(columns):
-        return jnp.concatenate([sums_head[half:head, columns], sums_tail[:, columns]], axis=0)
-
+    down, gate, up, gain_attn, gain_moe, layer_out, grad_tokens, sum_q, sum_k, sum_v, sum_o = hand_over(
+        sums_head, sums_tail, sum_gains, layer_out, grad_tokens, sum_q, sum_k, sum_v, sum_o
+    )
     return (
-        layer_out,
-        grad_tokens,
-        sum_gains[:, 0],
-        sum_q,
-        sum_k,
-        sum_v,
-        sum_o,
-        sum_gains[:, 1],
-        whole(slice(0, half)).astype(jnp.float32)[None],
-        whole(slice(half, 2 * half)).astype(jnp.float32)[None],
-        sums_head[:half].astype(jnp.float32)[None],
+        layer_out, grad_tokens, gain_attn, sum_q, sum_k, sum_v, sum_o, gain_moe, gate, up, down,
     )
 
 

time: 379 us -> 372 us (0.982)
  Pallas kernels: 350 us -> 360 us
  other arithmetic: 14.8 us -> 5.02 us
  local copies, waits for them, and re-layouts: 8.97 us -> 1.32 us
    pallas_call x1, Pallas kernels: 225 us -> 246 us  [up_to_attention_back(): pl.pallas_call(kernel, out_shape=(jax.ShapeDtypeStruct((width, width), lo...]
    pallas_call x1 -> x2, Pallas kernels: 125 us -> 114 us  [the longest x1 102 us: back_dense(): pl.pallas_call(kernel, out_shape=(jax.ShapeDtypeStruct((sum_rows, width),...]
    convert_element_type x2 -> x0, other arithmetic: 5.09 us -> none  [the longest x1 2.55 us: on_plane_device(): whole(slice(half, 2 * half)).astype(jnp.float32)[None]]
    unnamed x20 -> x0, local copies, waits for them, and re-layouts: 4.72 us -> none
    broadcast_in_dim x1 -> x0, other arithmetic: 4.65 us -> none  [on_plane_device(): sums_head[:half].astype(jnp.float32)[None]]
where the time goes in v7:
time: 372 us; the launch traced here: 368 us
  Pallas kernels  360 us (97%)
  other arithmetic  5.02 us (1%)
    pallas_call x1, Pallas kernels, up_to_attention_back(): pl.pallas_call(kernel, out_shape=(jax.ShapeDtypeStruct((width, width), lo...  246 us
    pallas_call x1, Pallas kernels, back_dense(): pl.pallas_call(kernel, out_shape=(jax.ShapeDtypeStruct((sum_rows, width),...  102 us
    pallas_call x1, Pallas kernels, hand_over(): pl.pallas_call(kernel, grid=(steps,), out_shape=(jax.ShapeDtypeStruct((1,...  12.6 us

profile of v7, /device:TPU:0, one launch (start us, length us, event | category | flops | bytes accessed | tf_op | source)
XLA Modules:
  0.0 367.6 jit_solution(1821013440606527804)
XLA Ops:
  0.6 0.7 pad_maximum_fusion.2
  1.3 0.8 reduce-window.8
  2.2 0.7 select_reduce_fusion.1
  2.9 0.1 dynamic-slice_convert_fusion
  3.0 0.6 broadcast_in_dim.44.starts_ref
  3.6 1.3 select_reduce_fusion.gate_ref
  4.9 0.1 copy.32
  5.0 0.6 pad.4.gains_ref
  5.6 0.5 fusion
  6.2 0.8 pad_maximum_fusion
  7.0 245.7 %up_to_attention_back.1 = (bf16[1536,1536]{1,0:T(8,128)(2,1)}, bf16[1536,640]{1,0:T(8,128)(2,1)}, bf16[1536,1536]{1,0:T(8,128)(2,1)}, bf16[256,1536]{1,0:T(8,128...) custom-call(bf16[48,1536]{1,0:T(8,128)(2,1)} %wq_ref.1, ...), custom_call_target="tpu_custom_call" | custom-call | tf_op jit(solution)/shard_map/up_to_attention_back/pallas_call | solution.py:1275
  252.7 101.8 %back_dense.1 = (bf16[1024,1536]{1,0:T(8,128)(2,1)}, bf16[256,1536]{1,0:T(8,128)(2,1)}, f32[256,1536]{1,0:T(8,128)}, f32[48,1536]{1,0:T(8,128)}, f32[48,256]{1,0...) custom-call(bf16[2304,1536]{1,0:T(8,128)(2,1)} %get-tuple-element.43.sums_ref, ...), custom_call_target="tpu_custom_call" | custom-call | tf_op jit(solution)/shard_map/back_dense/pallas_call | solution.py:1472
  354.5 12.6 %hand_over.1 = (f32[1,768,1536]{2,1,0:T(8,128)}, f32[1,1536,768]{2,1,0:T(8,128)}, f32[1,1536,768]{2,1,0:T(8,128)}, f32[48]{0:T(128)}, f32[48]{0:T(128)}, /*index...) custom-call(bf16[1408,1536]{1,0:T(8,128)(2,1)} %get-tuple-element.42, ...), custom_call_target="tpu_custom_call" | custom-call | tf_op jit(solution)/shard_map/hand_over/pallas_call | solution.py:1566
  (2 shorter events, 0.0 us)

commit v8 on v7

--- a/solution.py
+++ b/solution.py
@@ -1,4 +1,4 @@
-import functools
+import math
 
 import jax
 import jax.numpy as jnp
@@ -794,7 +794,8 @@
 
 
 def up_to_attention_back(
-    w_query, w_key, w_value, gains, w_out, tokens, cotangent, gates, w_gate, w_up, w_down, starts, cosine, sine
+    w_query, w_key, w_value, w_out, tokens, cotangent, w_gate, w_up, w_down, gain_attn, gain_moe, routes, gate_values,
+    lengths,
 ):
     rows, width = w_query.shape
     key_width = w_key.shape[1]
@@ -812,12 +813,12 @@
     q_width = HEADS * HD
 
     def kernel(
-        wq_ref, wk_ref, wv_ref, gains_ref, wo_ref, tok_hbm, cot_hbm, gate_ref, wg_ref, wu_ref, wd_ref, starts_ref, cos_ref,
-        sin_ref,
+        wq_ref, wk_ref, wv_ref, wo_ref, tok_hbm, cot_hbm, wg_ref, wu_ref, wd_ref, attn_ref, moe_ref, routes_ref,
+        values_ref, lengths_ref,
         out_q, out_kv, out_o, query_hbm, mixed_hbm, normed_hbm, middle_hbm, gain_rows_ref, sums_ref, prod_ref, total_ref,
         grad_mid_hbm, grad_pre_ref, gain_row_ref, w_out_ref,
         w_in, w_down, x_all, y_all, hidden, grad_hidden, grad_in, sums, sums_land, all_gate, gate_t, all_kv, lse_ref,
-        core_in, first_in, second_in, middle_ref, kv_land, here, there, freed, send, recv,
+        core_in, first_in, second_in, middle_ref, kv_land, cos_ref, sin_ref, both_gains, here, there, freed, send, recv,
     ):
         wires = Wires(send, recv)
         dp, z = wires.dp, wires.z
@@ -851,9 +852,7 @@
         moves = [
             (wk_ref, full_kv.at[own, pl.ds(0, key_width)]),
             (wv_ref, full_kv.at[own, pl.ds(key_width, kv_width - key_width)]),
-            (gains_ref, full_kv.at[own, pl.ds(kv_width, LANES)]),
             (cot_hbm, all_cot.at[cut_of(dp)]),
-            (gate_ref, all_gate.at[gate_rows(dp)]),
             (wq_ref, full_q.at[own]),
             (wo_ref, full_o.at[own]),
             (tok_hbm, tok_ref),
@@ -866,10 +865,21 @@
             (cot_hbm, cot_ref),
         ]
         moves = [pltpu.make_async_copy(a, b, here.at[i]) for i, (a, b) in enumerate(moves)]
-        locals_, load_down, load_in, later = moves[:8], moves[8], moves[9:11], moves[11:]
+        locals_, load_down, load_in, later = moves[:6], moves[6], moves[7:9], moves[9:]
         for one in locals_:
             one.start()
         load_down.start()
+        both_gains[...] = jnp.zeros_like(both_gains)
+        both_gains[0:1, :rows] = attn_ref[...].astype(jnp.float32)
+        both_gains[1:2, :rows] = moe_ref[...].astype(jnp.float32)
+        columns = jnp.concatenate([both_gains[...]] * (LANES // 8), axis=0).T
+        full_kv[own, kv_width:] = columns[:rows, :].astype(jnp.bfloat16)
+        numbers = lax.broadcasted_iota(jnp.int32, (planes, tok_rows), 0)
+        gates = jnp.zeros((planes, tok_rows), jnp.float32)
+        for place in range(routes_ref.shape[0]):
+            named = routes_ref[place : place + 1, :] == numbers
+            gates = gates + jnp.where(named, values_ref[place : place + 1, :], 0.0)
+        all_gate[gate_rows(dp), :] = gates
         greet(wires, range(1, planes), True)
         for one in locals_:
             one.wait()
@@ -898,10 +908,27 @@
             part = all_gate.at[gate_rows(owner)]
             return wires.copy(part, part, first + mask - 1, dp=masked(dp, mask))
 
+        def starts_of(places):
+            begin = jnp.zeros_like(places)
+            edge = jnp.zeros((1, 1), jnp.int32)
+            for number in range(lengths_ref.shape[1] - 1):
+                edge = edge + lengths_ref[0:1, number : number + 1]
+                begin = jnp.where(places >= edge, edge, begin)
+            return begin
+
+        def set_turns():
+            places = lax.broadcasted_iota(jnp.int32, (tok_rows, HD), 0) + z * tok_rows
+            lane = lax.broadcasted_iota(jnp.int32, (tok_rows, HD), 1)
+            power = lax.rem(lane, HD // 2).astype(jnp.float32) * (-math.log(rope_base) / (HD // 2))
+            angles = (places - starts_of(places)).astype(jnp.float32) * jnp.exp(power)
+            cos_ref[...] = jnp.cos(angles)
+            sine = jnp.sin(angles)
+            sin_ref[...] = jnp.where(lane < HD // 2, -sine, sine)
+
         def set_bias():
             key_place = lax.broadcasted_iota(jnp.int32, (keys, tok_rows), 0)
-            query_place = lax.broadcasted_iota(jnp.int32, (keys, tok_rows), 1) + z * tok_rows
-            allowed = (key_place >= starts_ref[0:1, :]) & (key_place <= query_place)
+            query_place = lax.broadcasted_iota(jnp.int32, (1, tok_rows), 1) + z * tok_rows
+            allowed = (key_place >= starts_of(query_place)) & (key_place <= query_place)
             bias[...] = jnp.where(allowed, 0.0, masked_score)
 
         line_kv.start(0)
@@ -910,7 +937,7 @@
             gate_copy(mask, dp).start()
         line_kv.wait(0)
         line_kv.start(1)
-        set_bias()
+        set_turns()
         line_kv.wait(1)
         line_kv.start(2)
         line_q.start(0)
@@ -922,6 +949,7 @@
         plane_kv.wait(0)
         plane_kv.start(1)
         plane_cot.start(1, far=False)
+        set_bias()
         line_q.wait(1)
         line_q.start(2)
         line_o.start(0)
@@ -1291,7 +1319,7 @@
             jax.ShapeDtypeStruct((8, width), f32),
             jax.ShapeDtypeStruct((group, width), low),
         ),
-        in_specs=[ANY] * 11 + [VMEM] * 3,
+        in_specs=[ANY] * 9 + [VMEM] * 5,
         out_specs=(ANY,) * 7 + (VMEM, ANY, ANY, VMEM, ANY, VMEM, VMEM, VMEM),
         scratch_shapes=[
             pltpu.VMEM((width, 2 * hidden_width), low),
@@ -1312,6 +1340,9 @@
         + [
             pltpu.VMEM((tok_rows, width), f32),
             LineReduce.scratch(tok_rows, kv_width, 1),
+            pltpu.VMEM((tok_rows, HD), f32),
+            pltpu.VMEM((tok_rows, HD), f32),
+            pltpu.VMEM((8, LANES), f32),
             pltpu.SemaphoreType.DMA((15,)),
             pltpu.SemaphoreType.DMA((18,)),
             pltpu.SemaphoreType.REGULAR,
@@ -1320,7 +1351,8 @@
         compiler_params=kernel_params(1, 63),
         name="up_to_attention_back",
     )(
-        w_query, w_key, w_value, gains, w_out, tokens, cotangent, gates, w_gate, w_up, w_down, starts, cosine, sine
+        w_query, w_key, w_value, w_out, tokens, cotangent, w_gate, w_up, w_down, gain_attn, gain_moe, routes, gate_values,
+        lengths,
     )
 
 
@@ -1436,9 +1468,8 @@
             one.wait()
         plane.step(0)
         summed.tick(2)
+        dense.step(3)
         plane.step(1)
-        summed.tick()
-        dense.step(3)
         plane.step(2)
         summed.tick(2)
         dense.step(4)
@@ -1609,33 +1640,12 @@
     lengths,
     cotangent,
 ):
-    tok_rows = tokens.shape[0]
-    ctx_size = lax.axis_size("ctx")
-    ctx_place = lax.axis_index("ctx")
-    group_places = jnp.arange(tok_rows * ctx_size, dtype=jnp.int32)
-    seg_all, within_all = seq_tables(lengths[0], group_places)
-    offset = ctx_place * tok_rows
-    own_places = offset + jnp.arange(tok_rows, dtype=jnp.int32)
-    within_own = lax.dynamic_slice_in_dim(within_all, offset, tok_rows)
-    kv_columns = KVH * HD
-    q_columns = HEADS * HD
-    gains = jnp.pad(jnp.stack([norm_attn, norm_moe], axis=1), ((0, 0), (0, LANES - 2)))
-    numbers = jnp.arange(8, dtype=jnp.int32)
-    gates = jnp.sum(
-        jnp.where(routes[None, :, :] == numbers[:, None, None], gate_values[None], 0.0), axis=2
-    )
-    half_size = HD // 2
-    frequency = rope_base ** (-jnp.arange(half_size, dtype=jnp.float32) / half_size)
-    angles = within_own.astype(jnp.float32)[:, None] * frequency[None, :]
-    cosine = jnp.concatenate([jnp.cos(angles), jnp.cos(angles)], axis=1)
-    sine = jnp.concatenate([-jnp.sin(angles), jnp.sin(angles)], axis=1)
-    starts = jnp.broadcast_to((own_places - within_own)[None, :], (8, tok_rows))
     (
         full_q, full_kv, _, _, _, normed_low, middle, gain_rows, partial_sums, produced, sums_head, grad_mid, grad_pre,
         gain_row, w_out_part,
     ) = up_to_attention_back(
-        w_query, w_key, w_value, gains, w_out, tokens, cotangent, gates, w_gate[0], w_up[0], w_down[0], starts, cosine,
-        sine,
+        w_query, w_key, w_value, w_out, tokens, cotangent, w_gate[0], w_up[0], w_down[0], norm_attn[None], norm_moe[None],
+        routes.T, gate_values.T, lengths,
     )
     sums_tail, layer_out, grad_tokens, sum_q, sum_k, sum_v, sum_gains, sum_o = back_dense(
         partial_sums,

time: 372 us -> 366 us (0.984)
  other arithmetic: 5.02 us -> 0 us
where the time goes in v8:
time: 366 us; the launch traced here: 361 us
  Pallas kernels  360 us (98%)
    pallas_call x1, Pallas kernels, up_to_attention_back(): pl.pallas_call(kernel, out_shape=(jax.ShapeDtypeStruct((width, width), lo...  246 us
    pallas_call x1, Pallas kernels, back_dense(): pl.pallas_call(kernel, out_shape=(jax.ShapeDtypeStruct((sum_rows, width),...  101 us
    pallas_call x1, Pallas kernels, hand_over(): pl.pallas_call(kernel, grid=(steps,), out_shape=(jax.ShapeDtypeStruct((1,...  12.6 us

profile of v8, /device:TPU:0, one launch (start us, length us, event | category | flops | bytes accessed | tf_op | source)
XLA Modules:
  0.0 360.9 jit_solution(3571186568846827323)
XLA Ops:
  0.6 245.8 %up_to_attention_back.1 = (bf16[1536,1536]{1,0:T(8,128)(2,1)}, bf16[1536,640]{1,0:T(8,128)(2,1)}, bf16[1536,1536]{1,0:T(8,128)(2,1)}, bf16[256,1536]{1,0:T(8,128...) custom-call(bf16[48,1536]{1,0:T(8,128)(2,1)} %wq_ref.1, ...), custom_call_target="tpu_custom_call" | custom-call | tf_op jit(solution)/shard_map/up_to_attention_back/pallas_call | solution.py:1303
  246.4 101.4 %back_dense.1 = (bf16[1024,1536]{1,0:T(8,128)(2,1)}, bf16[256,1536]{1,0:T(8,128)(2,1)}, f32[256,1536]{1,0:T(8,128)}, f32[48,1536]{1,0:T(8,128)}, f32[48,256]{1,0...) custom-call(bf16[2304,1536]{1,0:T(8,128)(2,1)} %get-tuple-element.43.sums_ref, ...), custom_call_target="tpu_custom_call" | custom-call | tf_op jit(solution)/shard_map/back_dense/pallas_call | solution.py:1503
  347.8 12.6 %hand_over.1 = (f32[1,768,1536]{2,1,0:T(8,128)}, f32[1,1536,768]{2,1,0:T(8,128)}, f32[1,1536,768]{2,1,0:T(8,128)}, f32[48]{0:T(128)}, f32[48]{0:T(128)}, /*index...) custom-call(bf16[1408,1536]{1,0:T(8,128)(2,1)} %get-tuple-element.42, ...), custom_call_target="tpu_custom_call" | custom-call | tf_op jit(solution)/shard_map/hand_over/pallas_call | solution.py:1597

commit v9 on v8

--- a/solution.py
+++ b/solution.py
@@ -1277,9 +1277,6 @@
         line.event(3)
         line.event(4)
         dense.step(5)
-        summed.tick(max(0, summed.all - summed.now))
-        save_last = save_sums(done_rows, sent_rows, 2)
-        save_last.start()
         line.event(5)
         line.finish((kv_out,))
         for pair in range(KVH):
@@ -1288,14 +1285,18 @@
                 kv_out[:, cut], cos_ref[...], -sin_ref[...]
             ).astype(jnp.bfloat16)
         grad_pre_ref[:, q_width + kv_width // 2 :] = kv_out[:, kv_width // 2 :].astype(jnp.bfloat16)
-        summed.finish()
         for block in range(8):
             save_made(block).wait()
-        for one in (save, save_mid, save_last):
-            one.wait()
+        save.wait()
+        save_mid.wait()
         line_keys.finish()
         for mask in range(1, planes):
             gate_copy(mask, dp).wait_send()
+        summed.tick(max(0, summed.all - summed.now))
+        save_last = save_sums(done_rows, sent_rows, 2)
+        save_last.start()
+        summed.finish()
+        save_last.wait()
 
     f32, low = jnp.float32, jnp.bfloat16
     copies = 4 * LineGather.COPIES + 5 * PlaneGather.COPIES + planes - 1
@@ -1483,20 +1484,19 @@
         in_line.event(2)
         summed.tick(2)
         in_line.event(3)
+        o_line.finish((out_ref,))
         in_line.event(4)
         plane.step(4)
         summed.tick(2)
         in_line.event(5)
+        in_line.finish((wq_ref, wk_ref, wv_ref, gains_ref))
         plane.step(5)
-        summed.tick(2)
 
         @pl.loop(0, tok_rows // tile)
         def _(step):
             cut = pl.ds(pl.multiple_of(step * tile, tile), tile)
             layer_ref[cut, :] = (middle_ref[cut, :] + moe[cut, :]).astype(jnp.bfloat16)
 
-        o_line.finish((out_ref,))
-        in_line.finish((wq_ref, wk_ref, wv_ref, gains_ref))
         summed.finish()
 
     f32, low = jnp.float32, jnp.bfloat16
@@ -1549,54 +1549,65 @@
 def hand_over(sums_head, sums_tail, gains, *others):
     done, width = sum(FIRST_CHUNKS[:-CARRIED]), sums_head.shape[1]
     hidden_width = width // 2
-    rows = 256
-    head_steps, tail_steps = done // rows, sums_tail.shape[0] // rows
-    down_steps = hidden_width // rows
-    steps = head_steps + tail_steps
-    count = len(others)
+    rows, tile = 256, 32
+    count, steps = len(others), (hidden_width + width) // rows
 
     def kernel(*refs):
         head_ref, tail_ref, gains_ref = refs[:3]
+        ins, outs = refs[3 : 3 + count], refs[8 + count : 8 + 2 * count]
         down_ref, gate_ref, up_ref, attn_ref, moe_ref = refs[3 + count : 8 + count]
-        step = pl.program_id(0)
-        for source, target in zip(refs[3 : 3 + count], refs[8 + count :]):
-            target[...] = source[...]
-
-        @pl.when(step == 0)
-        def _():
-            turned_gains = gains_ref[...].T
-            attn_ref[...] = turned_gains[0, :]
-            moe_ref[...] = turned_gains[1, :]
-
-        def put(values):
-            @pl.when(step < down_steps)
-            def _():
-                down_ref[0] = values
-
-            @pl.when(step >= down_steps)
-            def _():
-                gate_ref[0] = values[:, :hidden_width]
-                up_ref[0] = values[:, hidden_width:]
-
-        @pl.when(step < head_steps)
-        def _():
-            put(head_ref[...].astype(jnp.float32))
-
-        @pl.when(step >= head_steps)
-        def _():
-            put(tail_ref[...].astype(jnp.float32))
-
-    def by_rows(one):
-        if one.shape[0] % (8 * 16):
-            return pl.BlockSpec(one.shape, lambda i: (0, 0))
-        return pl.BlockSpec((one.shape[0] // 8, one.shape[1]), lambda i: (jnp.minimum(i, 7), 0))
+        low, wide, gate, up = refs[8 + 2 * count : 12 + 2 * count]
+        held, load, save = refs[12 + 2 * count : 12 + 3 * count], refs[-2], refs[-1]
+        loads, saves = [], []
+        for step in range(steps):
+            begin = step * rows
+            source, start = (head_ref, begin) if begin < done else (tail_ref, begin - done)
+            loads.append(
+                pltpu.make_async_copy(source.at[pl.ds(start, rows)], low.at[pl.ds(begin, rows)], load.at[step])
+            )
+        for number in range(count):
+            loads.append(pltpu.make_async_copy(ins[number], held[number], load.at[steps + number]))
+        for one in loads:
+            one.start()
+
+        def go(source, target, number):
+            saves.append(pltpu.make_async_copy(source, target, save.at[number]))
+            saves[-1].start()
+
+        for step in range(steps):
+            begin = step * rows
+            loads[step].wait()
+            down = begin < hidden_width
+            place = begin if down else begin - hidden_width
+
+            @pl.loop(0, rows // tile)
+            def _(part):
+                values = low[pl.ds(pl.multiple_of(begin + part * tile, tile), tile), :].astype(jnp.float32)
+                cut = pl.ds(pl.multiple_of(place + part * tile, tile), tile)
+                if down:
+                    wide[cut, :] = values
+                else:
+                    gate[cut, :] = values[:, :hidden_width]
+                    up[cut, :] = values[:, hidden_width:]
+
+            cut = pl.ds(place, rows)
+            if down:
+                go(wide.at[cut], down_ref.at[0, cut], step)
+            else:
+                go(gate.at[cut], gate_ref.at[0, cut], step)
+                go(up.at[cut], up_ref.at[0, cut], steps + step)
+        for number in range(count):
+            loads[steps + number].wait()
+            go(held[number], outs[number], 2 * steps + number)
+        turned_gains = gains_ref[...].T
+        attn_ref[...] = turned_gains[0, :]
+        moe_ref[...] = turned_gains[1, :]
+        for one in saves:
+            one.wait()
 
     f32 = jnp.float32
-    in_shape = (1, rows, hidden_width)
-    copied = [by_rows(one) for one in others]
     return pl.pallas_call(
         kernel,
-        grid=(steps,),
         out_shape=(
             jax.ShapeDtypeStruct((1, hidden_width, width), f32),
             jax.ShapeDtypeStruct((1, width, hidden_width), f32),
@@ -1605,20 +1616,16 @@
             jax.ShapeDtypeStruct((gains.shape[0],), f32),
         )
         + tuple(jax.ShapeDtypeStruct(one.shape, one.dtype) for one in others),
-        in_specs=[
-            pl.BlockSpec((rows, width), lambda i: (jnp.minimum(i, head_steps - 1), 0)),
-            pl.BlockSpec((rows, width), lambda i: (jnp.maximum(i - head_steps, 0), 0)),
-            pl.BlockSpec(gains.shape, lambda i: (0, 0)),
+        in_specs=[ANY, ANY, VMEM] + [ANY] * count,
+        out_specs=(ANY, ANY, ANY, VMEM, VMEM) + (ANY,) * count,
+        scratch_shapes=[
+            pltpu.VMEM((hidden_width + width, width), jnp.bfloat16),
+            pltpu.VMEM((hidden_width, width), f32),
+            pltpu.VMEM((width, hidden_width), f32),
+            pltpu.VMEM((width, hidden_width), f32),
         ]
-        + copied,
-        out_specs=(
-            pl.BlockSpec((1, rows, width), lambda i: (0, jnp.minimum(i, down_steps - 1), 0)),
-            pl.BlockSpec(in_shape, lambda i: (0, jnp.maximum(i - down_steps, 0), 0)),
-            pl.BlockSpec(in_shape, lambda i: (0, jnp.maximum(i - down_steps, 0), 0)),
-            pl.BlockSpec((gains.shape[0],), lambda i: (0,)),
-            pl.BlockSpec((gains.shape[0],), lambda i: (0,)),
-        )
-        + tuple(copied),
+        + [pltpu.VMEM(one.shape, one.dtype) for one in others]
+        + [pltpu.SemaphoreType.DMA((steps + count,)), pltpu.SemaphoreType.DMA((2 * steps + count,))],
         compiler_params=pltpu.CompilerParams(vmem_limit_bytes=63 * MIB),
         name="hand_over",
     )(sums_head, sums_tail, gains, *others)

time: 366 us -> 363 us (level)
  no operation moved by 1% of the time
where the time goes in v9:
time: 363 us; the launch traced here: 358 us
  Pallas kernels  357 us (98%)
    pallas_call x1, Pallas kernels, up_to_attention_back(): pl.pallas_call(kernel, out_shape=(jax.ShapeDtypeStruct((width, width), lo...  246 us
    pallas_call x1, Pallas kernels, back_dense(): pl.pallas_call(kernel, out_shape=(jax.ShapeDtypeStruct((sum_rows, width),...  101 us
    pallas_call x1, Pallas kernels, hand_over(): pl.pallas_call(kernel, out_shape=(jax.ShapeDtypeStruct((1, hidden_width,...  10.3 us

profile of v9, /device:TPU:0, one launch (start us, length us, event | category | flops | bytes accessed | tf_op | source)
XLA Modules:
  0.0 358.5 jit_solution(8033040230739616689)
XLA Ops:
  0.6 245.7 %up_to_attention_back.1 = (bf16[1536,1536]{1,0:T(8,128)(2,1)}, bf16[1536,640]{1,0:T(8,128)(2,1)}, bf16[1536,1536]{1,0:T(8,128)(2,1)}, bf16[256,1536]{1,0:T(8,128...) custom-call(bf16[48,1536]{1,0:T(8,128)(2,1)} %wq_ref.1, ...), custom_call_target="tpu_custom_call" | custom-call | tf_op jit(solution)/shard_map/up_to_attention_back/pallas_call | solution.py:1304
  246.4 101.4 %back_dense.1 = (bf16[1024,1536]{1,0:T(8,128)(2,1)}, bf16[256,1536]{1,0:T(8,128)(2,1)}, f32[256,1536]{1,0:T(8,128)}, f32[48,1536]{1,0:T(8,128)}, f32[48,256]{1,0...) custom-call(bf16[2304,1536]{1,0:T(8,128)(2,1)} %get-tuple-element.43.sums_ref, ...), custom_call_target="tpu_custom_call" | custom-call | tf_op jit(solution)/shard_map/back_dense/pallas_call | solution.py:1503
  347.8 10.3 %hand_over.1 = (f32[1,768,1536]{2,1,0:T(8,128)}, f32[1,1536,768]{2,1,0:T(8,128)}, f32[1,1536,768]{2,1,0:T(8,128)}, f32[48]{0:T(128)}, f32[48]{0:T(128)}, /*index...) custom-call(bf16[1408,1536]{1,0:T(8,128)(2,1)} %get-tuple-element.42, ...), custom_call_target="tpu_custom_call" | custom-call | tf_op jit(solution)/shard_map/hand_over/pallas_call | solution.py:1609
